TPU v7x, 32 devices: a whole 2x2x4 slice. The times are simulated.
32 devices in a mesh: row: 4 (over y, core), col: 8 (over z, x).
Axes of the slice: x: 2, y: 2, z: 4, core: 2. Of those that a mesh axis runs over, the one named last changes fastest.
Arguments:
- inputs: bfloat16 [256, 8192], P(('row', 'col')), may hold values from -6 to 6
- layer_norm_gain: float32 [8192], replicated, may hold values from 0.1 to 1.9
- w_in: bfloat16 [8192, 16384], P('row', 'col'), may hold values from -0.09375 to 0.09375
- w_out: bfloat16 [16384, 8192], P('col', 'row'), may hold values from -0.0625 to 0.0625
- pattern_in: int32 [64, 16], replicated, may hold values from 0 to 31, as said below
- pattern_out: int32 [32, 32], replicated, may hold values from 0 to 63, as said below
- out_grad: bfloat16 [256, 8192], P(('row', 'col')), may hold values from -6 to 6
Outputs:
- output: bfloat16 [256, 8192], P(('row', 'col'))
- grad_inputs: bfloat16 [256, 8192], P(('row', 'col'))
- grad_w_in: bfloat16 [8192, 16384], P('row', 'col')
- grad_w_out: bfloat16 [16384, 8192], P('col', 'row')
- norm_gain_gradient: float32 [8192], replicated
Inputs may be any that keep to these rules, and one draw needn't show every extreme that they name: `pattern_in`: each row lists 8192 / 512 different tile rows in increasing order. `pattern_out`: each row lists 16384 / 512 different tile rows in increasing order.
All inputs are finite; a program needn't handle non-finite values.
Results may differ from a plain program's by a relative error of at most 0.022.
Values may be sent and summed in bfloat16 or wider, within the bound.
No kernel may reach another device: no remote copies, remote signals or barrier semaphores. Data moves between devices by JAX's collectives and lax.ppermute only.
A program may use at most 128 MiB of HBM per device.

v0:
```python
import jax
import jax.numpy as jnp
from jax import lax
from jax.sharding import PartitionSpec as P

D = 8192
FF = 16384
BLOCK = 256


def block_mask(pattern, tile_rows):
    iota = jnp.arange(tile_rows, dtype=jnp.int32)
    return jnp.any(pattern[None, :, :] == iota[:, None, None], axis=2)


def apply_mask(weight, mask):
    rows_t, cols_t = mask.shape
    shaped = weight.reshape(rows_t, BLOCK, cols_t, BLOCK)
    kept = jnp.where(mask[:, None, :, None], shaped, jnp.zeros((), weight.dtype))
    return kept.reshape(weight.shape)


def gelu_value(h):
    inner = 0.7978845608 * (h + 0.044715 * h * h * h)
    return 0.5 * h * (1.0 + jnp.tanh(inner))


def gelu_slope(h):
    tanh_v = jnp.tanh(0.7978845608 * (h + 0.044715 * h * h * h))
    return 0.5 * (1.0 + tanh_v) + 0.5 * h * (1.0 - tanh_v * tanh_v) * 0.7978845608 * (
        1.0 + 0.134145 * h * h
    )


def dot_last(left, right):
    return lax.dot_general(
        left, right, (((1,), (1,)), ((), ())), preferred_element_type=jnp.float32
    )


def dot_first(left, right):
    return lax.dot_general(
        left, right, (((0,), (0,)), ((), ())), preferred_element_type=jnp.float32
    )


def shards(inputs, layer_norm_gain, w_in, w_out, pattern_in, pattern_out, out_grad):
    n_row = lax.axis_size("row")
    n_col = lax.axis_size("col")
    row_index = lax.axis_index("row")
    col_index = lax.axis_index("col")
    tok_here = inputs.shape[0]
    feat_tiles = w_in.shape[0] // BLOCK
    unit_tiles = w_in.shape[1] // BLOCK
    mask_in = lax.dynamic_slice(
        block_mask(pattern_in, D // BLOCK),
        (row_index * feat_tiles, col_index * unit_tiles),
        (feat_tiles, unit_tiles),
    )
    mask_out = lax.dynamic_slice(
        block_mask(pattern_out, FF // BLOCK),
        (col_index * unit_tiles, row_index * feat_tiles),
        (unit_tiles, feat_tiles),
    )
    w_in_e = apply_mask(w_in, mask_in)
    w_out_e = apply_mask(w_out, mask_out)
    xfloat = inputs.astype(jnp.float32)
    centered_input = xfloat - jnp.mean(xfloat, axis=1, keepdims=True)
    inverse_deviation = lax.rsqrt(
        jnp.mean(centered_input * centered_input, axis=1, keepdims=True) + 1e-05
    )
    standardized_input = centered_input * inverse_deviation
    normalized_input = (standardized_input * layer_norm_gain[None, :]).astype(jnp.bfloat16)
    swapped = lax.all_to_all(normalized_input, "row", split_axis=1, concat_axis=0, tiled=True)
    allrows = lax.all_gather(swapped, "col", axis=0, tiled=True)
    slice_width = allrows.shape[1]
    byrow = (
        allrows.reshape(n_col, n_row, tok_here, slice_width)
        .transpose(1, 0, 2, 3)
        .reshape(-1, slice_width)
    )
    hidden_pre = lax.psum_scatter(
        jnp.dot(byrow, w_in_e, preferred_element_type=jnp.float32).astype(jnp.bfloat16),
        "row",
        scatter_dimension=0,
        tiled=True,
    ).astype(jnp.float32)
    activation = gelu_value(hidden_pre).astype(jnp.bfloat16)
    w_out_full = lax.all_gather(w_out_e, "row", axis=1, tiled=True)
    summed = lax.psum_scatter(
        jnp.dot(activation, w_out_full, preferred_element_type=jnp.float32).astype(jnp.bfloat16),
        "col",
        scatter_dimension=0,
        tiled=True,
    ).astype(jnp.float32)
    output = (xfloat + summed).astype(jnp.bfloat16)
    grad_panel = lax.all_gather(out_grad, "col", axis=0, tiled=True)
    d_act = dot_last(grad_panel, w_out_full)
    d_pre = (d_act * gelu_slope(hidden_pre)).astype(jnp.bfloat16)
    w2_sum = lax.psum_scatter(
        dot_first(activation, grad_panel).astype(jnp.bfloat16),
        "row",
        scatter_dimension=1,
        tiled=True,
    )
    grad_w_out = apply_mask(w2_sum, mask_out)
    d_all = lax.all_gather(d_pre, "row", axis=0, tiled=True)
    unit_width = d_all.shape[1]
    panel_terms = jnp.einsum(
        "gtf,gth->gfh",
        byrow.reshape(n_row, -1, slice_width),
        d_all.reshape(n_row, -1, unit_width),
        preferred_element_type=jnp.float32,
    )
    panel_rounded = lax.optimization_barrier(panel_terms.astype(jnp.bfloat16))
    w1_sum = jnp.sum(panel_rounded.astype(jnp.float32), axis=0)
    d_order = (
        d_all.reshape(n_row, n_col, tok_here, unit_width)
        .transpose(1, 0, 2, 3)
        .reshape(-1, unit_width)
    )
    slices = lax.psum_scatter(
        dot_last(d_order, w_in_e).astype(jnp.bfloat16), "col", scatter_dimension=0, tiled=True
    ).astype(jnp.float32)
    normed_gradient = lax.all_to_all(
        slices.astype(jnp.bfloat16), "row", split_axis=0, concat_axis=1, tiled=True
    ).astype(slices.dtype)
    grad_w_in = apply_mask(w1_sum.astype(jnp.bfloat16), mask_in)
    norm_gain_gradient = lax.psum(
        jnp.sum(normed_gradient * standardized_input, axis=0), ("row", "col")
    )
    gain_scaled = normed_gradient * layer_norm_gain[None, :]
    backward_result = inverse_deviation * (
        gain_scaled
        - jnp.mean(gain_scaled, axis=1, keepdims=True)
        - standardized_input * jnp.mean(gain_scaled * standardized_input, axis=1, keepdims=True)
    )
    grad_inputs = (out_grad.astype(jnp.float32) + backward_result).astype(jnp.bfloat16)
    return (output, grad_inputs, grad_w_in, grad_w_out, norm_gain_gradient)


def solution(mesh):
    in_specs = (
        P(("row", "col"), None),
        P(),
        P("row", "col"),
        P("col", "row"),
        P(),
        P(),
        P(("row", "col"), None),
    )
    out_specs = (
        P(("row", "col"), None),
        P(("row", "col"), None),
        P("row", "col"),
        P("col", "row"),
        P(),
    )
    return jax.shard_map(shards, mesh=mesh, in_specs=in_specs, out_specs=out_specs, check_vma=False)
```

profile of v0, /device:TPU:0, one launch (start us, length us, event | category | flops | bytes accessed | tf_op | source)
XLA Modules:
  0.0 774.3 jit_solution(17682693704396659359)
XLA Ops:
  7.2 0.0 all-gather.5.cloned.1.call-start
  7.2 1.1 convert_reduce_fusion
  8.3 1.2 fusion.30
  9.5 1.0 fusion.23
  10.5 8.8 %all_to_all.32 = bf16[8,4,2048]{2,0,1:T(8,128)(2,1)} all-to-all(bf16[8,4,2048]{2,0,1:T(8,128)(2,1)S(1)} %bitcast.54), channel_id=1, replica_groups=mesh['row'=4,'col'=8] {'row'}, dimensions={1} | all-to-all | bytes 262144 | tf_op jit(solution)/shard_map/all_to_all | solution.py:74
  19.3 0.0 all-gather.5.cloned.1.call-update
  19.3 0.0 all-gather.9.cloned.1.call-start
  19.3 0.7 all-gather.9.cloned.1.call-update
  20.0 0.0 reduce-scatter.5.cloned.1.call-start
  20.1 0.8 fusion.32
  20.9 0.1 dynamic_slice.6
  20.9 1.2 broadcast_in_dim.44
  22.1 4.1 copy.24
  26.2 34.0 %all-gather.5.cloned.1.call-done = bf16[256,2048]{1,0:T(8,128)(2,1)} async-done(((bf16[32,2048]{1,0:T(8,128)(2,1)}), bf16[256,2048]{1,0:T(8,128)(2,1)}) %all-gather.5.cloned.1.call-update) | async-done | bytes 1048592 | tf_op jit(solution)/shard_map/all_gather | solution.py:75
  60.2 1.3 copy.20
  61.6 8.0 %fusion.2 = bf16[256,2048]{1,0:T(8,128)(2,1)} fusion(bf16[256,2048]{1,0:T(8,128)(2,1)S(1)} %bitcast.51, pred[2048,2048]{1,0:T(8,128)(4,1)} %bitcast.39, bf16[2048,2048]{1,0:T(8,128)(2,1)} %param.9), kind=kOutput, calls=%fused_computation.9 | convolution fusion | flops 2152202240 | bytes 14680064 | tf_op jit(solution)/shard_map/dot_general | solution.py:83
  69.6 0.0 reduce-scatter.11.cloned.1.call-start
  69.6 31.7 %all-gather.9.cloned.1.call-done = bf16[64,8192]{1,0:T(8,128)(2,1)} async-done(((bf16[8,8192]{1,0:T(8,128)(2,1)}), bf16[64,8192]{1,0:T(8,128)(2,1)}) %all-gather.9.cloned.1.call-update) | async-done | bytes 1048592 | tf_op jit(solution)/shard_map/all_gather | solution.py:97
  101.4 26.8 %reduce-scatter.5.cloned.1.call-done = bf16[64,2048]{1,0:T(8,128)(2,1)} async-done(((bf16[256,2048]{1,0:T(8,128)(2,1)}), bf16[64,2048]{1,0:T(8,128)(2,1)}) %reduce-scatter.5.cloned.1.call-update) | async-done | bytes 262160 | tf_op jit(solution)/shard_map/reduce_scatter | solution.py:82
  128.1 15.5 %convolution_convert_fusion = bf16[2048,8192]{1,0:T(8,128)(2,1)} fusion(bf16[64,8192]{1,0:T(8,128)(2,1)} %all-gather.9.cloned.1.call-done, bf16[64,2048]{1,0:T(8,128)(2,1)} %reduce-scatter.5.cloned.1.call-done), kind=kOutput, calls=%fused_computation | convolution fusion | flops 2165571584 | bytes 34865152 | tf_op jit(solution)/shard_map/dot_general | solution.py:42
  143.6 0.2 all-gather.7.cloned.1.call-start
  143.9 0.5 copy-done.7
  144.3 0.2 fusion.16
  144.6 0.1 dynamic_slice.7
  144.6 0.1 copy.21
  144.7 1.1 broadcast_in_dim.47
  145.9 4.3 copy.25
  150.1 228.4 %reduce-scatter.11.cloned.1.call-done = bf16[2048,2048]{1,0:T(8,128)(2,1)} async-done(((bf16[2048,8192]{1,0:T(8,128)(2,1)}), bf16[2048,2048]{1,0:T(8,128)(2,1)}) %reduce-scatter.11.cloned.1.call-update) | async-done | bytes 8388624 | tf_op jit(solution)/shard_map/reduce_scatter | solution.py:100
  378.6 12.3 %broadcast_select_fusion = (bf16[2048,2048]{1,0:T(8,128)(2,1)}, bf16[2048,2048]{1,0:T(8,128)(2,1)}) fusion(pred[2048,2048]{1,0:T(8,128)(4,1)} %bitcast.42, bf16[2048,2048]{1,0:T(8,128)(2,1)} %reduce-scatter.11.cloned.1.call-done, bf16[2048,2048]{1,0:T(8,128)(2,1)} %param.10), kind=kLoop, calls=%fused_computation.3 | loop fusion | flops 8388608 | bytes 37748736 | tf_op jit(solution)/shard_map/jit(_where)/select_n | solution.py:19
  390.9 0.0 all-gather.11.cloned.1.call-start
  391.0 201.6 %all-gather.7.cloned.1.call-done = bf16[2048,8192]{1,0:T(8,128)(2,1)} async-done(((bf16[2048,2048]{1,0:T(8,128)(2,1)}), bf16[2048,8192]{1,0:T(8,128)(2,1)}) %all-gather.7.cloned.1.call-update) | async-done | bytes 33554448 | tf_op jit(solution)/shard_map/all_gather | solution.py:89
  592.6 17.2 %fusion.5 = bf16[64,2048]{1,0:T(8,128)(2,1)} fusion(bf16[2048,8192]{1,0:T(8,128)(2,1)} %all-gather.7.cloned.1.call-done, bf16[64,8192]{1,0:T(8,128)(2,1)S(1)} %copy-done, bf16[64,2048]{1,0:T(8,128)(2,1)S(1)} %copy-done.4), kind=kOutput, calls=%fused_computation.13 | convolution fusion | flops 2150105088 | bytes 35127296 | tf_op jit(solution)/shard_map/dot_general | solution.py:36
  609.9 0.0 reduce-scatter.9.cloned.1.call-start
  609.9 16.8 %all-gather.11.cloned.1.call-done = bf16[256,2048]{1,0:T(8,128)(2,1)} async-done(((bf16[64,2048]{1,0:T(8,128)(2,1)}), bf16[256,2048]{1,0:T(8,128)(2,1)}) %all-gather.11.cloned.1.call-update) | async-done | bytes 1048592 | tf_op jit(solution)/shard_map/all_gather | solution.py:107
  626.7 1.3 copy.22
  628.1 8.1 %fusion.3 = bf16[256,2048]{1,0:T(8,128)(2,1)} fusion(bf16[256,2048]{1,0:T(8,128)(2,1)S(1)} %bitcast.52, pred[2048,2048]{1,0:T(8,128)(4,1)} %bitcast.40, bf16[2048,2048]{1,0:T(8,128)(2,1)} %param.9), kind=kOutput, calls=%fused_computation.10 | convolution fusion | flops 2152202240 | bytes 14680064 | tf_op jit(solution)/shard_map/dot_general | solution.py:36
  636.2 0.3 reduce-scatter.7.cloned.1.call-start
  636.5 14.9 %convolution_convert_fusion.2 = bf16[64,8192]{1,0:T(8,128)(2,1)} fusion(bf16[2048,8192]{1,0:T(8,128)(2,1)} %all-gather.7.cloned.1.call-done, bf16[64,2048]{1,0:T(8,128)(2,1)S(1)} %copy-done.4), kind=kOutput, calls=%fused_computation.2 | convolution fusion | flops 2149318656 | bytes 34865152 | tf_op jit(solution)/shard_map/dot_general | solution.py:91
  651.4 13.8 %convolution_convert_fusion.1 = bf16[4,2048,2048]{2,1,0:T(8,128)(2,1)} fusion(bf16[4,64,2048]{2,1,0:T(8,128)(2,1)S(1)} %bitcast.48, bf16[4,8,8,2048]{3,2,0,1:T(8,128)(2,1)S(1)} %bitcast.46), kind=kOutput, calls=%fused_computation.1 | convolution fusion | flops 2164260864 | bytes 35651584 | tf_op jit(solution)/shard_map/gtf,gth->gfh/dot_general | solution.py:109
  665.2 16.7 %reduce_sum.61 = bf16[2048,2048]{1,0:T(8,128)(2,1)} reduce(bf16[4,2048,2048]{2,1,0:T(8,128)(2,1)} %convolution_convert_fusion.1, bf16[]{:T(256)} %constant.35.clone.1), dimensions={0}, to_apply=%region_9.10 | reduce | flops 12582912 | bytes 41943040 | tf_op jit(solution)/shard_map/reduce_sum | solution.py:116
  681.9 17.9 %reduce-scatter.9.cloned.1.call-done = bf16[32,2048]{1,0:T(8,128)(2,1)} async-done(((bf16[256,2048]{1,0:T(8,128)(2,1)}), bf16[32,2048]{1,0:T(8,128)(2,1)}) %reduce-scatter.9.cloned.1.call-update) | async-done | bytes 131088 | tf_op jit(solution)/shard_map/reduce_scatter | solution.py:122
  699.8 3.3 all-to-all-start.1
  703.1 8.9 %broadcast_select_fusion.1 = bf16[2048,2048]{1,0:T(8,128)(2,1)} fusion(pred[2048,2048]{1,0:T(8,128)(4,1)} %bitcast.41, bf16[2048,2048]{1,0:T(8,128)(2,1)} %reduce_sum.61), kind=kLoop, calls=%fused_computation.4 | loop fusion | flops 4194304 | bytes 20971520 | tf_op jit(solution)/shard_map/jit(_where)/select_n | solution.py:19
  712.1 0.3 fusion.29
  712.4 41.2 %psum.7 = f32[8192]{0:T(1024)} all-reduce(f32[8192]{0:T(1024)S(1)} %get-tuple-element.5), channel_id=1, replica_groups=mesh['row'=4,'col'=8] {'row','col'}, use_global_device_ids=true, to_apply=%region_12.13 | all-reduce | flops 8192 | bytes 65536 | tf_op jit(solution)/shard_map/psum | solution.py:129
  753.6 0.2 multiply_reduce_fusion
  753.8 12.0 %reduce-scatter.7.cloned.1.call-done = bf16[8,8192]{1,0:T(8,128)(2,1)} async-done(((bf16[64,8192]{1,0:T(8,128)(2,1)}), bf16[8,8192]{1,0:T(8,128)(2,1)}) %reduce-scatter.7.cloned.1.call-update) | async-done | bytes 131088 | tf_op jit(solution)/shard_map/reduce_scatter | solution.py:90
  765.7 1.7 fusion.28
  (28 shorter events, 0.2 us)
Async XLA Ops:
  7.2 53.1 %all-gather.5.cloned.1.call-start = ((), (), s32[]{:S(2)}) async-start(), calls=%async_computation.6 | async-start | bytes 1179648 | tf_op jit(solution)/shard_map/all_gather | solution.py:75
  19.3 82.1 %all-gather.9.cloned.1.call-start = ((), (), s32[]{:S(2)}) async-start(), calls=%async_computation.10 | async-start | bytes 1179648 | tf_op jit(solution)/shard_map/all_gather | solution.py:97
  20.0 108.1 %reduce-scatter.5.cloned.1.call-start = ((), (), s32[]{:S(2)}) async-start(), calls=%async_computation.7 | async-start | bytes 1310720 | tf_op jit(solution)/shard_map/reduce_scatter | solution.py:82
  69.6 309.0 %reduce-scatter.11.cloned.1.call-start = ((), (), s32[]{:S(2)}) async-start(), calls=%async_computation.13 | async-start | bytes 41943040 | tf_op jit(solution)/shard_map/reduce_scatter | solution.py:100
  143.6 0.7 copy-start.7
  143.6 449.0 %all-gather.7.cloned.1.call-start = ((), (), s32[]{:S(2)}) async-start(), calls=%async_computation.8 | async-start | bytes 41943040 | tf_op jit(solution)/shard_map/all_gather | solution.py:89
  390.9 201.7 %copy-start = (bf16[64,8192]{1,0:T(8,128)(2,1)S(1)}, bf16[64,8192]{1,0:T(8,128)(2,1)}, u32[]{:S(2)}) copy-start(bf16[64,8192]{1,0:T(8,128)(2,1)} %all-gather.9.cloned.1.call-done) | copy-start | bytes 3145732
  390.9 201.7 %copy-start.4 = (bf16[64,2048]{1,0:T(8,128)(2,1)S(1)}, bf16[64,2048]{1,0:T(8,128)(2,1)}, u32[]{:S(2)}) copy-start(bf16[64,2048]{1,0:T(8,128)(2,1)} %reduce-scatter.5.cloned.1.call-done) | copy-start | bytes 786436
  390.9 235.8 %all-gather.11.cloned.1.call-start = ((), (), s32[]{:S(2)}) async-start(), calls=%async_computation.11 | async-start | bytes 1310720 | tf_op jit(solution)/shard_map/all_gather | solution.py:107
  609.9 89.9 %reduce-scatter.9.cloned.1.call-start = ((), (), s32[]{:S(2)}) async-start(), calls=%async_computation.12 | async-start | bytes 1179648 | tf_op jit(solution)/shard_map/reduce_scatter | solution.py:122
  628.0 8.4 %copy-start.6 = (f32[8192]{0:T(1024)S(1)}, f32[8192]{0:T(1024)}, u32[]{:S(2)}) copy-start(f32[8192]{0:T(1024)} %param.8) | copy-start | bytes 98308
  636.2 129.6 %reduce-scatter.7.cloned.1.call-start = ((), (), s32[]{:S(2)}) async-start(), calls=%async_computation.9 | async-start | bytes 1179648 | tf_op jit(solution)/shard_map/reduce_scatter | solution.py:90
  636.5 15.0 %copy-start.1 = (bf16[256,2048]{1,0:T(8,128)(2,1)S(1)}, bf16[256,2048]{1,0:T(8,128)(2,1)}, u32[]{:S(2)}) copy-start(bf16[256,2048]{1,0:T(8,128)(2,1)} %all-gather.5.cloned.1.call-done) | copy-start | bytes 3145732
  636.5 15.0 %copy-start.2 = (bf16[256,2048]{1,0:T(8,128)(2,1)S(1)}, bf16[256,2048]{1,0:T(8,128)(2,1)}, u32[]{:S(2)}) copy-start(bf16[256,2048]{1,0:T(8,128)(2,1)} %all-gather.11.cloned.1.call-done) | copy-start | bytes 3145732
  699.8 12.3 %all-to-all-start.1 = ((bf16[4,8,2048]{2,1,0:T(8,128)(2,1)}), bf16[4,8,2048]{2,1,0:T(8,128)(2,1)S(1)}, u32[]{:S(2)}, u32[]{:S(2)}) async-start(bf16[4,8,2048]{2,1,0:T(8,128)(2,1)} %bitcast.55), calls=%async_computation.4 | async-start | bytes 262144 | tf_op jit(solution)/shard_map/all_to_all | solution.py:125
  703.1 9.0 %copy-start.3 = (bf16[8,8192]{1,0:T(8,128)(2,1)S(1)}, bf16[8,8192]{1,0:T(8,128)(2,1)}, u32[]{:S(2)}) copy-start(bf16[8,8192]{1,0:T(8,128)(2,1)} %param.7) | copy-start | bytes 393220
  703.1 62.6 %copy-start.5 = (bf16[8,8192]{1,0:T(8,128)(2,1)S(1)}, bf16[8,8192]{1,0:T(8,128)(2,1)}, u32[]{:S(2)}) copy-start(bf16[8,8192]{1,0:T(8,128)(2,1)} %param.13) | copy-start | bytes 393220
Sparse Core Ops, SparseCore 0:
  19.4 40.7 all-gather.4
  62.4 38.9 all-gather.8
  104.5 23.6 reduce-scatter.4
  143.8 234.7 reduce-scatter.10
  391.1 201.5 all-gather.6
  610.0 16.7 all-gather.10
  636.3 63.4 reduce-scatter.8
  703.2 62.4 reduce-scatter.6
where the time goes:
time: 775 us; the launch traced here: 774 us
  waiting for transfers between devices  570 us (74%)
  matrix products  77.4 us (10%)
  blocking collectives  50 us (6%)
  other arithmetic  44.4 us (6%)
  between operations  14.3 us (2%)
  local copies, waits for them, and re-layouts  14 us (2%)
    reduce_scatter x1, waiting for transfers between devices, shards(): lax.psum_scatter(dot_first(activation, grad_panel).astype(jnp.bfloat16),...  228 us
    all_gather x1, waiting for transfers between devices, shards(): w_out_full = lax.all_gather(w_out_e, 'row', axis=1, tiled=True)  202 us
    psum x1, blocking collectives, shards(): lax.psum(jnp.sum(normed_gradient * standardized_input, axis=0), ('row', '...  41.2 us
    all_gather x1, waiting for transfers between devices, shards(): allrows = lax.all_gather(swapped, 'col', axis=0, tiled=True)  34 us
    all_gather x1, waiting for transfers between devices, shards(): grad_panel = lax.all_gather(out_grad, 'col', axis=0, tiled=True)  31.7 us
    reduce_scatter x1, waiting for transfers between devices, shards(): lax.psum_scatter(jnp.dot(byrow, w_in_e, preferred_element_type=jnp.float3...  26.8 us
    dot_general x2, matrix products, dot_last(): lax.dot_general(left, right, (((1,), (1,)), ((), ())), preferred_element_...  25.3 us
    select_n x2, other arithmetic, apply_mask(): jnp.where(mask[:, None, :, None], shaped, jnp.zeros((), weight.dtype))  21.2 us
  transfers between devices with their start and end apart: 9, of which 8 were waited for; matrix products, arithmetic and copies ran while one was open for 10% of the time, Pallas kernels for 0%

commit v1 on v0

v1 whole, which is shorter than its diff:
```python
import jax
import jax.numpy as jnp
from jax import lax
from jax.sharding import PartitionSpec as P

BLOCK = 256
BF16 = jnp.bfloat16
F32 = jnp.float32


def block_mask(pattern, tile_rows):
    iota = jnp.arange(tile_rows, dtype=jnp.int32)
    return jnp.any(pattern[None, :, :] == iota[:, None, None], axis=2)


def apply_mask(weight, mask):
    rows_t, cols_t = mask.shape
    shaped = weight.reshape(rows_t, BLOCK, cols_t, BLOCK)
    kept = jnp.where(mask[:, None, :, None], shaped, jnp.zeros((), weight.dtype))
    return kept.reshape(weight.shape)


def gelu_and_slope(h):
    tanh_v = jnp.tanh(0.7978845608 * (h + 0.044715 * h * h * h))
    value = 0.5 * h * (1.0 + tanh_v)
    slope = 0.5 * (1.0 + tanh_v) + 0.5 * h * (1.0 - tanh_v * tanh_v) * 0.7978845608 * (
        1.0 + 0.134145 * h * h
    )
    return value, slope


def dot(left, right):
    return jnp.dot(left, right, preferred_element_type=F32)


def dot_last(left, right):
    return lax.dot_general(left, right, (((1,), (1,)), ((), ())), preferred_element_type=F32)


def dot_first(left, right):
    return lax.dot_general(left, right, (((0,), (0,)), ((), ())), preferred_element_type=F32)


def swap(value, axis, distance):
    size = lax.axis_size(axis)
    return lax.ppermute(value, axis, [(i, i ^ distance) for i in range(size)])


def halves(value, bit, axis):
    low, high = jnp.split(value, 2, axis=axis)
    return jnp.where(bit, high, low), jnp.where(bit, low, high)


def ordered(mine, other, bit, axis):
    return jnp.where(
        bit,
        jnp.concatenate([other, mine], axis=axis),
        jnp.concatenate([mine, other], axis=axis),
    )


def shards(inputs, layer_norm_gain, w_in, w_out, pattern_in, pattern_out, out_grad):
    n_row = lax.axis_size("row")
    n_col = lax.axis_size("col")
    row_index = lax.axis_index("row")
    col_index = lax.axis_index("col")
    core_bit = row_index % 2 == 1
    far_bit = row_index // 2 == 1
    tok = inputs.shape[0]
    width = inputs.shape[1]
    feat, unit = w_in.shape
    feat_tiles, unit_tiles = feat // BLOCK, unit // BLOCK
    line = [1 << b for b in reversed(range(1, n_col.bit_length() - 1))]

    def to_features(value):
        keep, give = halves(value, far_bit, 1)
        got = swap(give, "row", 2)
        both = ordered(keep, got, far_bit, 0)
        keep, give = halves(both, core_bit, 1)
        return jnp.stack([keep, swap(give, "row", 1)])

    def to_tokens(value):
        got = swap(value[1], "row", 1)
        both = ordered(value[0], got, core_bit, 1)
        keep, give = halves(both, far_bit, 0)
        got = swap(give, "row", 2)
        return ordered(keep, got, far_bit, 1)

    def gather(block):
        own = [block]
        chunks = []
        pairs = [(block, swap(block, "col", 1))]
        for i, distance in enumerate(line):
            got = [swap(v, "col", distance) for v in own] if i == 0 else list(
                swap(jnp.stack(own), "col", distance)
            )
            near = [swap(v, "col", 1) for v in got] if i == 0 else list(
                swap(jnp.stack(got), "col", 1)
            )
            if i == 0:
                chunks.append([block, pairs[0][1], got[0], near[0]])
            else:
                chunks.append([v for pair in zip(got, near) for v in pair])
            own = own + got
        return chunks

    xfloat = inputs.astype(F32)
    centered_input = xfloat - jnp.mean(xfloat, axis=1, keepdims=True)
    inverse_deviation = lax.rsqrt(
        jnp.mean(centered_input * centered_input, axis=1, keepdims=True) + 1e-05
    )
    standardized_input = centered_input * inverse_deviation
    normalized_input = (standardized_input * layer_norm_gain[None, :]).astype(BF16)

    mask_in = lax.dynamic_slice(
        block_mask(pattern_in, width // BLOCK),
        (row_index * feat_tiles, col_index * unit_tiles),
        (feat_tiles, unit_tiles),
    )
    mask_out = lax.dynamic_slice(
        block_mask(pattern_out, n_col * unit_tiles),
        (col_index * unit_tiles, row_index * feat_tiles),
        (unit_tiles, feat_tiles),
    )
    w_in_e = lax.optimization_barrier(apply_mask(w_in, mask_in))
    w_out_e = lax.optimization_barrier(apply_mask(w_out, mask_out))

    x_chunks = gather(to_features(normalized_input))
    g_chunks = gather(to_features(out_grad))

    def sum_over_row(product):
        rounded = product.astype(BF16)
        got = swap(rounded[:, 1], "row", 1)
        pair = product[:, 0] + got.astype(F32)
        far = swap(pair.astype(BF16), "row", 2)
        total = (pair + far.astype(F32)).astype(BF16)
        return jnp.stack([total, swap(total, "row", 1)], axis=1).astype(F32)

    def flat(blocks):
        return jnp.stack(blocks).reshape(-1, blocks[0].shape[-1])

    def shaped(value, count):
        return value.reshape(count, 2, 2 * tok, value.shape[-1])

    acts, d_pres, out_parts, dn_parts = [], [], [], []
    x_flat = [flat(c) for c in x_chunks]
    g_flat = [flat(c) for c in g_chunks]
    for xc, gc, blocks in zip(x_flat, g_flat, x_chunks):
        n = len(blocks)
        pre = sum_over_row(shaped(dot(xc, w_in_e), n)).reshape(-1, unit)
        value, slope = gelu_and_slope(pre)
        act = value.astype(BF16)
        d_act = sum_over_row(shaped(dot_last(gc, w_out_e), n)).reshape(-1, unit)
        d_pre = (d_act * slope).astype(BF16)
        acts.append(act)
        d_pres.append(d_pre)
        out_parts.append(shaped(dot(act, w_out_e), n))
        dn_parts.append(shaped(dot_last(d_pre, w_in_e), n))

    def scatter(parts):
        held = []
        for part in parts:
            pairs = part.reshape((-1, 2) + part.shape[1:])
            got = swap(pairs[:, 1].astype(BF16), "col", 1)
            held.append(pairs[:, 0] + got.astype(F32))
        total = jnp.concatenate(held, axis=0)
        for distance in reversed(line):
            low, high = jnp.split(total, 2, axis=0)
            got = swap(high.astype(BF16), "col", distance)
            total = low + got.astype(F32)
        return total[0]

    summed = scatter(out_parts)
    output = (xfloat + to_tokens(summed.astype(BF16)).astype(F32)).astype(BF16)
    normed_gradient = to_tokens(scatter(dn_parts).astype(BF16)).astype(F32)

    gain_part = sum(
        jnp.sum(part.reshape(-1, feat) * xc.astype(F32), axis=0)
        for part, xc in zip(dn_parts, x_flat)
    )
    for b in range(n_col.bit_length() - 1):
        gain_part = gain_part + swap(gain_part, "col", 1 << b)
    pair = ordered(gain_part, swap(gain_part, "row", 1), core_bit, 0)
    norm_gain_gradient = ordered(pair, swap(pair, "row", 2), far_bit, 0) / layer_norm_gain

    x_all = jnp.concatenate(x_flat)
    g_all = jnp.concatenate(g_flat)
    grad_w_out = apply_mask(dot_first(jnp.concatenate(acts), g_all).astype(BF16), mask_out)
    grad_w_in = apply_mask(dot_first(x_all, jnp.concatenate(d_pres)).astype(BF16), mask_in)

    gain_scaled = normed_gradient * layer_norm_gain[None, :]
    backward_result = inverse_deviation * (
        gain_scaled
        - jnp.mean(gain_scaled, axis=1, keepdims=True)
        - standardized_input * jnp.mean(gain_scaled * standardized_input, axis=1, keepdims=True)
    )
    grad_inputs = (out_grad.astype(F32) + backward_result).astype(BF16)
    return (output, grad_inputs, grad_w_in, grad_w_out, norm_gain_gradient)


def solution(mesh):
    in_specs = (
        P(("row", "col"), None),
        P(),
        P("row", "col"),
        P("col", "row"),
        P(),
        P(),
        P(("row", "col"), None),
    )
    out_specs = (
        P(("row", "col"), None),
        P(("row", "col"), None),
        P("row", "col"),
        P("col", "row"),
        P(),
    )
    return jax.shard_map(shards, mesh=mesh, in_specs=in_specs, out_specs=out_specs, check_vma=False)
```

time: 775 us -> 164 us (0.21)
  waiting for transfers between devices: 570 us -> 50.3 us
  blocking collectives: 50 us -> 0 us
  matrix products: 77.4 us -> 31.2 us
  starting transfers between devices: 4.05 us -> 39.4 us
  other arithmetic: 44.4 us -> 29.9 us
  between operations: 14.3 us -> 1.39 us
    reduce_scatter x4 -> x0, waiting for transfers between devices: 285 us -> none  [the longest x1 228 us: shards(): lax.psum_scatter(dot_first(activation, grad_panel).astype(jnp.bfloat16),...]
    all_gather x4 -> x0, waiting for transfers between devices: 284 us -> none  [the longest x1 202 us: shards(): w_out_full = lax.all_gather(w_out_e, 'row', axis=1, tiled=True)]
    ppermute x0 -> x43, waiting for transfers between devices: none -> 50.3 us  [swap(): return lax.ppermute(value, axis, [(i, i ^ distance) for i in range(size)])]
    psum x1 -> x0, blocking collectives: 41.2 us -> none  [shards(): lax.psum(jnp.sum(normed_gradient * standardized_input, axis=0), ('row', '...]
    ppermute x0 -> x43, starting transfers between devices: none -> 39.4 us  [swap(): return lax.ppermute(value, axis, [(i, i ^ distance) for i in range(size)])]
    dot_general x3 -> x4, matrix products: 36.7 us -> 10 us  [dot(): return jnp.dot(left, right, preferred_element_type=F32)]
    reduce_sum x2 -> x0, other arithmetic: 17 us -> none  [the longest x1 16.7 us: shards(): w1_sum = jnp.sum(panel_rounded.astype(jnp.float32), axis=0)]
    dot_general x2 -> x4, matrix products: 25.3 us -> 11.8 us  [dot_last(): lax.dot_general(left, right, (((1,), (1,)), ((), ())), preferred_element_...]
  transfers between devices with their start and end apart: 9 -> 43, of which waited for: 8 -> 16; matrix products, arithmetic and copies ran while one was open for 10% -> 42% of each run, Pallas kernels for 0% -> 0%
where the time goes in v1:
time: 164 us
  waiting for transfers between devices  50.3 us (31%)
  starting transfers between devices  39.4 us (24%)
  matrix products  31.2 us (19%)
  other arithmetic  29.9 us (18%)
  local copies, waits for them, and re-layouts  11.6 us (7%)
    ppermute x43, waiting for transfers between devices, swap(): return lax.ppermute(value, axis, [(i, i ^ distance) for i in range(size)])  50.3 us
    ppermute x43, starting transfers between devices, swap(): return lax.ppermute(value, axis, [(i, i ^ distance) for i in range(size)])  39.4 us
    select_n x2, other arithmetic, apply_mask(): jnp.where(mask[:, None, :, None], shaped, jnp.zeros((), weight.dtype))  17.7 us
    dot_general x4, matrix products, dot_last(): lax.dot_general(left, right, (((1,), (1,)), ((), ())), preferred_element_...  11.8 us
    dot_general x4, matrix products, dot(): return jnp.dot(left, right, preferred_element_type=F32)  10 us
    dot_general x2, matrix products, dot_first(): lax.dot_general(left, right, (((0,), (0,)), ((), ())), preferred_element_...  9.39 us
    unnamed x24, local copies, waits for them, and re-layouts  8.37 us
  transfers between devices with their start and end apart: 43, of which 16 were waited for; matrix products, arithmetic and copies ran while one was open for 42% of the time, Pallas kernels for 0%

profile of v1, /device:TPU:0, one launch (start us, length us, event | category | flops | bytes accessed | tf_op | source)
XLA Modules:
  0.0 163.9 jit_solution(273767552384614500)
XLA Ops:
  0.7 1.1 convert_reduce_fusion
  1.8 1.2 fusion.78
  2.9 1.0 fusion.72
  4.0 3.0 %collective-permute-start = (bf16[8,4096]{1,0:T(8,128)(2,1)S(1)}, bf16[8,4096]{1,0:T(8,128)(2,1)S(1)}, u32[]{:S(2)}, u32[]{:S(2)}) collective-permute-start(bf16[8,4096]{1,0:T(8,128)(2,1)S(1)} %get-tuple-element.39), channel_id=1, source_target_pairs={{0,16},{8,24},{16,0},{24,8},{1,17},{9,25},{17,1},{25,9},{2,18},{10... | collective-permute-start | bytes 196616 | tf_op jit(solution)/shard_map/ppermute | solution.py:46
  8.8 1.1 broadcast_in_dim.44
  10.0 4.1 %copy.82 = pred[256,8,8,256]{3,1,2,0:T(8,128)(4,1)} copy(pred[256,8,8,256]{3,2,1,0:T(8,128)(4,1)S(1)} %bitcast.197) | data formatting | bytes 8388608
  14.5 1.1 broadcast_in_dim.47
  15.7 4.2 %copy.83 = pred[256,8,8,256]{3,1,2,0:T(8,128)(4,1)} copy(pred[256,8,8,256]{3,2,1,0:T(8,128)(4,1)S(1)} %bitcast.198) | data formatting | bytes 8388608
  19.9 8.9 %broadcast_select_fusion.1 = bf16[2048,2048]{1,0:T(8,128)(2,1)} fusion(pred[2048,2048]{1,0:T(8,128)(4,1)} %bitcast.195, bf16[2048,2048]{1,0:T(8,128)(2,1)} %param.9), kind=kLoop, calls=%fused_computation.15 | loop fusion | flops 4194304 | bytes 20971520 | tf_op jit(solution)/shard_map/jit(_where)/select_n | solution.py:19
  28.7 8.9 %broadcast_select_fusion = bf16[2048,2048]{1,0:T(8,128)(2,1)} fusion(pred[2048,2048]{1,0:T(8,128)(4,1)} %bitcast.193, bf16[2048,2048]{1,0:T(8,128)(2,1)} %param.10), kind=kLoop, calls=%fused_computation.14 | loop fusion | flops 4194304 | bytes 20971520 | tf_op jit(solution)/shard_map/jit(_where)/select_n | solution.py:19
  39.0 3.1 %collective-permute-start.3 = (bf16[2,16,2048]{2,1,0:T(8,128)(2,1)S(1)}, bf16[2,16,2048]{2,1,0:T(8,128)(2,1)S(1)}, u32[]{:S(2)}, u32[]{:S(2)}) collective-permute-start(bf16[2,16,2048]{2,1,0:T(8,128)(2,1)S(1)} %get-tuple-element.36), channel_id=1, source_target_pairs={{0,4},{1,5},{2,6},{3,7},{4,0},{5,1},{6,2},{7,3},{8,12},{9,13},{10,... | collective-permute-start | bytes 393224 | tf_op jit(solution)/shard_map/ppermute | solution.py:46
  42.1 1.5 collective-permute-start.2
  44.3 7.7 %collective-permute-done.3 = bf16[2,16,2048]{2,1,0:T(8,128)(2,1)S(1)} collective-permute-done((bf16[2,16,2048]{2,1,0:T(8,128)(2,1)S(1)}, bf16[2,16,2048]{2,1,0:T(8,128)(2,1)S(1)}, u32[]{:S(2)}, u32[]{:S(2)}) %collective-permute-start.3) | collective-permute-done | bytes 131104 | tf_op jit(solution)/shard_map/ppermute | solution.py:46
  52.5 1.6 collective-permute-start.4
  54.5 1.7 %collective-permute-start.28 = (bf16[2,2,16,2048]{3,2,1,0:T(8,128)(2,1)S(1)}, bf16[2,2,16,2048]{3,2,1,0:T(8,128)(2,1)S(1)}, u32[]{:S(2)}, u32[]{:S(2)}) collective-permute-start(bf16[2,2,16,2048]{3,2,1,0:T(8,128)(2,1)S(1)} %pad_maximum_fusion.5), channel_id=1, source_target_pairs={{0,2},{1,3},{2,0},{3,1},{4,6},{5,7},{6,4},{7,5},{8,10},{9,11},{10,... | collective-permute-start | bytes 786440 | tf_op jit(solution)/shard_map/ppermute | solution.py:46
  57.6 4.8 %fusion.10 = f32[4,2,16,2048]{3,2,1,0:T(8,128)S(1)} fusion(bf16[2048,2048]{1,0:T(8,128)(2,1)} %broadcast_select_fusion.1, bf16[1,2,16,2048]{3,2,1,0:T(8,128)(2,1)S(1)} %bitcast.233, bf16[1,2,16,2048]{3,2,1,0:T(8,128)(2,1)S(1)} %bitcast.216, bf16[1,2,16,2048]{3,2,1,0:T(8,128)(2,1)S(1)} %bitcast.227, bf16[1,2,16,2048]{3,2,1,0:T(8,128)(2,1)S(1)} %get-tuple-element.35), kind=kOutput, calls=%fused_computation.10 | convolution fusion | flops 1074528256 | bytes 9961472 | tf_op jit(solution)/shard_map/dot_general | solution.py:33
  62.6 3.1 %fusion.2 = f32[4,2,16,2048]{3,2,1,0:T(8,128)S(1)} fusion(bf16[2048,2048]{1,0:T(8,128)(2,1)S(1)} %bitcast.200, bf16[1,2,16,2048]{3,2,1,0:T(8,128)(2,1)S(1)} %bitcast.231, bf16[1,2,16,2048]{3,2,1,0:T(8,128)(2,1)S(1)} %bitcast.219, bf16[1,2,16,2048]{3,2,1,0:T(8,128)(2,1)S(1)} %bitcast.229, bf16[1,2,16,2048]{3,2,1,0:T(8,128)(2,1)S(1)} %get-tuple-element.25), kind=kOutput, calls=%fused_computation.2 | convolution fusion | flops 1074528256 | bytes 9961472 | tf_op jit(solution)/shard_map/dot_general | solution.py:37
  66.4 1.6 collective-permute-start.10
  68.6 1.6 collective-permute-start.6
  70.9 4.7 %collective-permute-done.10 = bf16[2,2,16,2048]{3,2,1,0:T(8,128)(2,1)S(1)} collective-permute-done((bf16[2,2,16,2048]{3,2,1,0:T(8,128)(2,1)S(1)}, bf16[2,2,16,2048]{3,2,1,0:T(8,128)(2,1)S(1)}, u32[]{:S(2)}, u32[]{:S(2)}) %collective-permute-start.10) | collective-permute-done | bytes 262176 | tf_op jit(solution)/shard_map/ppermute | solution.py:46
  75.7 1.3 fusion.8
  77.2 3.1 %collective-permute-done.29 = bf16[2,2,16,2048]{3,2,1,0:T(8,128)(2,1)S(1)} collective-permute-done((bf16[2,2,16,2048]{3,2,1,0:T(8,128)(2,1)S(1)}, bf16[2,2,16,2048]{3,2,1,0:T(8,128)(2,1)S(1)}, u32[]{:S(2)}, u32[]{:S(2)}) %collective-permute-start.29) | collective-permute-done | bytes 262176 | tf_op jit(solution)/shard_map/ppermute | solution.py:46
  80.3 2.9 %fusion = f32[4,2,16,2048]{3,2,1,0:T(8,128)S(1)} fusion(bf16[2048,2048]{1,0:T(8,128)(2,1)S(1)} %bitcast.200, bf16[1,2,16,2048]{3,2,1,0:T(8,128)(2,1)S(1)} %get-tuple-element.14, bf16[1,2,16,2048]{3,2,1,0:T(8,128)(2,1)S(1)} %get-tuple-element.12, bf16[1,2,16,2048]{3,2,1,0:T(8,128)(2,1)S(1)} %get-tuple-element.13, bf16[1,2,16,2048]{3,2,1,0:T(8,128)(2,1)S(1)} %get-tuple-element.11), kind=kOutput, calls=%fused_computation | convolution fusion | flops 1074528256 | bytes 9961472 | tf_op jit(solution)/shard_map/dot_general | solution.py:37
  84.3 1.6 collective-permute-start.12
  87.6 2.9 %multiply_reduce_fusion.1 = (f32[2048]{0:T(1024)S(1)}, f32[128,2048]{1,0:T(8,128)S(1)}) fusion(bf16[4,2,16,2048]{3,2,1,0:T(8,128)(2,1)S(1)} %pad_maximum_fusion, bf16[128,2048]{1,0:T(8,128)(2,1)S(1)} %get-tuple-element.8, bf16[2048,2048]{1,0:T(8,128)(2,1)S(1)} %bitcast.192), kind=kOutput, calls=%fused_computation.69 | convolution fusion | flops 1074526208 | bytes 10493952 | tf_op jit(solution)/shard_map/dot_general | solution.py:37
  90.5 1.6 collective-permute-start.27
  92.1 1.5 fusion.6
  93.8 4.9 %collective-permute-done.31 = bf16[4,16,2048]{2,1,0:T(8,128)(2,1)S(1)} collective-permute-done((bf16[4,16,2048]{2,1,0:T(8,128)(2,1)S(1)}, bf16[4,16,2048]{2,1,0:T(8,128)(2,1)S(1)}, u32[]{:S(2)}, u32[]{:S(2)}) %collective-permute-start.31) | collective-permute-done | bytes 262176 | tf_op jit(solution)/shard_map/ppermute | solution.py:46
  98.9 1.6 collective-permute-start.8
  101.7 2.9 %multiply_reduce_fusion = (f32[2048]{0:T(1024)S(1)}, f32[128,2048]{1,0:T(8,128)S(1)}) fusion(bf16[4,2,16,2048]{3,2,1,0:T(8,128)(2,1)S(1)} %pad_maximum_fusion.1, bf16[128,2048]{1,0:T(8,128)(2,1)S(1)} %get-tuple-element.10, bf16[2048,2048]{1,0:T(8,128)(2,1)S(1)} %bitcast.192), kind=kOutput, calls=%fused_computation.68 | convolution fusion | flops 1074526208 | bytes 10493952 | tf_op jit(solution)/shard_map/dot_general | solution.py:37
  104.7 1.3 collective-permute-start.38
  106.9 1.5 collective-permute-done.38
  108.4 3.2 %collective-permute-start.39 = (f32[2048]{0:T(1024)S(1)}, f32[2048]{0:T(1024)S(1)}, u32[]{:S(2)}, u32[]{:S(2)}) collective-permute-start(f32[2048]{0:T(1024)S(1)} %add.160), channel_id=1, source_target_pairs={{0,2},{1,3},{2,0},{3,1},{4,6},{5,7},{6,4},{7,5},{8,10},{9,11},{10,... | collective-permute-start | bytes 24584 | tf_op jit(solution)/shard_map/ppermute | solution.py:46
  111.7 2.4 %fusion.4 = f32[2,2,2,16,2048]{4,3,2,0,1:T(8,128)S(1)} fusion(bf16[2048,2048]{1,0:T(8,128)(2,1)S(1)} %bitcast.200, bf16[2,2,1,16,2048]{4,3,2,1,0:T(8,128)(2,1)} %bitcast.222, bf16[2,2,1,16,2048]{4,3,2,1,0:T(8,128)(2,1)S(1)} %bitcast.208), kind=kOutput, calls=%fused_computation.4 | convolution fusion | flops 1076625408 | bytes 9961472 | tf_op jit(solution)/shard_map/dot_general | solution.py:33
  114.1 1.3 collective-permute-start.40
  115.5 1.4 collective-permute-start.14
  116.9 1.9 %collective-permute-done.40 = f32[2048]{0:T(1024)S(1)} collective-permute-done((f32[2048]{0:T(1024)S(1)}, f32[2048]{0:T(1024)S(1)}, u32[]{:S(2)}, u32[]{:S(2)}) %collective-permute-start.40) | collective-permute-done | bytes 8224 | tf_op jit(solution)/shard_map/ppermute | solution.py:46
  118.8 4.7 %convert_select_fusion.1 = bf16[2048,2048]{1,0:T(8,128)(2,1)} fusion(pred[2048,2048]{1,0:T(8,128)(4,1)S(1)} %bitcast.196, bf16[128,2048]{1,0:T(8,128)(2,1)S(1)} %bitcast.206, bf16[128,2048]{1,0:T(8,128)(2,1)S(1)} %bitcast.205, bf16[128,2048]{1,0:T(8,128)(2,1)S(1)} %get-tuple-element.10, bf16[128,2048]{1,0:T(8,128)(2,1)S(1)} %get-tuple-element.8), kind=kOutput, calls=%fused_computation.13 | convolution fusion | flops 2160066560 | bytes 14680064 | tf_op jit(solution)/shard_map/dot_general | solution.py:41
  123.5 1.6 collective-permute-start.42
  125.0 4.7 %convert_select_fusion = bf16[2048,2048]{1,0:T(8,128)(2,1)} fusion(pred[2048,2048]{1,0:T(8,128)(4,1)S(1)} %bitcast.194, bf16[128,2048]{1,0:T(8,128)(2,1)S(1)} %get-tuple-element.9, bf16[128,2048]{1,0:T(8,128)(2,1)S(1)} %get-tuple-element.7, bf16[128,2048]{1,0:T(8,128)(2,1)S(1)} %bitcast.214, bf16[128,2048]{1,0:T(8,128)(2,1)S(1)} %bitcast.213), kind=kOutput, calls=%fused_computation.12 | convolution fusion | flops 2160066560 | bytes 14680064 | tf_op jit(solution)/shard_map/dot_general | solution.py:41
  130.4 1.0 fusion.49
  131.4 1.2 collective-permute-start.34
  133.6 7.0 %collective-permute-done.34 = bf16[2,2,16,2048]{3,2,1,0:T(8,128)(2,1)S(1)} collective-permute-done((bf16[2,2,16,2048]{3,2,1,0:T(8,128)(2,1)S(1)}, bf16[2,2,16,2048]{3,2,1,0:T(8,128)(2,1)S(1)}, u32[]{:S(2)}, u32[]{:S(2)}) %collective-permute-start.34) | collective-permute-done | bytes 262176 | tf_op jit(solution)/shard_map/ppermute | solution.py:46
  140.7 1.3 collective-permute-start.35
  142.0 5.9 %collective-permute-done.15 = bf16[2,2,16,2048]{3,2,1,0:T(8,128)(2,1)S(1)} collective-permute-done((bf16[2,2,16,2048]{3,2,1,0:T(8,128)(2,1)S(1)}, bf16[2,2,16,2048]{3,2,1,0:T(8,128)(2,1)S(1)}, u32[]{:S(2)}, u32[]{:S(2)}) %collective-permute-start.15) | collective-permute-done | bytes 262176 | tf_op jit(solution)/shard_map/ppermute | solution.py:46
  147.9 1.0 fusion.58
  149.6 7.3 %collective-permute-done.16 = bf16[1,2,16,2048]{3,2,1,0:T(8,128)(2,1)S(1)} collective-permute-done((bf16[1,2,16,2048]{3,2,1,0:T(8,128)(2,1)S(1)}, bf16[1,2,16,2048]{3,2,1,0:T(8,128)(2,1)S(1)}, u32[]{:S(2)}, u32[]{:S(2)}) %collective-permute-start.16) | collective-permute-done | bytes 131104 | tf_op jit(solution)/shard_map/ppermute | solution.py:46
  159.3 2.7 %collective-permute-done.37 = bf16[8,4096]{1,0:T(8,128)(2,1)S(1)} collective-permute-done((bf16[8,4096]{1,0:T(8,128)(2,1)S(1)}, bf16[8,4096]{1,0:T(8,128)(2,1)S(1)}, u32[]{:S(2)}, u32[]{:S(2)}) %collective-permute-start.37) | collective-permute-done | bytes 65568 | tf_op jit(solution)/shard_map/ppermute | solution.py:46
  (155 shorter events, 20.7 us)
Async XLA Ops:
  0.6 13.5 %copy-start.6 = (s32[32,32]{1,0:T(8,128)S(1)}, s32[32,32]{1,0:T(8,128)}, u32[]{:S(2)}) copy-start(s32[32,32]{1,0:T(8,128)} %param.12) | copy-start | bytes 12292
  4.0 33.6 %collective-permute-start = (bf16[8,4096]{1,0:T(8,128)(2,1)S(1)}, bf16[8,4096]{1,0:T(8,128)(2,1)S(1)}, u32[]{:S(2)}, u32[]{:S(2)}) collective-permute-start(bf16[8,4096]{1,0:T(8,128)(2,1)S(1)} %get-tuple-element.39), channel_id=1, source_target_pairs={{0,16},{8,24},{16,0},{24,8},{1,17},{9,25},{17,1},{25,9},{2,18},{10... | collective-permute-start | bytes 196616 | tf_op jit(solution)/shard_map/ppermute | solution.py:46
  7.9 29.9 %collective-permute-start.19 = (bf16[8,4096]{1,0:T(8,128)(2,1)S(1)}, bf16[8,4096]{1,0:T(8,128)(2,1)S(1)}, u32[]{:S(2)}, u32[]{:S(2)}) collective-permute-start(bf16[8,4096]{1,0:T(8,128)(2,1)S(1)} %get-tuple-element.29), channel_id=1, source_target_pairs={{0,16},{8,24},{16,0},{24,8},{1,17},{9,25},{17,1},{25,9},{2,18},{10... | collective-permute-start | bytes 196616 | tf_op jit(solution)/shard_map/ppermute | solution.py:46
  37.6 25.0 %slice-start.2 = ((s8[8388608]{0:T(1024)(128)(4,1)}), s8[4194304]{0:T(1024)(128)(4,1)S(1)}, s32[]{:S(2)}) async-start(s8[8388608]{0:T(1024)(128)(4,1)} %bitcast.199), calls=%async_computation.2 | async-start | bytes 8388608
  37.7 1.3 collective-permute-start.1
  37.8 5.8 %collective-permute-start.20 = (bf16[16,2048]{1,0:T(8,128)(2,1)S(1)}, bf16[16,2048]{1,0:T(8,128)(2,1)S(1)}, u32[]{:S(2)}, u32[]{:S(2)}) collective-permute-start(bf16[16,2048]{1,0:T(8,128)(2,1)S(1)} %get-tuple-element.28), channel_id=1, source_target_pairs={{0,8},{8,0},{16,24},{24,16},{1,9},{9,1},{17,25},{25,17},{2,10},{10... | collective-permute-start | bytes 196616 | tf_op jit(solution)/shard_map/ppermute | solution.py:46
  39.0 13.0 %collective-permute-start.3 = (bf16[2,16,2048]{2,1,0:T(8,128)(2,1)S(1)}, bf16[2,16,2048]{2,1,0:T(8,128)(2,1)S(1)}, u32[]{:S(2)}, u32[]{:S(2)}) collective-permute-start(bf16[2,16,2048]{2,1,0:T(8,128)(2,1)S(1)} %get-tuple-element.36), channel_id=1, source_target_pairs={{0,4},{1,5},{2,6},{3,7},{4,0},{5,1},{6,2},{7,3},{8,12},{9,13},{10,... | collective-permute-start | bytes 393224 | tf_op jit(solution)/shard_map/ppermute | solution.py:46
  42.1 14.0 %collective-permute-start.2 = (bf16[2,16,2048]{2,1,0:T(8,128)(2,1)S(1)}, bf16[2,16,2048]{2,1,0:T(8,128)(2,1)S(1)}, u32[]{:S(2)}, u32[]{:S(2)}) collective-permute-start(bf16[2,16,2048]{2,1,0:T(8,128)(2,1)S(1)} %get-tuple-element.36), channel_id=1, source_target_pairs={{0,1},{1,0},{2,3},{3,2},{4,5},{5,4},{6,7},{7,6},{8,9},{9,8},{10,11... | collective-permute-start | bytes 393224 | tf_op jit(solution)/shard_map/ppermute | solution.py:46
  43.7 10.8 %collective-permute-start.22 = (bf16[2,16,2048]{2,1,0:T(8,128)(2,1)S(1)}, bf16[2,16,2048]{2,1,0:T(8,128)(2,1)S(1)}, u32[]{:S(2)}, u32[]{:S(2)}) collective-permute-start(bf16[2,16,2048]{2,1,0:T(8,128)(2,1)S(1)} %get-tuple-element.26), channel_id=1, source_target_pairs={{0,4},{1,5},{2,6},{3,7},{4,0},{5,1},{6,2},{7,3},{8,12},{9,13},{10,... | collective-permute-start | bytes 393224 | tf_op jit(solution)/shard_map/ppermute | solution.py:46
  44.1 18.5 %collective-permute-start.21 = (bf16[2,16,2048]{2,1,0:T(8,128)(2,1)S(1)}, bf16[2,16,2048]{2,1,0:T(8,128)(2,1)S(1)}, u32[]{:S(2)}, u32[]{:S(2)}) collective-permute-start(bf16[2,16,2048]{2,1,0:T(8,128)(2,1)S(1)} %get-tuple-element.26), channel_id=1, source_target_pairs={{0,1},{1,0},{2,3},{3,2},{4,5},{5,4},{6,7},{7,6},{8,9},{9,8},{10,11... | collective-permute-start | bytes 393224 | tf_op jit(solution)/shard_map/ppermute | solution.py:46
  52.1 14.3 %collective-permute-start.9 = (bf16[2,2,16,2048]{3,2,1,0:T(8,128)(2,1)S(1)}, bf16[2,2,16,2048]{3,2,1,0:T(8,128)(2,1)S(1)}, u32[]{:S(2)}, u32[]{:S(2)}) collective-permute-start(bf16[2,2,16,2048]{3,2,1,0:T(8,128)(2,1)S(1)} %pad_maximum_fusion.4), channel_id=1, source_target_pairs={{0,2},{1,3},{2,0},{3,1},{4,6},{5,7},{6,4},{7,5},{8,10},{9,11},{10,... | collective-permute-start | bytes 786440 | tf_op jit(solution)/shard_map/ppermute | solution.py:46
  52.5 5.1 %collective-permute-start.4 = (bf16[2,16,2048]{2,1,0:T(8,128)(2,1)S(1)}, bf16[2,16,2048]{2,1,0:T(8,128)(2,1)S(1)}, u32[]{:S(2)}, u32[]{:S(2)}) collective-permute-start(bf16[2,16,2048]{2,1,0:T(8,128)(2,1)S(1)} %collective-permute-done.3), channel_id=1, source_target_pairs={{0,1},{1,0},{2,3},{3,2},{4,5},{5,4},{6,7},{7,6},{8,9},{9,8},{10,11... | collective-permute-start | bytes 393224 | tf_op jit(solution)/shard_map/ppermute | solution.py:46
  54.5 13.5 %collective-permute-start.28 = (bf16[2,2,16,2048]{3,2,1,0:T(8,128)(2,1)S(1)}, bf16[2,2,16,2048]{3,2,1,0:T(8,128)(2,1)S(1)}, u32[]{:S(2)}, u32[]{:S(2)}) collective-permute-start(bf16[2,2,16,2048]{3,2,1,0:T(8,128)(2,1)S(1)} %pad_maximum_fusion.5), channel_id=1, source_target_pairs={{0,2},{1,3},{2,0},{3,1},{4,6},{5,7},{6,4},{7,5},{8,10},{9,11},{10,... | collective-permute-start | bytes 786440 | tf_op jit(solution)/shard_map/ppermute | solution.py:46
  56.1 6.5 %collective-permute-start.23 = (bf16[2,16,2048]{2,1,0:T(8,128)(2,1)S(1)}, bf16[2,16,2048]{2,1,0:T(8,128)(2,1)S(1)}, u32[]{:S(2)}, u32[]{:S(2)}) collective-permute-start(bf16[2,16,2048]{2,1,0:T(8,128)(2,1)S(1)} %collective-permute-done.22), channel_id=1, source_target_pairs={{0,1},{1,0},{2,3},{3,2},{4,5},{5,4},{6,7},{7,6},{8,9},{9,8},{10,11... | collective-permute-start | bytes 393224 | tf_op jit(solution)/shard_map/ppermute | solution.py:46
  62.4 6.2 %collective-permute-start.5 = (bf16[4,16,2048]{2,1,0:T(8,128)(2,1)S(1)}, bf16[4,16,2048]{2,1,0:T(8,128)(2,1)S(1)}, u32[]{:S(2)}, u32[]{:S(2)}) collective-permute-start(bf16[4,16,2048]{2,1,0:T(8,128)(2,1)S(1)} %fusion.80), channel_id=1, source_target_pairs={{0,8},{8,0},{16,24},{24,16},{1,9},{9,1},{17,25},{25,17},{2,10},{10... | collective-permute-start | bytes 786440 | tf_op jit(solution)/shard_map/ppermute | solution.py:46
  65.7 4.5 %collective-permute-start.24 = (bf16[4,16,2048]{2,1,0:T(8,128)(2,1)S(1)}, bf16[4,16,2048]{2,1,0:T(8,128)(2,1)S(1)}, u32[]{:S(2)}, u32[]{:S(2)}) collective-permute-start(bf16[4,16,2048]{2,1,0:T(8,128)(2,1)S(1)} %fusion.84), channel_id=1, source_target_pairs={{0,8},{8,0},{16,24},{24,16},{1,9},{9,1},{17,25},{25,17},{2,10},{10... | collective-permute-start | bytes 786440 | tf_op jit(solution)/shard_map/ppermute | solution.py:46
  66.4 9.2 %collective-permute-start.10 = (bf16[2,2,16,2048]{3,2,1,0:T(8,128)(2,1)S(1)}, bf16[2,2,16,2048]{3,2,1,0:T(8,128)(2,1)S(1)}, u32[]{:S(2)}, u32[]{:S(2)}) collective-permute-start(bf16[2,2,16,2048]{3,2,1,0:T(8,128)(2,1)S(1)} %collective-permute-done.9), channel_id=1, source_target_pairs={{0,1},{1,0},{2,3},{3,2},{4,5},{5,4},{6,7},{7,6},{8,9},{9,8},{10,11... | collective-permute-start | bytes 786440 | tf_op jit(solution)/shard_map/ppermute | solution.py:46
  68.0 12.3 %collective-permute-start.29 = (bf16[2,2,16,2048]{3,2,1,0:T(8,128)(2,1)S(1)}, bf16[2,2,16,2048]{3,2,1,0:T(8,128)(2,1)S(1)}, u32[]{:S(2)}, u32[]{:S(2)}) collective-permute-start(bf16[2,2,16,2048]{3,2,1,0:T(8,128)(2,1)S(1)} %collective-permute-done.28), channel_id=1, source_target_pairs={{0,1},{1,0},{2,3},{3,2},{4,5},{5,4},{6,7},{7,6},{8,9},{9,8},{10,11... | collective-permute-start | bytes 786440 | tf_op jit(solution)/shard_map/ppermute | solution.py:46
  68.6 14.8 %collective-permute-start.6 = (bf16[4,16,2048]{2,1,0:T(8,128)(2,1)S(1)}, bf16[4,16,2048]{2,1,0:T(8,128)(2,1)S(1)}, u32[]{:S(2)}, u32[]{:S(2)}) collective-permute-start(bf16[4,16,2048]{2,1,0:T(8,128)(2,1)S(1)} %fusion.63), channel_id=1, source_target_pairs={{0,16},{8,24},{16,0},{24,8},{1,17},{9,25},{17,1},{25,9},{2,18},{10... | collective-permute-start | bytes 786440 | tf_op jit(solution)/shard_map/ppermute | solution.py:46
  70.3 13.8 %collective-permute-start.25 = (bf16[4,16,2048]{2,1,0:T(8,128)(2,1)S(1)}, bf16[4,16,2048]{2,1,0:T(8,128)(2,1)S(1)}, u32[]{:S(2)}, u32[]{:S(2)}) collective-permute-start(bf16[4,16,2048]{2,1,0:T(8,128)(2,1)S(1)} %fusion.65), channel_id=1, source_target_pairs={{0,16},{8,24},{16,0},{24,8},{1,17},{9,25},{17,1},{25,9},{2,18},{10... | collective-permute-start | bytes 786440 | tf_op jit(solution)/shard_map/ppermute | solution.py:46
  77.0 7.2 %collective-permute-start.11 = (bf16[4,16,2048]{2,1,0:T(8,128)(2,1)S(1)}, bf16[4,16,2048]{2,1,0:T(8,128)(2,1)S(1)}, u32[]{:S(2)}, u32[]{:S(2)}) collective-permute-start(bf16[4,16,2048]{2,1,0:T(8,128)(2,1)S(1)} %fusion.82), channel_id=1, source_target_pairs={{0,8},{8,0},{16,24},{24,16},{1,9},{9,1},{17,25},{25,17},{2,10},{10... | collective-permute-start | bytes 786440 | tf_op jit(solution)/shard_map/ppermute | solution.py:46
  83.3 2.6 %collective-permute-start.30 = (bf16[4,16,2048]{2,1,0:T(8,128)(2,1)S(1)}, bf16[4,16,2048]{2,1,0:T(8,128)(2,1)S(1)}, u32[]{:S(2)}, u32[]{:S(2)}) collective-permute-start(bf16[4,16,2048]{2,1,0:T(8,128)(2,1)S(1)} %fusion.85), channel_id=1, source_target_pairs={{0,8},{8,0},{16,24},{24,16},{1,9},{9,1},{17,25},{25,17},{2,10},{10... | collective-permute-start | bytes 786440 | tf_op jit(solution)/shard_map/ppermute | solution.py:46
  83.5 3.0 %collective-permute-start.7 = (bf16[4,16,2048]{2,1,0:T(8,128)(2,1)S(1)}, bf16[4,16,2048]{2,1,0:T(8,128)(2,1)S(1)}, u32[]{:S(2)}, u32[]{:S(2)}) collective-permute-start(bf16[4,16,2048]{2,1,0:T(8,128)(2,1)S(1)} %add_convert_fusion.3), channel_id=1, source_target_pairs={{0,8},{8,0},{16,24},{24,16},{1,9},{9,1},{17,25},{25,17},{2,10},{10... | collective-permute-start | bytes 786440 | tf_op jit(solution)/shard_map/ppermute | solution.py:46
  84.2 2.5 %collective-permute-start.26 = (bf16[4,16,2048]{2,1,0:T(8,128)(2,1)S(1)}, bf16[4,16,2048]{2,1,0:T(8,128)(2,1)S(1)}, u32[]{:S(2)}, u32[]{:S(2)}) collective-permute-start(bf16[4,16,2048]{2,1,0:T(8,128)(2,1)S(1)} %add_convert_fusion.1), channel_id=1, source_target_pairs={{0,8},{8,0},{16,24},{24,16},{1,9},{9,1},{17,25},{25,17},{2,10},{10... | collective-permute-start | bytes 786440 | tf_op jit(solution)/shard_map/ppermute | solution.py:46
  84.3 9.3 %collective-permute-start.12 = (bf16[4,16,2048]{2,1,0:T(8,128)(2,1)S(1)}, bf16[4,16,2048]{2,1,0:T(8,128)(2,1)S(1)}, u32[]{:S(2)}, u32[]{:S(2)}) collective-permute-start(bf16[4,16,2048]{2,1,0:T(8,128)(2,1)S(1)} %fusion.64), channel_id=1, source_target_pairs={{0,16},{8,24},{16,0},{24,8},{1,17},{9,25},{17,1},{25,9},{2,18},{10... | collective-permute-start | bytes 786440 | tf_op jit(solution)/shard_map/ppermute | solution.py:46
  85.9 12.7 %collective-permute-start.31 = (bf16[4,16,2048]{2,1,0:T(8,128)(2,1)S(1)}, bf16[4,16,2048]{2,1,0:T(8,128)(2,1)S(1)}, u32[]{:S(2)}, u32[]{:S(2)}) collective-permute-start(bf16[4,16,2048]{2,1,0:T(8,128)(2,1)S(1)} %fusion.66), channel_id=1, source_target_pairs={{0,16},{8,24},{16,0},{24,8},{1,17},{9,25},{17,1},{25,9},{2,18},{10... | collective-permute-start | bytes 786440 | tf_op jit(solution)/shard_map/ppermute | solution.py:46
  90.5 43.1 %collective-permute-start.27 = (bf16[2,2,16,2048]{3,2,1,0:T(8,128)(2,1)S(1)}, bf16[2,2,16,2048]{3,2,1,0:T(8,128)(2,1)S(1)}, u32[]{:S(2)}, u32[]{:S(2)}) collective-permute-start(bf16[2,2,16,2048]{3,2,1,0:T(8,128)(2,1)S(1)} %fusion.86), channel_id=1, source_target_pairs={{0,1},{1,0},{2,3},{3,2},{4,5},{5,4},{6,7},{7,6},{8,9},{9,8},{10,11... | collective-permute-start | bytes 786440 | tf_op jit(solution)/shard_map/ppermute | solution.py:46
  93.7 6.7 %collective-permute-start.13 = (bf16[4,16,2048]{2,1,0:T(8,128)(2,1)S(1)}, bf16[4,16,2048]{2,1,0:T(8,128)(2,1)S(1)}, u32[]{:S(2)}, u32[]{:S(2)}) collective-permute-start(bf16[4,16,2048]{2,1,0:T(8,128)(2,1)S(1)} %add_convert_fusion.2), channel_id=1, source_target_pairs={{0,8},{8,0},{16,24},{24,16},{1,9},{9,1},{17,25},{25,17},{2,10},{10... | collective-permute-start | bytes 786440 | tf_op jit(solution)/shard_map/ppermute | solution.py:46
  98.8 1.9 %collective-permute-start.32 = (bf16[4,16,2048]{2,1,0:T(8,128)(2,1)S(1)}, bf16[4,16,2048]{2,1,0:T(8,128)(2,1)S(1)}, u32[]{:S(2)}, u32[]{:S(2)}) collective-permute-start(bf16[4,16,2048]{2,1,0:T(8,128)(2,1)S(1)} %add_convert_fusion), channel_id=1, source_target_pairs={{0,8},{8,0},{16,24},{24,16},{1,9},{9,1},{17,25},{25,17},{2,10},{10... | collective-permute-start | bytes 786440 | tf_op jit(solution)/shard_map/ppermute | solution.py:46
  98.9 43.2 %collective-permute-start.8 = (bf16[2,2,16,2048]{3,2,1,0:T(8,128)(2,1)S(1)}, bf16[2,2,16,2048]{3,2,1,0:T(8,128)(2,1)}, u32[]{:S(2)}, u32[]{:S(2)}) collective-permute-start(bf16[2,2,16,2048]{3,2,1,0:T(8,128)(2,1)S(1)} %fusion.81), channel_id=1, source_target_pairs={{0,1},{1,0},{2,3},{3,2},{4,5},{5,4},{6,7},{7,6},{8,9},{9,8},{10,11... | collective-permute-start | bytes 786440 | tf_op jit(solution)/shard_map/ppermute | solution.py:46
  104.7 14.1 %copy-start.1 = (pred[256,8,8,256]{3,1,2,0:T(8,128)(4,1)S(1)}, pred[256,8,8,256]{3,1,2,0:T(8,128)(4,1)}, u32[]{:S(2)}) copy-start(pred[256,8,8,256]{3,1,2,0:T(8,128)(4,1)} %copy.82) | copy-start | bytes 12582916
  104.7 3.7 %collective-permute-start.38 = (f32[2048]{0:T(1024)S(1)}, f32[2048]{0:T(1024)S(1)}, u32[]{:S(2)}, u32[]{:S(2)}) collective-permute-start(f32[2048]{0:T(1024)S(1)} %add.159), channel_id=1, source_target_pairs={{0,1},{1,0},{2,3},{3,2},{4,5},{5,4},{6,7},{7,6},{8,9},{9,8},{10,11... | collective-permute-start | bytes 24584 | tf_op jit(solution)/shard_map/ppermute | solution.py:46
  106.0 24.4 %collective-permute-start.33 = (bf16[2,2,16,2048]{3,2,1,0:T(8,128)(2,1)S(1)}, bf16[2,2,16,2048]{3,2,1,0:T(8,128)(2,1)}, u32[]{:S(2)}, u32[]{:S(2)}) collective-permute-start(bf16[2,2,16,2048]{3,2,1,0:T(8,128)(2,1)S(1)} %fusion.87), channel_id=1, source_target_pairs={{0,1},{1,0},{2,3},{3,2},{4,5},{5,4},{6,7},{7,6},{8,9},{9,8},{10,11... | collective-permute-start | bytes 786440 | tf_op jit(solution)/shard_map/ppermute | solution.py:46
  108.4 5.7 %collective-permute-start.39 = (f32[2048]{0:T(1024)S(1)}, f32[2048]{0:T(1024)S(1)}, u32[]{:S(2)}, u32[]{:S(2)}) collective-permute-start(f32[2048]{0:T(1024)S(1)} %add.160), channel_id=1, source_target_pairs={{0,2},{1,3},{2,0},{3,1},{4,6},{5,7},{6,4},{7,5},{8,10},{9,11},{10,... | collective-permute-start | bytes 24584 | tf_op jit(solution)/shard_map/ppermute | solution.py:46
  114.1 4.6 %collective-permute-start.40 = (f32[2048]{0:T(1024)S(1)}, f32[2048]{0:T(1024)S(1)}, u32[]{:S(2)}, u32[]{:S(2)}) collective-permute-start(f32[2048]{0:T(1024)S(1)} %add.161), channel_id=1, source_target_pairs={{0,4},{1,5},{2,6},{3,7},{4,0},{5,1},{6,2},{7,3},{8,12},{9,13},{10,... | collective-permute-start | bytes 24584 | tf_op jit(solution)/shard_map/ppermute | solution.py:46
  115.5 17.1 %collective-permute-start.14 = (bf16[2,2,16,2048]{3,2,1,0:T(8,128)(2,1)S(1)}, bf16[2,2,16,2048]{3,2,1,0:T(8,128)(2,1)S(1)}, u32[]{:S(2)}, u32[]{:S(2)}) collective-permute-start(bf16[2,2,16,2048]{3,2,1,0:T(8,128)(2,1)S(1)} %fusion.83), channel_id=1, source_target_pairs={{0,1},{1,0},{2,3},{3,2},{4,5},{5,4},{6,7},{7,6},{8,9},{9,8},{10,11... | collective-permute-start | bytes 786440 | tf_op jit(solution)/shard_map/ppermute | solution.py:46
  118.7 4.7 %collective-permute-start.41 = (f32[2048]{0:T(1024)S(1)}, f32[2048]{0:T(1024)S(1)}, u32[]{:S(2)}, u32[]{:S(2)}) collective-permute-start(f32[2048]{0:T(1024)S(1)} %add.162), channel_id=1, source_target_pairs={{0,8},{8,0},{16,24},{24,16},{1,9},{9,1},{17,25},{25,17},{2,10},{10... | collective-permute-start | bytes 24584 | tf_op jit(solution)/shard_map/ppermute | solution.py:46
  123.5 6.3 %collective-permute-start.42 = (f32[4096]{0:T(1024)S(1)}, f32[4096]{0:T(1024)S(1)}, u32[]{:S(2)}, u32[]{:S(2)}) collective-permute-start(f32[4096]{0:T(1024)S(1)} %maximum_select_fusion.7), channel_id=1, source_target_pairs={{0,16},{8,24},{16,0},{24,8},{1,17},{9,25},{17,1},{25,9},{2,18},{10... | collective-permute-start | bytes 49160 | tf_op jit(solution)/shard_map/ppermute | solution.py:46
  129.7 32.3 %copy-start.2 = (bf16[8,8192]{1,0:T(8,128)(2,1)S(1)}, bf16[8,8192]{1,0:T(8,128)(2,1)}, u32[]{:S(2)}) copy-start(bf16[8,8192]{1,0:T(8,128)(2,1)} %param.7) | copy-start | bytes 393220
  129.7 33.3 %copy-start.4 = (bf16[8,8192]{1,0:T(8,128)(2,1)S(1)}, bf16[8,8192]{1,0:T(8,128)(2,1)}, u32[]{:S(2)}) copy-start(bf16[8,8192]{1,0:T(8,128)(2,1)} %param.13) | copy-start | bytes 393220
  131.4 9.2 %collective-permute-start.34 = (bf16[2,2,16,2048]{3,2,1,0:T(8,128)(2,1)S(1)}, bf16[2,2,16,2048]{3,2,1,0:T(8,128)(2,1)S(1)}, u32[]{:S(2)}, u32[]{:S(2)}) collective-permute-start(bf16[2,2,16,2048]{3,2,1,0:T(8,128)(2,1)S(1)} %fusion.49), channel_id=1, source_target_pairs={{0,2},{1,3},{2,0},{3,1},{4,6},{5,7},{6,4},{7,5},{8,10},{9,11},{10,... | collective-permute-start | bytes 786440 | tf_op jit(solution)/shard_map/ppermute | solution.py:46
  132.6 15.3 %collective-permute-start.15 = (bf16[2,2,16,2048]{3,2,1,0:T(8,128)(2,1)S(1)}, bf16[2,2,16,2048]{3,2,1,0:T(8,128)(2,1)S(1)}, u32[]{:S(2)}, u32[]{:S(2)}) collective-permute-start(bf16[2,2,16,2048]{3,2,1,0:T(8,128)(2,1)S(1)} %fusion.55), channel_id=1, source_target_pairs={{0,2},{1,3},{2,0},{3,1},{4,6},{5,7},{6,4},{7,5},{8,10},{9,11},{10,... | collective-permute-start | bytes 786440 | tf_op jit(solution)/shard_map/ppermute | solution.py:46
  140.7 8.7 %collective-permute-start.35 = (bf16[1,2,16,2048]{3,2,1,0:T(8,128)(2,1)S(1)}, bf16[1,2,16,2048]{3,2,1,0:T(8,128)(2,1)S(1)}, u32[]{:S(2)}, u32[]{:S(2)}) collective-permute-start(bf16[1,2,16,2048]{3,2,1,0:T(8,128)(2,1)S(1)} %split.112), channel_id=1, source_target_pairs={{0,4},{1,5},{2,6},{3,7},{4,0},{5,1},{6,2},{7,3},{8,12},{9,13},{10,... | collective-permute-start | bytes 393224 | tf_op jit(solution)/shard_map/ppermute | solution.py:46
  149.0 7.9 %collective-permute-start.16 = (bf16[1,2,16,2048]{3,2,1,0:T(8,128)(2,1)S(1)}, bf16[1,2,16,2048]{3,2,1,0:T(8,128)(2,1)S(1)}, u32[]{:S(2)}, u32[]{:S(2)}) collective-permute-start(bf16[1,2,16,2048]{3,2,1,0:T(8,128)(2,1)S(1)} %split.113), channel_id=1, source_target_pairs={{0,4},{1,5},{2,6},{3,7},{4,0},{5,1},{6,2},{7,3},{8,12},{9,13},{10,... | collective-permute-start | bytes 393224 | tf_op jit(solution)/shard_map/ppermute | solution.py:46
  149.5 7.5 %collective-permute-start.36 = (bf16[16,2048]{1,0:T(8,128)(2,1)S(1)}, bf16[16,2048]{1,0:T(8,128)(2,1)S(1)}, u32[]{:S(2)}, u32[]{:S(2)}) collective-permute-start(bf16[16,2048]{1,0:T(8,128)(2,1)S(1)} %get-tuple-element.23), channel_id=1, source_target_pairs={{0,8},{8,0},{16,24},{24,16},{1,9},{9,1},{17,25},{25,17},{2,10},{10... | collective-permute-start | bytes 196616 | tf_op jit(solution)/shard_map/ppermute | solution.py:46
  156.9 1.3 collective-permute-start.17
  157.0 5.0 %collective-permute-start.37 = (bf16[8,4096]{1,0:T(8,128)(2,1)S(1)}, bf16[8,4096]{1,0:T(8,128)(2,1)S(1)}, u32[]{:S(2)}, u32[]{:S(2)}) collective-permute-start(bf16[8,4096]{1,0:T(8,128)(2,1)S(1)} %get-tuple-element.22), channel_id=1, source_target_pairs={{0,16},{8,24},{16,0},{24,8},{1,17},{9,25},{17,1},{25,9},{2,18},{10... | collective-permute-start | bytes 196616 | tf_op jit(solution)/shard_map/ppermute | solution.py:46
  158.3 4.7 %collective-permute-start.18 = (bf16[8,4096]{1,0:T(8,128)(2,1)S(1)}, bf16[8,4096]{1,0:T(8,128)(2,1)S(1)}, u32[]{:S(2)}, u32[]{:S(2)}) collective-permute-start(bf16[8,4096]{1,0:T(8,128)(2,1)S(1)} %get-tuple-element.31), channel_id=1, source_target_pairs={{0,16},{8,24},{16,0},{24,8},{1,17},{9,25},{17,1},{25,9},{2,18},{10... | collective-permute-start | bytes 196616 | tf_op jit(solution)/shard_map/ppermute | solution.py:46
  (6 other events, 46.4 us)

commit v2 on v1

v2 whole, which is shorter than its diff:
```python
import functools

import jax
import jax.numpy as jnp
from jax import lax
from jax.experimental import pallas as pl
from jax.experimental.pallas import tpu as pltpu
from jax.sharding import PartitionSpec as P

BLOCK = 256
PANEL = 1024
BF16 = jnp.bfloat16
F32 = jnp.float32
VMEM = pl.BlockSpec(memory_space=pltpu.VMEM)
SMEM = pl.BlockSpec(memory_space=pltpu.SMEM)
NO_COST = pl.CostEstimate(flops=0, bytes_accessed=0, transcendentals=0)


def kept_tiles(pattern, first_row, rows, first_column, columns):
    own = lax.dynamic_slice_in_dim(pattern, first_column, columns, 0)
    iota = first_row + jnp.arange(rows, dtype=jnp.int32)
    return jnp.any(own[None, :, :] == iota[:, None, None], axis=2).astype(jnp.int32)


def masked(keep_tile, value):
    return jnp.where(keep_tile == 1, value, jnp.zeros_like(value))


def keep_kernel(mask_ref, weight_ref, out_ref, copied):
    rows, columns = mask_ref.shape

    def each(kept, other):
        @pl.loop(0, rows)
        def _(i):
            for j in range(columns):
                here = (pl.ds(pl.multiple_of(i * BLOCK, BLOCK), BLOCK), pl.ds(j * BLOCK, BLOCK))

                @pl.when(mask_ref[i, j] == 1)
                def _():
                    kept(pltpu.make_async_copy(weight_ref.at[here], out_ref.at[here], copied.at[i, j]))

                if other is not None:

                    @pl.when(mask_ref[i, j] != 1)
                    def _():
                        other(here)

    def clear(here):
        out_ref[here] = jnp.zeros((BLOCK, BLOCK), out_ref.dtype)

    each(lambda copy: copy.start(), clear)
    each(lambda copy: copy.wait(), None)


def keep(weight, mask):
    return pl.pallas_call(
        keep_kernel,
        out_shape=pltpu.VMEM(weight.shape, weight.dtype),
        in_specs=[SMEM, pl.BlockSpec(memory_space=pltpu.HBM)],
        out_specs=VMEM,
        scratch_shapes=[pltpu.SemaphoreType.DMA(mask.shape)],
        compiler_params=pltpu.CompilerParams(vmem_limit_bytes=2 << 20),
        cost_estimate=NO_COST,
    )(mask, pltpu.with_memory_space_constraint(weight, pltpu.HBM))


def product_kernel(left_ref, weight_ref, out_ref):
    width = weight_ref.shape[1]
    panel = min(PANEL, width)

    @pl.loop(0, width // panel)
    def _(k):
        here = pl.ds(pl.multiple_of(k * panel, panel), panel)
        out_ref[:, here] = jnp.dot(
            left_ref[...], weight_ref[:, here], preferred_element_type=F32
        )


def product(left, weight):
    return pl.pallas_call(
        product_kernel,
        out_shape=jax.ShapeDtypeStruct((left.shape[0], weight.shape[1]), F32),
        in_specs=[VMEM, VMEM],
        out_specs=VMEM,
        compiler_params=pltpu.CompilerParams(vmem_limit_bytes=6 << 20),
        cost_estimate=NO_COST,
    )(left, pltpu.with_memory_space_constraint(weight, pltpu.VMEM))


def outer_kernel(mask_ref, left_ref, right_ref, out_ref):
    i = pl.program_id(0)
    tiles = out_ref.shape[0] // BLOCK
    turned = left_ref[...].T
    for j in range(out_ref.shape[1] // BLOCK):
        here = slice(j * BLOCK, (j + 1) * BLOCK)
        full = jnp.dot(turned, right_ref[:, here], preferred_element_type=F32)
        for t in range(tiles):
            rows = slice(t * BLOCK, (t + 1) * BLOCK)
            out_ref[rows, here] = masked(mask_ref[i * tiles + t, j], full[rows]).astype(
                out_ref.dtype
            )


def outer(left, right, mask):
    tokens, rows = left.shape
    columns = right.shape[1]
    step = 2 * BLOCK
    return pl.pallas_call(
        outer_kernel,
        grid=(rows // step,),
        out_shape=jax.ShapeDtypeStruct((rows, columns), BF16),
        in_specs=[
            SMEM,
            pl.BlockSpec((tokens, step), lambda i: (0, i)),
            pl.BlockSpec((tokens, columns), lambda i: (0, 0)),
        ],
        out_specs=pl.BlockSpec((step, columns), lambda i: (i, 0)),
        compiler_params=pltpu.CompilerParams(vmem_limit_bytes=12 << 20),
        cost_estimate=NO_COST,
    )(mask, left, right)


def normalise_kernel(
    far_ref, input_hbm, gain_hbm, kept_ref, given_ref, standard_ref, deviation_ref, input_ref, gain_ref, copied
):
    copies = [
        pltpu.make_async_copy(input_hbm, input_ref, copied.at[0]),
        pltpu.make_async_copy(gain_hbm, gain_ref, copied.at[1]),
    ]
    for copy in copies:
        copy.start()
    for copy in copies:
        copy.wait()
    xfloat = input_ref[...].astype(F32)
    centered = xfloat - jnp.mean(xfloat, axis=1, keepdims=True)
    deviation = lax.rsqrt(jnp.mean(centered * centered, axis=1, keepdims=True) + 1e-05)
    standard = centered * deviation
    normed = standard * gain_ref[...]
    half = normed.shape[1] // 2
    low, high = normed[:, :half], normed[:, half:]
    far = far_ref[0] == 1
    kept_ref[...] = jnp.where(far, high, low).astype(BF16)
    given_ref[...] = jnp.where(far, low, high).astype(BF16)
    standard_ref[...] = standard
    deviation_ref[...] = deviation


def normalise(inputs, gain, far):
    tok, width = inputs.shape
    half = jax.ShapeDtypeStruct((tok, width // 2), BF16)
    return pl.pallas_call(
        normalise_kernel,
        out_shape=(
            half,
            half,
            jax.ShapeDtypeStruct((tok, width), F32),
            jax.ShapeDtypeStruct((tok, 1), F32),
        ),
        in_specs=[SMEM] + [pl.BlockSpec(memory_space=pltpu.HBM)] * 2,
        out_specs=(VMEM,) * 4,
        scratch_shapes=[
            pltpu.VMEM(inputs.shape, inputs.dtype),
            pltpu.VMEM(gain.shape, gain.dtype),
            pltpu.SemaphoreType.DMA((2,)),
        ],
        compiler_params=pltpu.CompilerParams(vmem_limit_bytes=6 << 20),
        cost_estimate=NO_COST,
    )(far, *(pltpu.with_memory_space_constraint(v, pltpu.HBM) for v in (inputs, gain)))


def turn_kernel(weight_ref, out_ref):
    columns = weight_ref.shape[1]

    @pl.loop(0, columns // BLOCK)
    def _(k):
        here = pl.ds(pl.multiple_of(k * BLOCK, BLOCK), BLOCK)
        out_ref[here, :] = weight_ref[:, here].T


def turn(weight):
    return pl.pallas_call(
        turn_kernel,
        out_shape=pltpu.VMEM(weight.shape[::-1], weight.dtype),
        in_specs=[VMEM],
        out_specs=VMEM,
        compiler_params=pltpu.CompilerParams(vmem_limit_bytes=6 << 20),
        cost_estimate=NO_COST,
    )(pltpu.with_memory_space_constraint(weight, pltpu.VMEM))


def gelu_and_slope(h):
    tanh_v = jnp.tanh(0.7978845608 * (h + 0.044715 * h * h * h))
    value = 0.5 * h * (1.0 + tanh_v)
    slope = 0.5 * (1.0 + tanh_v) + 0.5 * h * (1.0 - tanh_v * tanh_v) * 0.7978845608 * (
        1.0 + 0.134145 * h * h
    )
    return value, slope


def swap(value, axis, distance):
    size = lax.axis_size(axis)
    return lax.ppermute(value, axis, [(i, i ^ distance) for i in range(size)])


def halves(value, bit, axis):
    low, high = jnp.split(value, 2, axis=axis)
    return jnp.where(bit, high, low), jnp.where(bit, low, high)


def ordered(mine, other, bit, axis):
    return jnp.where(
        bit,
        jnp.concatenate([other, mine], axis=axis),
        jnp.concatenate([mine, other], axis=axis),
    )


class Plan:
    def __init__(self, staged):
        self.staged = staged
        self.tasks = []

    def work(self, stage, function, *deps):
        self.tasks.append((stage if self.staged else 0, function, deps))
        return len(self.tasks) - 1

    def swap(self, stage, axis, distance, dep):
        return self.work(stage, functools.partial(swap, axis=axis, distance=distance), dep)

    def run(self, results):
        values = {}
        for stage in sorted({t[0] for t in self.tasks}):
            for task, (when, function, deps) in enumerate(self.tasks):
                if when == stage:
                    values[task] = function(*(values[d] for d in deps))
            wanted = {d for when, _, deps in self.tasks if when > stage for d in deps}
            live = sorted((wanted | set(results)) & set(values))
            values.update(zip(live, lax.optimization_barrier(tuple(values[n] for n in live))))
        return tuple(values[n] for n in results)


def second(pair):
    return pair[1]


def to_bf16(value):
    return value.astype(BF16)


def shards(inputs, layer_norm_gain, w_in, w_out, pattern_in, pattern_out, out_grad):
    n_col = lax.axis_size("col")
    row_index = lax.axis_index("row")
    col_index = lax.axis_index("col")
    core_bit = row_index % 2 == 1
    far_bit = row_index // 2 == 1
    tok = inputs.shape[0]
    feat, unit = w_in.shape
    feat_tiles, unit_tiles = feat // BLOCK, unit // BLOCK
    line = [1 << b for b in reversed(range(1, n_col.bit_length() - 1))]
    last = len(line)
    places = [2] + [1 << i for i in range(1, last)]

    plan = Plan(last == 2)
    work, swapped = plan.work, plan.swap

    def to_core(v, got):
        return halves(ordered(v[0], got, far_bit, 0), core_bit, 1)

    g0 = work(0, lambda: halves(out_grad, far_bit, 1))
    gfar = swapped(0, "row", 2, work(0, second, g0))
    x0 = work(
        0,
        lambda: normalise(inputs, layer_norm_gain[None, :], far_bit.astype(jnp.int32)[None]),
    )
    xfar = swapped(0, "row", 2, work(0, second, x0))
    x1, g1 = work(0, to_core, x0, xfar), work(0, to_core, g0, gfar)
    core = swapped(0, "row", 1, work(0, lambda x, g: jnp.stack([x[1], g[1]]), x1, g1))
    xown = work(0, lambda v, got: jnp.stack([v[0], got[0]])[None], x1, core)
    gown = work(0, lambda v, got: jnp.stack([v[0], got[1]])[None], g1, core)

    mask_in = work(1, lambda: kept_tiles(
        pattern_in, row_index * feat_tiles, feat_tiles, col_index * unit_tiles, unit_tiles
    ))
    mask_out = work(1, lambda: kept_tiles(
        pattern_out, col_index * unit_tiles, unit_tiles, row_index * feat_tiles, feat_tiles
    ))
    in_e = work(1, lambda mask: keep(w_in, mask), mask_in)
    out_e = work(2, lambda mask: keep(w_out, mask), mask_out)

    def give_half(*parts):
        return jnp.concatenate([v[v.shape[0] // 2 :] for v in parts]).astype(BF16)

    def add_half(*parts):
        kept = jnp.concatenate([v[: v.shape[0] // 2] for v in parts[:-1]])
        return kept + parts[-1].astype(F32)

    def row_sum(stages, parts, sizes):
        first, core_stage, back, unpack = stages
        got = swapped(core_stage, "row", 1, work(first, give_half, *parts))
        pair = work(core_stage, add_half, *parts, got)
        rounded = work(core_stage, to_bf16, pair)
        far = swapped(core_stage, "row", 2, rounded)
        total = work(back, lambda v, got: (v + got.astype(F32)).astype(BF16), pair, far)
        other = swapped(back, "row", 1, total)
        sums, start = [], 0
        for size in sizes:
            rows = slice(start, start + size)
            start = rows.stop
            sums.append(work(
                unpack,
                lambda v, got, rows=rows: jnp.concatenate([v[rows], got[rows]]).astype(F32),
                total,
                other,
            ))
        return sums, rounded

    def chunk(*parts):
        return jnp.concatenate(parts).swapaxes(0, 1).reshape(-1, feat)

    def join(*parts):
        return jnp.concatenate(parts)

    def behind(value, *others):
        return lax.optimization_barrier((value,) + others)[0]

    near = swapped(1, "col", 1, work(1, join, xown, gown))
    xline, gline = [swapped(1, "col", line[0], xown)], []
    xnear, gnear = [swapped(2, "col", 1, xline[0])], []
    xheld, gheld = [xown, xline[0]], [gown]
    xfirst, gfirst = work(2, lambda v: v[:1], near), work(2, lambda v: v[1:], near)
    for i in range(1, last):
        xline.append(swapped(1 + i, "col", line[i], work(1 + i, join, *xheld)))
        xheld.append(xline[i])
    gline.append(swapped(2, "col", line[0], gown))
    gheld.append(gline[0])
    sizes = [n * 4 * tok for n in places]
    xc = [work(2, chunk, xown, xfirst, xline[0], xnear[0])]
    xp = [work(2, product, xc[0], in_e)]
    (total,), rounded = row_sum((2, 3, 4, 4), xp, sizes[:1])
    pre = [total]
    for i in range(1, last):
        gnear.append(swapped(2 + i, "col", 1, gline[i - 1]))
        xnear.append(swapped(2 + i, "col", 1, xline[i]))
        held = work(2 + i, join, *gheld)
        gline.append(swapped(2 + i, "col", line[i], work(2 + i, behind, held, rounded)))
        gheld.append(gline[i])
    out_t = work(3, turn, out_e)
    gc = [work(3, chunk, gown, gfirst, gline[0], gnear[0])]
    gp = [work(3, product, gc[0], out_t)]
    gnear.append(swapped(4, "col", 1, gline[-1]))
    d_act = []
    for i in range(1, last):
        xc.append(work(4, chunk, xline[i], xnear[i]))
        xp.append(work(4, product, xc[i], in_e))
        sums, rounded = row_sum(
            (4, 4, 5, 5), [xp[i], gp[i - 1]], [sizes[i], sizes[i - 1]]
        )
        pre.append(sums[0])
        d_act.append(sums[1])
        late = work(4, behind, gline[i], rounded)
        gc.append(work(4, chunk, late, gnear[i]))
        gp.append(work(4, product, gc[i], out_t))
    in_t = work(4, turn, in_e)
    d_act.append(row_sum((4, 5, 6, 6), gp[-1:], sizes[-1:])[0][0])

    def forward(pre):
        value, slope = gelu_and_slope(pre)
        return value.astype(BF16), slope

    def places_first(value):
        return value.reshape(2, -1, 2 * tok, value.shape[-1]).swapaxes(0, 1)

    def give_near(i, v):
        v = places_first(v)
        return (v[v.shape[0] // 2 :] if i else v[1::2]).astype(BF16)

    def keep_near(i, v, got):
        v = places_first(v)
        return (v[: v.shape[0] // 2] if i else v[::2]) + got.astype(F32)

    made = [work(4 + i, forward, pre[i]) for i in range(last)]
    act = [work(4 + i, lambda v: v[0], made[i]) for i in range(last)]
    yp = [work(4 + i, product, act[i], out_e) for i in range(last)]
    ygive = [work(4 + i, functools.partial(give_near, i), yp[i]) for i in range(last)]
    ynear = [swapped(4 + i, "col", 1, ygive[i]) for i in range(last)]
    d_pre = [
        work(5 + i, lambda v, made: (v * made[1]).astype(BF16), d_act[i], made[i])
        for i in range(last)
    ]
    np_ = [work(5 + i, product, d_pre[i], in_t) for i in range(last)]
    last_give = work(4 + last, functools.partial(give_near, last - 1), np_[-1])

    def add(v, got):
        return v + got

    def gain_terms(*parts):
        left, right = parts[:last], parts[last:]
        return sum(jnp.sum(n * x.astype(F32), axis=0) for n, x in zip(left, right))

    gain = work(6, gain_terms, *np_, *xc)
    for b, distance in enumerate([1] + line[::-1]):
        gain = work(min(7 + b, 9), add, gain, swapped(min(6 + b, 8), "col", distance, gain))

    nnear = [
        swapped(7, "col", 1, work(7, functools.partial(give_near, i), np_[i]))
        for i in range(last - 1)
    ] + [swapped(4 + last, "col", 1, last_give)]

    def line_sum(stage, products, got, late):
        sums = [
            work(
                stage if i or not late else stage + last - 1,
                functools.partial(keep_near, i),
                products[i],
                got[i],
            )
            for i in range(last)
        ]
        for i in reversed(range(1, last)):
            when = stage + last - 1 - i
            moved = swapped(when, "col", line[i], work(when, to_bf16, sums[i]))
            for m in range(i):
                first = sum(places[:m])
                sums[m] = work(
                    when + 1,
                    lambda v, got, first=first: v + got[first : first + v.shape[0]].astype(F32),
                    sums[m],
                    moved,
                )
        give = work(stage + last - 1, lambda v: v[1].astype(BF16), sums[0])
        moved = swapped(stage + last - 1, "col", line[0], give)
        return give, work(
            stage + last, lambda v, got: (v[0] + got.astype(F32)).astype(BF16), sums[0], moved
        )

    def to_far(v, got):
        return halves(ordered(v[0], got, core_bit, 1), far_bit, 0)

    _, y = line_sum(6, yp, ynear, False)
    last_sent, n = line_sum(7, np_, nnear, True)
    y1 = work(8, to_far, y, swapped(8, "row", 1, work(8, second, y)))
    n1 = work(9, to_far, n, swapped(9, "row", 1, work(9, second, n)))
    yfar = swapped(9, "row", 2, work(9, second, y1))
    nfar = swapped(9, "row", 2, work(9, second, n1))
    output = work(9, lambda v, got: (
        inputs.astype(F32) + ordered(v[0], got, far_bit, 1).astype(F32)
    ).astype(BF16), y1, yfar)

    got = swapped(9, "row", 1, gain)
    gain = work(9, lambda v, got: ordered(v, got, core_bit, 0), gain, got)
    gain = work(9, lambda v, other: behind(v, other[0]), gain, n1)
    got = swapped(9, "row", 2, gain)
    gain_gradient = work(
        9, lambda v, got: ordered(v, got, far_bit, 0) / layer_norm_gain, gain, got
    )

    def input_gradient(v, got, made):
        standard, deviation = made[2:]
        scaled = ordered(v[0], got, far_bit, 1).astype(F32) * layer_norm_gain[None, :]
        result = deviation * (
            scaled
            - jnp.mean(scaled, axis=1, keepdims=True)
            - standard * jnp.mean(scaled * standard, axis=1, keepdims=True)
        )
        return (out_grad.astype(F32) + result).astype(BF16)

    grad_inputs = work(9, input_gradient, n1, nfar, x0)

    def weight_gradient(mask, before, *parts):
        left, right = parts[:last], parts[last:]
        return outer(jnp.concatenate(left), jnp.concatenate(right), behind(mask, before))

    grad_w_out = work(4 + last, weight_gradient, mask_out, last_give, *act, *gc)
    grad_w_in = work(8, weight_gradient, mask_in, last_sent, *xc, *d_pre)

    return plan.run((output, grad_inputs, grad_w_in, grad_w_out, gain_gradient))


def solution(mesh):
    in_specs = (
        P(("row", "col"), None),
        P(),
        P("row", "col"),
        P("col", "row"),
        P(),
        P(),
        P(("row", "col"), None),
    )
    out_specs = (
        P(("row", "col"), None),
        P(("row", "col"), None),
        P("row", "col"),
        P("col", "row"),
        P(),
    )
    return jax.shard_map(shards, mesh=mesh, in_specs=in_specs, out_specs=out_specs, check_vma=False)
```

time: 164 us -> 122 us (0.74)
  Pallas kernels: 0 us -> 37.4 us
  matrix products: 31.2 us -> 0 us
  other arithmetic: 29.9 us -> 7.96 us
  waiting for transfers between devices: 50.3 us -> 31.8 us
  local copies, waits for them, and re-layouts: 11.6 us -> 1.94 us
  starting transfers between devices: 39.4 us -> 41.6 us
    pallas_call x0 -> x15, Pallas kernels: none -> 37.4 us  [the longest x8 11.8 us: product(): pl.pallas_call(product_kernel, out_shape=jax.ShapeDtypeStruct((left.shape...]
    dot_general x10 -> x0, matrix products: 31.2 us -> none  [the longest x4 11.8 us: dot_last(): lax.dot_general(left, right, (((1,), (1,)), ((), ())), preferred_element_...]
    ppermute x43 -> x38, waiting for transfers between devices: 50.3 us -> 31.8 us  [swap(): return lax.ppermute(value, axis, [(i, i ^ distance) for i in range(size)])]
    select_n x2 -> x0, other arithmetic: 17.7 us -> none  [apply_mask(): jnp.where(mask[:, None, :, None], shaped, jnp.zeros((), weight.dtype))]
    unnamed x24 -> x12, local copies, waits for them, and re-layouts: 8.37 us -> 0.04 us
    convert_element_type x20 -> x16, other arithmetic: 5.47 us -> 2.47 us  [the longest x1 0.79 us: input_gradient(): return (out_grad.astype(F32) + result).astype(BF16)]
    broadcast_in_dim x2 -> x0, local copies, waits for them, and re-layouts: 2.3 us -> none  [apply_mask(): jnp.where(mask[:, None, :, None], shaped, jnp.zeros((), weight.dtype))]
    ppermute x43 -> x38, starting transfers between devices: 39.4 us -> 41.6 us  [swap(): return lax.ppermute(value, axis, [(i, i ^ distance) for i in range(size)])]
  transfers between devices with their start and end apart: 43 -> 38, of which waited for: 16 -> 19; matrix products, arithmetic and copies ran while one was open for 42% -> 6% of each run, Pallas kernels for 0% -> 29%
where the time goes in v2:
time: 122 us
  starting transfers between devices  41.6 us (34%)
  Pallas kernels  37.4 us (31%)
  waiting for transfers between devices  31.8 us (26%)
  other arithmetic  7.96 us (7%)
  local copies, waits for them, and re-layouts  1.94 us (2%)
  between operations  1.48 us (1%)
    ppermute x38, starting transfers between devices, swap(): return lax.ppermute(value, axis, [(i, i ^ distance) for i in range(size)])  41.6 us
    ppermute x38, waiting for transfers between devices, swap(): return lax.ppermute(value, axis, [(i, i ^ distance) for i in range(size)])  31.8 us
    pallas_call x8, Pallas kernels, product(): pl.pallas_call(product_kernel, out_shape=jax.ShapeDtypeStruct((left.shape...  11.8 us
    pallas_call x2, Pallas kernels, outer(): pl.pallas_call(outer_kernel, grid=(rows // step,), out_shape=jax.ShapeDty...  11.4 us
    pallas_call x2, Pallas kernels, keep(): pl.pallas_call(keep_kernel, out_shape=pltpu.VMEM(weight.shape, weight.dty...  7.4 us
    pallas_call x2, Pallas kernels, turn(): pl.pallas_call(turn_kernel, out_shape=pltpu.VMEM(weight.shape[::-1], weig...  5.54 us
  transfers between devices with their start and end apart: 38, of which 19 were waited for; matrix products, arithmetic and copies ran while one was open for 6% of the time, Pallas kernels for 29%

profile of v2, /device:TPU:0, one launch (start us, length us, event | category | flops | bytes accessed | tf_op | source)
XLA Modules:
  0.0 122.2 jit_solution(1626983498126364507)
XLA Ops:
  0.7 0.9 broadcast_select_fusion.5
  1.6 3.0 %collective-permute-start.1 = (bf16[8,4096]{1,0:T(8,128)(2,1)S(1)}, bf16[8,4096]{1,0:T(8,128)(2,1)S(1)}, u32[]{:S(2)}, u32[]{:S(2)}) collective-permute-start(bf16[8,4096]{1,0:T(8,128)(2,1)S(1)} %get-tuple-element.305), channel_id=1, source_target_pairs={{0,16},{8,24},{16,0},{24,8},{1,17},{9,25},{17,1},{25,9},{2,18},{10... | collective-permute-start | bytes 196616 | tf_op jit(solution)/shard_map/ppermute | solution.py:202
  4.6 1.3 %shard_map.110 = (bf16[8,4096]{1,0:T(8,128)(2,1)S(1)}, bf16[8,4096]{1,0:T(8,128)(2,1)S(1)}, f32[8,8192]{1,0:T(8,128)S(1)}, f32[8,1]{1,0:T(8,128)S(1)}) custom-call(s32[1]{0:T(128)} %bitcast.far_ref, bf16[8,8192]{1,0:T(8,128)(2,1)} %input_hbm.1, f32[1,8192]{1,0:T(1,128)} %bitcast.104), custom_call_target="tpu_custom_call" | custom-call | tf_op jit(solution)/shard_map/pallas_call | solution.py:151
  6.9 3.3 %collective-permute-done = bf16[8,4096]{1,0:T(8,128)(2,1)S(1)} collective-permute-done((bf16[8,4096]{1,0:T(8,128)(2,1)S(1)}, bf16[8,4096]{1,0:T(8,128)(2,1)S(1)}, u32[]{:S(2)}, u32[]{:S(2)}) %collective-permute-start) | collective-permute-done | bytes 65568 | tf_op jit(solution)/shard_map/ppermute | solution.py:202
  10.7 1.0 collective-permute-done.2
  11.8 1.6 %collective-permute-start.3 = (bf16[2,2,16,2048]{3,2,1,0:T(8,128)(2,1)S(1)}, bf16[2,2,16,2048]{3,2,1,0:T(8,128)(2,1)S(1)}, u32[]{:S(2)}, u32[]{:S(2)}) collective-permute-start(bf16[2,2,16,2048]{3,2,1,0:T(8,128)(2,1)S(1)} %pad_maximum_fusion.7), channel_id=1, source_target_pairs={{0,1},{1,0},{2,3},{3,2},{4,5},{5,4},{6,7},{7,6},{8,9},{9,8},{10,11... | collective-permute-start | bytes 786440 | tf_op jit(solution)/shard_map/ppermute | solution.py:202
  13.3 2.6 %collective-permute-start.4 = (bf16[1,2,16,2048]{3,2,1,0:T(8,128)(2,1)S(1)}, bf16[1,2,16,2048]{3,2,1,0:T(8,128)(2,1)S(1)}, u32[]{:S(2)}, u32[]{:S(2)}) collective-permute-start(bf16[1,2,16,2048]{3,2,1,0:T(8,128)(2,1)S(1)} %get-tuple-element.153), channel_id=1, source_target_pairs={{0,4},{1,5},{2,6},{3,7},{4,0},{5,1},{6,2},{7,3},{8,12},{9,13},{10,... | collective-permute-start | bytes 393224 | tf_op jit(solution)/shard_map/ppermute | solution.py:202
  16.2 3.7 %shard_map.111.weight_ref = bf16[2048,2048]{1,0:T(8,128)(2,1)S(1)} custom-call(s32[8,8]{1,0:T(8,128)S(1)} %convert_element_type.143.mask_ref, bf16[2048,2048]{1,0:T(8,128)(2,1)} %weight_ref.2), custom_call_target="tpu_custom_call" | custom-call | tf_op jit(solution)/shard_map/pallas_call | solution.py:56
  20.0 2.3 %collective-permute-done.4 = bf16[1,2,16,2048]{3,2,1,0:T(8,128)(2,1)S(1)} collective-permute-done((bf16[1,2,16,2048]{3,2,1,0:T(8,128)(2,1)S(1)}, bf16[1,2,16,2048]{3,2,1,0:T(8,128)(2,1)S(1)}, u32[]{:S(2)}, u32[]{:S(2)}) %collective-permute-start.4) | collective-permute-done | bytes 131104 | tf_op jit(solution)/shard_map/ppermute | solution.py:202
  23.6 3.4 %collective-permute-start.6 = (bf16[1,2,16,2048]{3,2,1,0:T(8,128)(2,1)S(1)}, bf16[1,2,16,2048]{3,2,1,0:T(8,128)(2,1)S(1)}, u32[]{:S(2)}, u32[]{:S(2)}) collective-permute-start(bf16[1,2,16,2048]{3,2,1,0:T(8,128)(2,1)S(1)} %get-tuple-element.165), channel_id=1, source_target_pairs={{0,4},{1,5},{2,6},{3,7},{4,0},{5,1},{6,2},{7,3},{8,12},{9,13},{10,... | collective-permute-start | bytes 393224 | tf_op jit(solution)/shard_map/ppermute | solution.py:202
  27.1 3.7 %shard_map.112.weight_ref = bf16[2048,2048]{1,0:T(8,128)(2,1)S(1)} custom-call(s32[8,8]{1,0:T(8,128)S(1)} %convert_element_type.144.mask_ref, bf16[2048,2048]{1,0:T(8,128)(2,1)} %weight_ref.3), custom_call_target="tpu_custom_call" | custom-call | tf_op jit(solution)/shard_map/pallas_call | solution.py:56
  30.9 1.5 %shard_map.113 = f32[128,2048]{1,0:T(8,128)S(1)} custom-call(bf16[128,2048]{1,0:T(8,128)(2,1)S(1)} %bitcast.82, bf16[2048,2048]{1,0:T(8,128)(2,1)S(1)} %shard_map.111.weight_ref), custom_call_target="tpu_custom_call" | custom-call | tf_op jit(solution)/shard_map/pallas_call | solution.py:80
  32.7 1.5 %collective-permute-start.10 = (bf16[2,2,16,2048]{3,2,1,0:T(8,128)(2,1)S(1)}, bf16[2,2,16,2048]{3,2,1,0:T(8,128)(2,1)S(1)}, u32[]{:S(2)}, u32[]{:S(2)}) collective-permute-start(bf16[2,2,16,2048]{3,2,1,0:T(8,128)(2,1)S(1)} %collective-permute-done.5), channel_id=1, source_target_pairs={{0,1},{1,0},{2,3},{3,2},{4,5},{5,4},{6,7},{7,6},{8,9},{9,8},{10,11... | collective-permute-start | bytes 786440 | tf_op jit(solution)/shard_map/ppermute | solution.py:202
  34.8 0.8 collective-permute-start.9
  35.7 3.1 %collective-permute-start.11 = (bf16[2,2,16,2048]{3,2,1,0:T(8,128)(2,1)S(1)}, bf16[2,2,16,2048]{3,2,1,0:T(8,128)(2,1)S(1)}, u32[]{:S(2)}, u32[]{:S(2)}) collective-permute-start(bf16[2,2,16,2048]{3,2,1,0:T(8,128)(2,1)S(1)} %pad_maximum_fusion.9), channel_id=1, source_target_pairs={{0,2},{1,3},{2,0},{3,1},{4,6},{5,7},{6,4},{7,5},{8,10},{9,11},{10,... | collective-permute-start | bytes 786440 | tf_op jit(solution)/shard_map/ppermute | solution.py:202
  38.7 2.8 %shard_map.114.weight_ref = bf16[2048,2048]{1,0:T(8,128)(2,1)S(1)} custom-call(bf16[2048,2048]{1,0:T(8,128)(2,1)S(1)} %shard_map.112.weight_ref), custom_call_target="tpu_custom_call" | custom-call | tf_op jit(solution)/shard_map/pallas_call | solution.py:181
  41.5 2.7 %collective-permute-done.12 = bf16[1,2,16,2048]{3,2,1,0:T(8,128)(2,1)S(1)} collective-permute-done((bf16[1,2,16,2048]{3,2,1,0:T(8,128)(2,1)S(1)}, bf16[1,2,16,2048]{3,2,1,0:T(8,128)(2,1)S(1)}, u32[]{:S(2)}, u32[]{:S(2)}) %collective-permute-start.12) | collective-permute-done | bytes 131104 | tf_op jit(solution)/shard_map/ppermute | solution.py:202
  44.4 1.5 %shard_map.115 = f32[128,2048]{1,0:T(8,128)S(1)} custom-call(bf16[128,2048]{1,0:T(8,128)(2,1)S(1)} %bitcast.88, bf16[2048,2048]{1,0:T(8,128)(2,1)S(1)} %shard_map.114.weight_ref), custom_call_target="tpu_custom_call" | custom-call | tf_op jit(solution)/shard_map/pallas_call | solution.py:80
  46.0 1.5 %shard_map.116 = f32[128,2048]{1,0:T(8,128)S(1)} custom-call(bf16[128,2048]{1,0:T(8,128)(2,1)S(1)} %bitcast.85, bf16[2048,2048]{1,0:T(8,128)(2,1)S(1)} %shard_map.111.weight_ref), custom_call_target="tpu_custom_call" | custom-call | tf_op jit(solution)/shard_map/pallas_call | solution.py:80
  47.7 1.6 %collective-permute-start.15 = (bf16[2,2,16,2048]{3,2,1,0:T(8,128)(2,1)S(1)}, bf16[2,2,16,2048]{3,2,1,0:T(8,128)(2,1)S(1)}, u32[]{:S(2)}, u32[]{:S(2)}) collective-permute-start(bf16[2,2,16,2048]{3,2,1,0:T(8,128)(2,1)S(1)} %collective-permute-done.11), channel_id=1, source_target_pairs={{0,1},{1,0},{2,3},{3,2},{4,5},{5,4},{6,7},{7,6},{8,9},{9,8},{10,11... | collective-permute-start | bytes 786440 | tf_op jit(solution)/shard_map/ppermute | solution.py:202
  51.7 1.5 %shard_map.119 = f32[128,2048]{1,0:T(8,128)S(1)} custom-call(bf16[128,2048]{1,0:T(8,128)(2,1)S(1)} %get-tuple-element.220.left_ref, bf16[2048,2048]{1,0:T(8,128)(2,1)S(1)} %shard_map.112.weight_ref), custom_call_target="tpu_custom_call" | custom-call | tf_op jit(solution)/shard_map/pallas_call | solution.py:80
  53.3 0.9 collective-permute-start.17
  54.2 2.8 %shard_map.118.weight_ref = bf16[2048,2048]{1,0:T(8,128)(2,1)S(1)} custom-call(bf16[2048,2048]{1,0:T(8,128)(2,1)S(1)} %shard_map.111.weight_ref), custom_call_target="tpu_custom_call" | custom-call | tf_op jit(solution)/shard_map/pallas_call | solution.py:181
  57.1 1.5 %shard_map.117 = f32[128,2048]{1,0:T(8,128)S(1)} custom-call(bf16[128,2048]{1,0:T(8,128)(2,1)S(1)} %bitcast.90, bf16[2048,2048]{1,0:T(8,128)(2,1)S(1)} %shard_map.114.weight_ref), custom_call_target="tpu_custom_call" | custom-call | tf_op jit(solution)/shard_map/pallas_call | solution.py:80
  58.7 3.5 %collective-permute-done.17 = bf16[2,2,16,2048]{3,2,1,0:T(8,128)(2,1)S(1)} collective-permute-done((bf16[2,2,16,2048]{3,2,1,0:T(8,128)(2,1)S(1)}, bf16[2,2,16,2048]{3,2,1,0:T(8,128)(2,1)S(1)}, u32[]{:S(2)}, u32[]{:S(2)}) %collective-permute-start.17) | collective-permute-done | bytes 262176 | tf_op jit(solution)/shard_map/ppermute | solution.py:202
  62.1 1.9 %collective-permute-done.14 = bf16[128,2048]{1,0:T(8,128)(2,1)S(1)} collective-permute-done((bf16[128,2048]{1,0:T(8,128)(2,1)S(1)}, bf16[128,2048]{1,0:T(8,128)(2,1)S(1)}, u32[]{:S(2)}, u32[]{:S(2)}) %collective-permute-start.14) | collective-permute-done | bytes 524320 | tf_op jit(solution)/shard_map/ppermute | solution.py:202
  67.1 1.4 %shard_map.120 = f32[128,2048]{1,0:T(8,128)S(1)} custom-call(bf16[128,2048]{1,0:T(8,128)(2,1)S(1)} %get-tuple-element.221.left_ref, bf16[2048,2048]{1,0:T(8,128)(2,1)S(1)} %shard_map.112.weight_ref), custom_call_target="tpu_custom_call" | custom-call | tf_op jit(solution)/shard_map/pallas_call | solution.py:80
  68.7 1.3 %collective-permute-start.21 = (bf16[2,2,16,2048]{3,2,1,0:T(8,128)(2,1)S(1)}, bf16[2,2,16,2048]{3,2,1,0:T(8,128)(2,1)S(1)}, u32[]{:S(2)}, u32[]{:S(2)}) collective-permute-start(bf16[2,2,16,2048]{3,2,1,0:T(8,128)(2,1)S(1)} %slice.147), channel_id=1, source_target_pairs={{0,1},{1,0},{2,3},{3,2},{4,5},{5,4},{6,7},{7,6},{8,9},{9,8},{10,11... | collective-permute-start | bytes 786440 | tf_op jit(solution)/shard_map/ppermute | solution.py:202
  70.1 1.5 %shard_map.121 = f32[128,2048]{1,0:T(8,128)S(1)} custom-call(bf16[128,2048]{1,0:T(8,128)(2,1)S(1)} %multiply_convert_fusion.1.left_ref, bf16[2048,2048]{1,0:T(8,128)(2,1)S(1)} %shard_map.118.weight_ref), custom_call_target="tpu_custom_call" | custom-call | tf_op jit(solution)/shard_map/pallas_call | solution.py:80
  71.6 2.4 %collective-permute-done.19 = bf16[64,2048]{1,0:T(8,128)(2,1)S(1)} collective-permute-done((bf16[64,2048]{1,0:T(8,128)(2,1)S(1)}, bf16[64,2048]{1,0:T(8,128)(2,1)S(1)}, u32[]{:S(2)}, u32[]{:S(2)}) %collective-permute-start.19) | collective-permute-done | bytes 262176 | tf_op jit(solution)/shard_map/ppermute | solution.py:202
  74.1 3.2 %collective-permute-done.21 = bf16[2,2,16,2048]{3,2,1,0:T(8,128)(2,1)S(1)} collective-permute-done((bf16[2,2,16,2048]{3,2,1,0:T(8,128)(2,1)S(1)}, bf16[2,2,16,2048]{3,2,1,0:T(8,128)(2,1)S(1)}, u32[]{:S(2)}, u32[]{:S(2)}) %collective-permute-start.21) | collective-permute-done | bytes 262176 | tf_op jit(solution)/shard_map/ppermute | solution.py:202
  77.7 3.4 %collective-permute-start.25 = (bf16[2,2,16,2048]{3,2,1,0:T(8,128)(2,1)S(1)}, bf16[2,2,16,2048]{3,2,1,0:T(8,128)(2,1)S(1)}, u32[]{:S(2)}, u32[]{:S(2)}) collective-permute-start(bf16[2,2,16,2048]{3,2,1,0:T(8,128)(2,1)S(1)} %fusion.19), channel_id=1, source_target_pairs={{0,2},{1,3},{2,0},{3,1},{4,6},{5,7},{6,4},{7,5},{8,10},{9,11},{10,... | collective-permute-start | bytes 786440 | tf_op jit(solution)/shard_map/ppermute | solution.py:202
  81.3 1.5 %shard_map.122 = f32[128,2048]{1,0:T(8,128)S(1)} custom-call(bf16[128,2048]{1,0:T(8,128)(2,1)S(1)} %multiply_convert_fusion.left_ref, bf16[2048,2048]{1,0:T(8,128)(2,1)S(1)} %shard_map.118.weight_ref), custom_call_target="tpu_custom_call" | custom-call | tf_op jit(solution)/shard_map/pallas_call | solution.py:80
  83.0 1.3 %collective-permute-start.24 = (bf16[2,2,16,2048]{3,2,1,0:T(8,128)(2,1)S(1)}, bf16[2,2,16,2048]{3,2,1,0:T(8,128)(2,1)S(1)}, u32[]{:S(2)}, u32[]{:S(2)}) collective-permute-start(bf16[2,2,16,2048]{3,2,1,0:T(8,128)(2,1)S(1)} %slice.150), channel_id=1, source_target_pairs={{0,1},{1,0},{2,3},{3,2},{4,5},{5,4},{6,7},{7,6},{8,9},{9,8},{10,11... | collective-permute-start | bytes 786440 | tf_op jit(solution)/shard_map/ppermute | solution.py:202
  85.4 5.8 %shard_map.123 = bf16[2048,2048]{1,0:T(8,128)(2,1)} custom-call(s32[8,8]{1,0:T(8,128)S(1)} %convert_element_type.144.mask_ref, bf16[256,2048]{1,0:T(8,128)(2,1)S(1)} %pad_maximum_fusion.left_ref, bf16[256,2048]{1,0:T(8,128)(2,1)S(1)} %pad_maximum_fusion.1.right_ref), custom_call_target="tpu_custom_call" | custom-call | tf_op jit(solution)/shard_map/pallas_call | solution.py:108
  91.9 1.3 %collective-permute-start.27 = (bf16[2,2,16,2048]{3,2,1,0:T(8,128)(2,1)S(1)}, bf16[2,2,16,2048]{3,2,1,0:T(8,128)(2,1)S(1)}, u32[]{:S(2)}, u32[]{:S(2)}) collective-permute-start(bf16[2,2,16,2048]{3,2,1,0:T(8,128)(2,1)S(1)} %slice.127), channel_id=1, source_target_pairs={{0,1},{1,0},{2,3},{3,2},{4,5},{5,4},{6,7},{7,6},{8,9},{9,8},{10,11... | collective-permute-start | bytes 786440 | tf_op jit(solution)/shard_map/ppermute | solution.py:202
  93.4 1.0 collective-permute-start.29
  94.4 1.8 %collective-permute-start.28 = (bf16[2,16,2048]{2,1,0:T(8,128)(2,1)S(1)}, bf16[2,16,2048]{2,1,0:T(8,128)(2,1)S(1)}, u32[]{:S(2)}, u32[]{:S(2)}) collective-permute-start(bf16[2,16,2048]{2,1,0:T(8,128)(2,1)S(1)} %fusion.23), channel_id=1, source_target_pairs={{0,4},{1,5},{2,6},{3,7},{4,0},{5,1},{6,2},{7,3},{8,12},{9,13},{10,... | collective-permute-start | bytes 393224 | tf_op jit(solution)/shard_map/ppermute | solution.py:202
  96.3 1.1 collective-permute-start.26
  97.3 6.4 %collective-permute-done.26 = f32[2048]{0:T(1024)S(1)} collective-permute-done((f32[2048]{0:T(1024)S(1)}, f32[2048]{0:T(1024)S(1)}, u32[]{:S(2)}, u32[]{:S(2)}) %collective-permute-start.26) | collective-permute-done | bytes 8224 | tf_op jit(solution)/shard_map/ppermute | solution.py:202
  103.8 1.8 %collective-permute-start.30 = (f32[2048]{0:T(1024)S(1)}, f32[2048]{0:T(1024)S(1)}, u32[]{:S(2)}, u32[]{:S(2)}) collective-permute-start(f32[2048]{0:T(1024)S(1)} %add.144), channel_id=1, source_target_pairs={{0,4},{1,5},{2,6},{3,7},{4,0},{5,1},{6,2},{7,3},{8,12},{9,13},{10,... | collective-permute-start | bytes 24584 | tf_op jit(solution)/shard_map/ppermute | solution.py:202
  105.8 1.3 %collective-permute-start.31 = (bf16[2,16,2048]{2,1,0:T(8,128)(2,1)S(1)}, bf16[2,16,2048]{2,1,0:T(8,128)(2,1)S(1)}, u32[]{:S(2)}, u32[]{:S(2)}) collective-permute-start(bf16[2,16,2048]{2,1,0:T(8,128)(2,1)S(1)} %fusion.24), channel_id=1, source_target_pairs={{0,4},{1,5},{2,6},{3,7},{4,0},{5,1},{6,2},{7,3},{8,12},{9,13},{10,... | collective-permute-start | bytes 393224 | tf_op jit(solution)/shard_map/ppermute | solution.py:202
  107.4 5.6 %shard_map.124 = bf16[2048,2048]{1,0:T(8,128)(2,1)} custom-call(s32[8,8]{1,0:T(8,128)S(1)} %convert_element_type.143.mask_ref, bf16[256,2048]{1,0:T(8,128)(2,1)S(1)} %pad_maximum_fusion.2.left_ref, bf16[256,2048]{1,0:T(8,128)(2,1)S(1)} %pad_maximum_fusion.3.right_ref), custom_call_target="tpu_custom_call" | custom-call | tf_op jit(solution)/shard_map/pallas_call | solution.py:108
  113.1 1.0 collective-permute-start.33
  115.7 1.2 collective-permute-start.36
  116.9 0.9 collective-permute-start.37
  118.5 1.0 collective-permute-done.36
  120.2 1.0 collective-permute-done.37
  (152 shorter events, 17.8 us)
Async XLA Ops:
  0.6 12.7 %copy-start = (s32[32,32]{1,0:T(8,128)S(1)}, s32[32,32]{1,0:T(8,128)}, u32[]{:S(2)}) copy-start(s32[32,32]{1,0:T(8,128)} %param.12) | copy-start | bytes 12292
  1.6 5.3 %collective-permute-start.1 = (bf16[8,4096]{1,0:T(8,128)(2,1)S(1)}, bf16[8,4096]{1,0:T(8,128)(2,1)S(1)}, u32[]{:S(2)}, u32[]{:S(2)}) collective-permute-start(bf16[8,4096]{1,0:T(8,128)(2,1)S(1)} %get-tuple-element.305), channel_id=1, source_target_pairs={{0,16},{8,24},{16,0},{24,8},{1,17},{9,25},{17,1},{25,9},{2,18},{10... | collective-permute-start | bytes 196616 | tf_op jit(solution)/shard_map/ppermute | solution.py:202
  5.9 4.3 %collective-permute-start = (bf16[8,4096]{1,0:T(8,128)(2,1)S(1)}, bf16[8,4096]{1,0:T(8,128)(2,1)S(1)}, u32[]{:S(2)}, u32[]{:S(2)}) collective-permute-start(bf16[8,4096]{1,0:T(8,128)(2,1)S(1)} %get-tuple-element.139), channel_id=1, source_target_pairs={{0,16},{8,24},{16,0},{24,8},{1,17},{9,25},{17,1},{25,9},{2,18},{10... | collective-permute-start | bytes 196616 | tf_op jit(solution)/shard_map/ppermute | solution.py:202
  10.3 1.4 %collective-permute-start.2 = (bf16[2,16,2048]{2,1,0:T(8,128)(2,1)S(1)}, bf16[2,16,2048]{2,1,0:T(8,128)(2,1)S(1)}, u32[]{:S(2)}, u32[]{:S(2)}) collective-permute-start(bf16[2,16,2048]{2,1,0:T(8,128)(2,1)S(1)} %pad_maximum_fusion.10), channel_id=1, source_target_pairs={{0,8},{8,0},{16,24},{24,16},{1,9},{9,1},{17,25},{25,17},{2,10},{10... | collective-permute-start | bytes 393224 | tf_op jit(solution)/shard_map/ppermute | solution.py:202
  11.8 10.5 %collective-permute-start.3 = (bf16[2,2,16,2048]{3,2,1,0:T(8,128)(2,1)S(1)}, bf16[2,2,16,2048]{3,2,1,0:T(8,128)(2,1)S(1)}, u32[]{:S(2)}, u32[]{:S(2)}) collective-permute-start(bf16[2,2,16,2048]{3,2,1,0:T(8,128)(2,1)S(1)} %pad_maximum_fusion.7), channel_id=1, source_target_pairs={{0,1},{1,0},{2,3},{3,2},{4,5},{5,4},{6,7},{7,6},{8,9},{9,8},{10,11... | collective-permute-start | bytes 786440 | tf_op jit(solution)/shard_map/ppermute | solution.py:202
  13.3 9.0 %collective-permute-start.4 = (bf16[1,2,16,2048]{3,2,1,0:T(8,128)(2,1)S(1)}, bf16[1,2,16,2048]{3,2,1,0:T(8,128)(2,1)S(1)}, u32[]{:S(2)}, u32[]{:S(2)}) collective-permute-start(bf16[1,2,16,2048]{3,2,1,0:T(8,128)(2,1)S(1)} %get-tuple-element.153), channel_id=1, source_target_pairs={{0,4},{1,5},{2,6},{3,7},{4,0},{5,1},{6,2},{7,3},{8,12},{9,13},{10,... | collective-permute-start | bytes 393224 | tf_op jit(solution)/shard_map/ppermute | solution.py:202
  22.3 8.4 %collective-permute-start.7 = (bf16[1,2,16,2048]{3,2,1,0:T(8,128)(2,1)S(1)}, bf16[1,2,16,2048]{3,2,1,0:T(8,128)(2,1)S(1)}, u32[]{:S(2)}, u32[]{:S(2)}) collective-permute-start(bf16[1,2,16,2048]{3,2,1,0:T(8,128)(2,1)S(1)} %collective-permute-done.4), channel_id=1, source_target_pairs={{0,1},{1,0},{2,3},{3,2},{4,5},{5,4},{6,7},{7,6},{8,9},{9,8},{10,11... | collective-permute-start | bytes 393224 | tf_op jit(solution)/shard_map/ppermute | solution.py:202
  22.9 9.8 %collective-permute-start.5 = (bf16[2,2,16,2048]{3,2,1,0:T(8,128)(2,1)S(1)}, bf16[2,2,16,2048]{3,2,1,0:T(8,128)(2,1)S(1)}, u32[]{:S(2)}, u32[]{:S(2)}) collective-permute-start(bf16[2,2,16,2048]{3,2,1,0:T(8,128)(2,1)S(1)} %pad_maximum_fusion.8), channel_id=1, source_target_pairs={{0,2},{1,3},{2,0},{3,1},{4,6},{5,7},{6,4},{7,5},{8,10},{9,11},{10,... | collective-permute-start | bytes 786440 | tf_op jit(solution)/shard_map/ppermute | solution.py:202
  23.6 8.8 %collective-permute-start.6 = (bf16[1,2,16,2048]{3,2,1,0:T(8,128)(2,1)S(1)}, bf16[1,2,16,2048]{3,2,1,0:T(8,128)(2,1)S(1)}, u32[]{:S(2)}, u32[]{:S(2)}) collective-permute-start(bf16[1,2,16,2048]{3,2,1,0:T(8,128)(2,1)S(1)} %get-tuple-element.165), channel_id=1, source_target_pairs={{0,4},{1,5},{2,6},{3,7},{4,0},{5,1},{6,2},{7,3},{8,12},{9,13},{10,... | collective-permute-start | bytes 393224 | tf_op jit(solution)/shard_map/ppermute | solution.py:202
  32.7 2.1 %collective-permute-start.8 = (bf16[64,2048]{1,0:T(8,128)(2,1)S(1)}, bf16[64,2048]{1,0:T(8,128)(2,1)S(1)}, u32[]{:S(2)}, u32[]{:S(2)}) collective-permute-start(bf16[64,2048]{1,0:T(8,128)(2,1)S(1)} %slice.188), channel_id=1, source_target_pairs={{0,8},{8,0},{16,24},{24,16},{1,9},{9,1},{17,25},{25,17},{2,10},{10... | collective-permute-start | bytes 786440 | tf_op jit(solution)/shard_map/ppermute | solution.py:202
  32.7 13.2 %collective-permute-start.10 = (bf16[2,2,16,2048]{3,2,1,0:T(8,128)(2,1)S(1)}, bf16[2,2,16,2048]{3,2,1,0:T(8,128)(2,1)S(1)}, u32[]{:S(2)}, u32[]{:S(2)}) collective-permute-start(bf16[2,2,16,2048]{3,2,1,0:T(8,128)(2,1)S(1)} %collective-permute-done.5), channel_id=1, source_target_pairs={{0,1},{1,0},{2,3},{3,2},{4,5},{5,4},{6,7},{7,6},{8,9},{9,8},{10,11... | collective-permute-start | bytes 786440 | tf_op jit(solution)/shard_map/ppermute | solution.py:202
  34.2 10.0 %collective-permute-start.12 = (bf16[1,2,16,2048]{3,2,1,0:T(8,128)(2,1)S(1)}, bf16[1,2,16,2048]{3,2,1,0:T(8,128)(2,1)S(1)}, u32[]{:S(2)}, u32[]{:S(2)}) collective-permute-start(bf16[1,2,16,2048]{3,2,1,0:T(8,128)(2,1)S(1)} %collective-permute-done.6), channel_id=1, source_target_pairs={{0,1},{1,0},{2,3},{3,2},{4,5},{5,4},{6,7},{7,6},{8,9},{9,8},{10,11... | collective-permute-start | bytes 393224 | tf_op jit(solution)/shard_map/ppermute | solution.py:202
  34.8 11.0 %collective-permute-start.9 = (bf16[64,2048]{1,0:T(8,128)(2,1)S(1)}, bf16[64,2048]{1,0:T(8,128)(2,1)S(1)}, u32[]{:S(2)}, u32[]{:S(2)}) collective-permute-start(bf16[64,2048]{1,0:T(8,128)(2,1)S(1)} %get-tuple-element.277), channel_id=1, source_target_pairs={{0,16},{8,24},{16,0},{24,8},{1,17},{9,25},{17,1},{25,9},{2,18},{10... | collective-permute-start | bytes 786440 | tf_op jit(solution)/shard_map/ppermute | solution.py:202
  35.7 10.2 %collective-permute-start.11 = (bf16[2,2,16,2048]{3,2,1,0:T(8,128)(2,1)S(1)}, bf16[2,2,16,2048]{3,2,1,0:T(8,128)(2,1)S(1)}, u32[]{:S(2)}, u32[]{:S(2)}) collective-permute-start(bf16[2,2,16,2048]{3,2,1,0:T(8,128)(2,1)S(1)} %pad_maximum_fusion.9), channel_id=1, source_target_pairs={{0,2},{1,3},{2,0},{3,1},{4,6},{5,7},{6,4},{7,5},{8,10},{9,11},{10,... | collective-permute-start | bytes 786440 | tf_op jit(solution)/shard_map/ppermute | solution.py:202
  45.8 1.8 %copy-start.2 = (f32[128,2048]{1,0:T(8,128)}, f32[128,2048]{1,0:T(8,128)S(1)}, u32[]{:S(2)}) copy-start(f32[128,2048]{1,0:T(8,128)S(1)} %shard_map.115) | copy-start | bytes 3145732
  47.6 2.0 %collective-permute-start.13 = (bf16[128,2048]{1,0:T(8,128)(2,1)S(1)}, bf16[128,2048]{1,0:T(8,128)(2,1)S(1)}, u32[]{:S(2)}, u32[]{:S(2)}) collective-permute-start(bf16[128,2048]{1,0:T(8,128)(2,1)S(1)} %pad_maximum_fusion.4), channel_id=1, source_target_pairs={{0,8},{8,0},{16,24},{24,16},{1,9},{9,1},{17,25},{25,17},{2,10},{10... | collective-permute-start | bytes 1572872 | tf_op jit(solution)/shard_map/ppermute | solution.py:202
  47.7 1.9 %slice-start = ((f32[128,2048]{1,0:T(8,128)}), f32[64,2048]{1,0:T(8,128)S(1)}, s32[]{:S(2)}) async-start(f32[128,2048]{1,0:T(8,128)} %copy-done.2), calls=%async_computation | async-start | bytes 1048576 | tf_op jit(solution)/shard_map/slice | solution.py:294
  47.7 9.3 %collective-permute-start.15 = (bf16[2,2,16,2048]{3,2,1,0:T(8,128)(2,1)S(1)}, bf16[2,2,16,2048]{3,2,1,0:T(8,128)(2,1)S(1)}, u32[]{:S(2)}, u32[]{:S(2)}) collective-permute-start(bf16[2,2,16,2048]{3,2,1,0:T(8,128)(2,1)S(1)} %collective-permute-done.11), channel_id=1, source_target_pairs={{0,1},{1,0},{2,3},{3,2},{4,5},{5,4},{6,7},{7,6},{8,9},{9,8},{10,11... | collective-permute-start | bytes 786440 | tf_op jit(solution)/shard_map/ppermute | solution.py:202
  49.4 1.6 %collective-permute-start.16 = (bf16[64,2048]{1,0:T(8,128)(2,1)S(1)}, bf16[64,2048]{1,0:T(8,128)(2,1)S(1)}, u32[]{:S(2)}, u32[]{:S(2)}) collective-permute-start(bf16[64,2048]{1,0:T(8,128)(2,1)S(1)} %add_convert_fusion.2), channel_id=1, source_target_pairs={{0,8},{8,0},{16,24},{24,16},{1,9},{9,1},{17,25},{25,17},{2,10},{10... | collective-permute-start | bytes 786440 | tf_op jit(solution)/shard_map/ppermute | solution.py:202
  49.8 14.2 %collective-permute-start.14 = (bf16[128,2048]{1,0:T(8,128)(2,1)S(1)}, bf16[128,2048]{1,0:T(8,128)(2,1)S(1)}, u32[]{:S(2)}, u32[]{:S(2)}) collective-permute-start(bf16[128,2048]{1,0:T(8,128)(2,1)S(1)} %get-tuple-element.275), channel_id=1, source_target_pairs={{0,16},{8,24},{16,0},{24,8},{1,17},{9,25},{17,1},{25,9},{2,18},{10... | collective-permute-start | bytes 1572872 | tf_op jit(solution)/shard_map/ppermute | solution.py:202
  53.3 8.8 %collective-permute-start.17 = (bf16[2,2,16,2048]{3,2,1,0:T(8,128)(2,1)S(1)}, bf16[2,2,16,2048]{3,2,1,0:T(8,128)(2,1)S(1)}, u32[]{:S(2)}, u32[]{:S(2)}) collective-permute-start(bf16[2,2,16,2048]{3,2,1,0:T(8,128)(2,1)S(1)} %slice.117), channel_id=1, source_target_pairs={{0,1},{1,0},{2,3},{3,2},{4,5},{5,4},{6,7},{7,6},{8,9},{9,8},{10,11... | collective-permute-start | bytes 786440 | tf_op jit(solution)/shard_map/ppermute | solution.py:202
  64.0 1.5 %collective-permute-start.18 = (bf16[64,2048]{1,0:T(8,128)(2,1)S(1)}, bf16[64,2048]{1,0:T(8,128)(2,1)S(1)}, u32[]{:S(2)}, u32[]{:S(2)}) collective-permute-start(bf16[64,2048]{1,0:T(8,128)(2,1)S(1)} %slice.185), channel_id=1, source_target_pairs={{0,8},{8,0},{16,24},{24,16},{1,9},{9,1},{17,25},{25,17},{2,10},{10... | collective-permute-start | bytes 786440 | tf_op jit(solution)/shard_map/ppermute | solution.py:202
  64.2 2.1 %collective-permute-start.20 = (bf16[128,2048]{1,0:T(8,128)(2,1)S(1)}, bf16[128,2048]{1,0:T(8,128)(2,1)S(1)}, u32[]{:S(2)}, u32[]{:S(2)}) collective-permute-start(bf16[128,2048]{1,0:T(8,128)(2,1)S(1)} %add_convert_fusion), channel_id=1, source_target_pairs={{0,8},{8,0},{16,24},{24,16},{1,9},{9,1},{17,25},{25,17},{2,10},{10... | collective-permute-start | bytes 1572872 | tf_op jit(solution)/shard_map/ppermute | solution.py:202
  65.6 8.4 %collective-permute-start.19 = (bf16[64,2048]{1,0:T(8,128)(2,1)S(1)}, bf16[64,2048]{1,0:T(8,128)(2,1)S(1)}, u32[]{:S(2)}, u32[]{:S(2)}) collective-permute-start(bf16[64,2048]{1,0:T(8,128)(2,1)S(1)} %get-tuple-element.273), channel_id=1, source_target_pairs={{0,16},{8,24},{16,0},{24,8},{1,17},{9,25},{17,1},{25,9},{2,18},{10... | collective-permute-start | bytes 786440 | tf_op jit(solution)/shard_map/ppermute | solution.py:202
  68.7 8.6 %collective-permute-start.21 = (bf16[2,2,16,2048]{3,2,1,0:T(8,128)(2,1)S(1)}, bf16[2,2,16,2048]{3,2,1,0:T(8,128)(2,1)S(1)}, u32[]{:S(2)}, u32[]{:S(2)}) collective-permute-start(bf16[2,2,16,2048]{3,2,1,0:T(8,128)(2,1)S(1)} %slice.147), channel_id=1, source_target_pairs={{0,1},{1,0},{2,3},{3,2},{4,5},{5,4},{6,7},{7,6},{8,9},{9,8},{10,11... | collective-permute-start | bytes 786440 | tf_op jit(solution)/shard_map/ppermute | solution.py:202
  77.3 3.9 %collective-permute-start.22 = (bf16[64,2048]{1,0:T(8,128)(2,1)S(1)}, bf16[64,2048]{1,0:T(8,128)(2,1)S(1)}, u32[]{:S(2)}, u32[]{:S(2)}) collective-permute-start(bf16[64,2048]{1,0:T(8,128)(2,1)S(1)} %add_convert_fusion.1), channel_id=1, source_target_pairs={{0,8},{8,0},{16,24},{24,16},{1,9},{9,1},{17,25},{25,17},{2,10},{10... | collective-permute-start | bytes 786440 | tf_op jit(solution)/shard_map/ppermute | solution.py:202
  77.7 13.6 %collective-permute-start.25 = (bf16[2,2,16,2048]{3,2,1,0:T(8,128)(2,1)S(1)}, bf16[2,2,16,2048]{3,2,1,0:T(8,128)(2,1)S(1)}, u32[]{:S(2)}, u32[]{:S(2)}) collective-permute-start(bf16[2,2,16,2048]{3,2,1,0:T(8,128)(2,1)S(1)} %fusion.19), channel_id=1, source_target_pairs={{0,2},{1,3},{2,0},{3,1},{4,6},{5,7},{6,4},{7,5},{8,10},{9,11},{10,... | collective-permute-start | bytes 786440 | tf_op jit(solution)/shard_map/ppermute | solution.py:202
  83.0 8.7 %collective-permute-start.24 = (bf16[2,2,16,2048]{3,2,1,0:T(8,128)(2,1)S(1)}, bf16[2,2,16,2048]{3,2,1,0:T(8,128)(2,1)S(1)}, u32[]{:S(2)}, u32[]{:S(2)}) collective-permute-start(bf16[2,2,16,2048]{3,2,1,0:T(8,128)(2,1)S(1)} %slice.150), channel_id=1, source_target_pairs={{0,1},{1,0},{2,3},{3,2},{4,5},{5,4},{6,7},{7,6},{8,9},{9,8},{10,11... | collective-permute-start | bytes 786440 | tf_op jit(solution)/shard_map/ppermute | solution.py:202
  84.5 7.2 %collective-permute-start.23 = (f32[2048]{0:T(1024)S(1)}, f32[2048]{0:T(1024)S(1)}, u32[]{:S(2)}, u32[]{:S(2)}) collective-permute-start(f32[2048]{0:T(1024)S(1)} %add.138), channel_id=1, source_target_pairs={{0,1},{1,0},{2,3},{3,2},{4,5},{5,4},{6,7},{7,6},{8,9},{9,8},{10,11... | collective-permute-start | bytes 24584 | tf_op jit(solution)/shard_map/ppermute | solution.py:202
  91.9 11.9 %collective-permute-start.27 = (bf16[2,2,16,2048]{3,2,1,0:T(8,128)(2,1)S(1)}, bf16[2,2,16,2048]{3,2,1,0:T(8,128)(2,1)S(1)}, u32[]{:S(2)}, u32[]{:S(2)}) collective-permute-start(bf16[2,2,16,2048]{3,2,1,0:T(8,128)(2,1)S(1)} %slice.127), channel_id=1, source_target_pairs={{0,1},{1,0},{2,3},{3,2},{4,5},{5,4},{6,7},{7,6},{8,9},{9,8},{10,11... | collective-permute-start | bytes 786440 | tf_op jit(solution)/shard_map/ppermute | solution.py:202
  93.4 10.4 %collective-permute-start.29 = (bf16[2,2,16,2048]{3,2,1,0:T(8,128)(2,1)S(1)}, bf16[2,2,16,2048]{3,2,1,0:T(8,128)(2,1)S(1)}, u32[]{:S(2)}, u32[]{:S(2)}) collective-permute-start(bf16[2,2,16,2048]{3,2,1,0:T(8,128)(2,1)S(1)} %fusion.18), channel_id=1, source_target_pairs={{0,2},{1,3},{2,0},{3,1},{4,6},{5,7},{6,4},{7,5},{8,10},{9,11},{10,... | collective-permute-start | bytes 786440 | tf_op jit(solution)/shard_map/ppermute | solution.py:202
  94.4 9.3 %collective-permute-start.28 = (bf16[2,16,2048]{2,1,0:T(8,128)(2,1)S(1)}, bf16[2,16,2048]{2,1,0:T(8,128)(2,1)S(1)}, u32[]{:S(2)}, u32[]{:S(2)}) collective-permute-start(bf16[2,16,2048]{2,1,0:T(8,128)(2,1)S(1)} %fusion.23), channel_id=1, source_target_pairs={{0,4},{1,5},{2,6},{3,7},{4,0},{5,1},{6,2},{7,3},{8,12},{9,13},{10,... | collective-permute-start | bytes 393224 | tf_op jit(solution)/shard_map/ppermute | solution.py:202
  96.3 7.5 %collective-permute-start.26 = (f32[2048]{0:T(1024)S(1)}, f32[2048]{0:T(1024)S(1)}, u32[]{:S(2)}, u32[]{:S(2)}) collective-permute-start(f32[2048]{0:T(1024)S(1)} %add.141), channel_id=1, source_target_pairs={{0,2},{1,3},{2,0},{3,1},{4,6},{5,7},{6,4},{7,5},{8,10},{9,11},{10,... | collective-permute-start | bytes 24584 | tf_op jit(solution)/shard_map/ppermute | solution.py:202
  103.8 9.3 %collective-permute-start.30 = (f32[2048]{0:T(1024)S(1)}, f32[2048]{0:T(1024)S(1)}, u32[]{:S(2)}, u32[]{:S(2)}) collective-permute-start(f32[2048]{0:T(1024)S(1)} %add.144), channel_id=1, source_target_pairs={{0,4},{1,5},{2,6},{3,7},{4,0},{5,1},{6,2},{7,3},{8,12},{9,13},{10,... | collective-permute-start | bytes 24584 | tf_op jit(solution)/shard_map/ppermute | solution.py:202
  105.8 7.3 %collective-permute-start.31 = (bf16[2,16,2048]{2,1,0:T(8,128)(2,1)S(1)}, bf16[2,16,2048]{2,1,0:T(8,128)(2,1)S(1)}, u32[]{:S(2)}, u32[]{:S(2)}) collective-permute-start(bf16[2,16,2048]{2,1,0:T(8,128)(2,1)S(1)} %fusion.24), channel_id=1, source_target_pairs={{0,4},{1,5},{2,6},{3,7},{4,0},{5,1},{6,2},{7,3},{8,12},{9,13},{10,... | collective-permute-start | bytes 393224 | tf_op jit(solution)/shard_map/ppermute | solution.py:202
  107.1 5.9 %collective-permute-start.32 = (bf16[16,2048]{1,0:T(8,128)(2,1)S(1)}, bf16[16,2048]{1,0:T(8,128)(2,1)S(1)}, u32[]{:S(2)}, u32[]{:S(2)}) collective-permute-start(bf16[16,2048]{1,0:T(8,128)(2,1)S(1)} %get-tuple-element.297), channel_id=1, source_target_pairs={{0,8},{8,0},{16,24},{24,16},{1,9},{9,1},{17,25},{25,17},{2,10},{10... | collective-permute-start | bytes 196616 | tf_op jit(solution)/shard_map/ppermute | solution.py:202
  107.4 10.4 %copy-start.3 = (bf16[8,8192]{1,0:T(8,128)(2,1)S(1)}, bf16[8,8192]{1,0:T(8,128)(2,1)}, u32[]{:S(2)}) copy-start(bf16[8,8192]{1,0:T(8,128)(2,1)} %input_hbm.1) | copy-start | bytes 393220
  107.4 14.8 %copy-start.1 = (s32[32,32]{1,0:T(8,128)S(1)}, s32[32,32]{1,0:T(8,128)}, u32[]{:S(2)}) copy-start(s32[32,32]{1,0:T(8,128)} %param.12) | copy-start | bytes 12292
  113.0 6.6 %copy-start.5 = (f32[8192]{0:T(1024)S(1)}, f32[8192]{0:T(1024)}, u32[]{:S(2)}) copy-start(f32[8192]{0:T(1024)} %param.8) | copy-start | bytes 98308
  113.0 8.4 %copy-start.4 = (bf16[8,8192]{1,0:T(8,128)(2,1)S(1)}, bf16[8,8192]{1,0:T(8,128)(2,1)}, u32[]{:S(2)}) copy-start(bf16[8,8192]{1,0:T(8,128)(2,1)} %param.13) | copy-start | bytes 393220
  113.1 4.7 %collective-permute-start.33 = (bf16[8,4096]{1,0:T(8,128)(2,1)S(1)}, bf16[8,4096]{1,0:T(8,128)(2,1)S(1)}, u32[]{:S(2)}, u32[]{:S(2)}) collective-permute-start(bf16[8,4096]{1,0:T(8,128)(2,1)S(1)} %get-tuple-element.255), channel_id=1, source_target_pairs={{0,16},{8,24},{16,0},{24,8},{1,17},{9,25},{17,1},{25,9},{2,18},{10... | collective-permute-start | bytes 196616 | tf_op jit(solution)/shard_map/ppermute | solution.py:202
  114.1 1.2 collective-permute-start.34
  114.3 1.3 %collective-permute-start.35 = (bf16[16,2048]{1,0:T(8,128)(2,1)S(1)}, bf16[16,2048]{1,0:T(8,128)(2,1)S(1)}, u32[]{:S(2)}, u32[]{:S(2)}) collective-permute-start(bf16[16,2048]{1,0:T(8,128)(2,1)S(1)} %get-tuple-element.293), channel_id=1, source_target_pairs={{0,8},{8,0},{16,24},{24,16},{1,9},{9,1},{17,25},{25,17},{2,10},{10... | collective-permute-start | bytes 196616 | tf_op jit(solution)/shard_map/ppermute | solution.py:202
  115.7 3.8 %collective-permute-start.36 = (f32[4096]{0:T(1024)S(1)}, f32[4096]{0:T(1024)S(1)}, u32[]{:S(2)}, u32[]{:S(2)}) collective-permute-start(f32[4096]{0:T(1024)S(1)} %maximum_select_fusion.7), channel_id=1, source_target_pairs={{0,16},{8,24},{16,0},{24,8},{1,17},{9,25},{17,1},{25,9},{2,18},{10... | collective-permute-start | bytes 49160 | tf_op jit(solution)/shard_map/ppermute | solution.py:202
  116.9 4.3 %collective-permute-start.37 = (bf16[8,4096]{1,0:T(8,128)(2,1)S(1)}, bf16[8,4096]{1,0:T(8,128)(2,1)S(1)}, u32[]{:S(2)}, u32[]{:S(2)}) collective-permute-start(bf16[8,4096]{1,0:T(8,128)(2,1)S(1)} %get-tuple-element.291), channel_id=1, source_target_pairs={{0,16},{8,24},{16,0},{24,8},{1,17},{9,25},{17,1},{25,9},{2,18},{10... | collective-permute-start | bytes 196616 | tf_op jit(solution)/shard_map/ppermute | solution.py:202

commit v3 on v2

--- a/solution.py
+++ b/solution.py
@@ -239,6 +239,10 @@
         return tuple(values[n] for n in results)
 
 
+def first(pair):
+    return pair[0]
+
+
 def second(pair):
     return pair[1]
 
@@ -266,25 +270,38 @@
     def to_core(v, got):
         return halves(ordered(v[0], got, far_bit, 0), core_bit, 1)
 
+    def across(stage, dep):
+        return swapped(stage, ("row", "col"), 2 * n_col + line[0], dep)
+
     g0 = work(0, lambda: halves(out_grad, far_bit, 1))
     gfar = swapped(0, "row", 2, work(0, second, g0))
     x0 = work(
         0,
         lambda: normalise(inputs, layer_norm_gain[None, :], far_bit.astype(jnp.int32)[None]),
     )
-    xfar = swapped(0, "row", 2, work(0, second, x0))
+    xgive = work(0, second, x0)
+    xline0 = work(
+        0,
+        lambda v, got: (v,  got),
+        swapped(0, "col", line[0], work(0, first, x0)),
+        across(0, xgive),
+    )
+    xfar = swapped(0, "row", 2, xgive)
     x1, g1 = work(0, to_core, x0, xfar), work(0, to_core, g0, gfar)
-    core = swapped(0, "row", 1, work(0, lambda x, g: jnp.stack([x[1], g[1]]), x1, g1))
-    xown = work(0, lambda v, got: jnp.stack([v[0], got[0]])[None], x1, core)
-    gown = work(0, lambda v, got: jnp.stack([v[0], got[1]])[None], g1, core)
-
-    mask_in = work(1, lambda: kept_tiles(
+    mask_in = work(0, lambda: kept_tiles(
         pattern_in, row_index * feat_tiles, feat_tiles, col_index * unit_tiles, unit_tiles
     ))
-    mask_out = work(1, lambda: kept_tiles(
+    mask_out = work(0, lambda: kept_tiles(
         pattern_out, col_index * unit_tiles, unit_tiles, row_index * feat_tiles, feat_tiles
     ))
-    in_e = work(1, lambda mask: keep(w_in, mask), mask_in)
+    in_e = work(0, lambda mask: keep(w_in, mask), mask_in)
+    x2 = work(0, lambda v, w: to_core(*lax.optimization_barrier((v, v[1], w))[:2]), xline0, in_e)
+    core = swapped(0, "row", 1, work(0, lambda *v: jnp.stack([w[1] for w in v]), x1, x2, g1))
+    xown, xline0, gown = [
+        work(0, lambda v, got, n=n: jnp.stack([v[0], got[n]])[None], v, core)
+        for n, v in enumerate((x1, x2, g1))
+    ]
+
     out_e = work(2, lambda mask: keep(w_out, mask), mask_out)
 
     def give_half(*parts):
@@ -295,8 +312,8 @@
         return kept + parts[-1].astype(F32)
 
     def row_sum(stages, parts, sizes):
-        first, core_stage, back, unpack = stages
-        got = swapped(core_stage, "row", 1, work(first, give_half, *parts))
+        begin, core_stage, back, unpack = stages
+        got = swapped(core_stage, "row", 1, work(begin, give_half, *parts))
         pair = work(core_stage, add_half, *parts, got)
         rounded = work(core_stage, to_bf16, pair)
         far = swapped(core_stage, "row", 2, rounded)
@@ -323,11 +340,11 @@
     def behind(value, *others):
         return lax.optimization_barrier((value,) + others)[0]
 
-    near = swapped(1, "col", 1, work(1, join, xown, gown))
-    xline, gline = [swapped(1, "col", line[0], xown)], []
-    xnear, gnear = [swapped(2, "col", 1, xline[0])], []
-    xheld, gheld = [xown, xline[0]], [gown]
-    xfirst, gfirst = work(2, lambda v: v[:1], near), work(2, lambda v: v[1:], near)
+    near = swapped(2, "col", 1, work(2, join, xown, xline0))
+    xline, gline = [xline0], []
+    xfirst, xnear = work(2, lambda v: v[:1], near), [work(2, lambda v: v[1:], near)]
+    gfirst, gnear = swapped(2, "col", 1, gown), []
+    xheld, gheld = [xown, xline0], [gown]
     for i in range(1, last):
         xline.append(swapped(1 + i, "col", line[i], work(1 + i, join, *xheld)))
         xheld.append(xline[i])
@@ -379,7 +396,7 @@
         return (v[: v.shape[0] // 2] if i else v[::2]) + got.astype(F32)
 
     made = [work(4 + i, forward, pre[i]) for i in range(last)]
-    act = [work(4 + i, lambda v: v[0], made[i]) for i in range(last)]
+    act = [work(4 + i, first, made[i]) for i in range(last)]
     yp = [work(4 + i, product, act[i], out_e) for i in range(last)]
     ygive = [work(4 + i, functools.partial(give_near, i), yp[i]) for i in range(last)]
     ynear = [swapped(4 + i, "col", 1, ygive[i]) for i in range(last)]
@@ -399,7 +416,13 @@
 
     gain = work(6, gain_terms, *np_, *xc)
     for b, distance in enumerate([1] + line[::-1]):
-        gain = work(min(7 + b, 9), add, gain, swapped(min(6 + b, 8), "col", distance, gain))
+        gain = work(7 if b < last else 8, add, gain, swapped(min(6 + b, 7), "col", distance, gain))
+    got = swapped(8, "row", 1, gain)
+    gain = work(8, lambda v, got: ordered(v, got, core_bit, 0), gain, got)
+    got = swapped(8, "row", 2, gain)
+    gain_gradient = work(
+        8, lambda v, got: ordered(v, got, far_bit, 0) / layer_norm_gain, gain, got
+    )
 
     nnear = [
         swapped(7, "col", 1, work(7, functools.partial(give_near, i), np_[i]))
@@ -407,7 +430,7 @@
     ] + [swapped(4 + last, "col", 1, last_give)]
 
     def line_sum(stage, products, got, late):
-        sums = [
+        sums, gives = [
             work(
                 stage if i or not late else stage + last - 1,
                 functools.partial(keep_near, i),
@@ -415,48 +438,48 @@
                 got[i],
             )
             for i in range(last)
-        ]
+        ], []
         for i in reversed(range(1, last)):
             when = stage + last - 1 - i
-            moved = swapped(when, "col", line[i], work(when, to_bf16, sums[i]))
+            gives.append(work(when, to_bf16, sums[i]))
+            moved = swapped(when, "col", line[i], gives[-1])
             for m in range(i):
-                first = sum(places[:m])
+                start = sum(places[:m])
                 sums[m] = work(
                     when + 1,
-                    lambda v, got, first=first: v + got[first : first + v.shape[0]].astype(F32),
+                    lambda v, got, start=start: v + got[start : start + v.shape[0]].astype(F32),
                     sums[m],
                     moved,
                 )
-        give = work(stage + last - 1, lambda v: v[1].astype(BF16), sums[0])
-        moved = swapped(stage + last - 1, "col", line[0], give)
-        return give, work(
-            stage + last, lambda v, got: (v[0] + got.astype(F32)).astype(BF16), sums[0], moved
-        )
-
-    def to_far(v, got):
-        return halves(ordered(v[0], got, core_bit, 1), far_bit, 0)
-
-    _, y = line_sum(6, yp, ynear, False)
-    last_sent, n = line_sum(7, np_, nnear, True)
-    y1 = work(8, to_far, y, swapped(8, "row", 1, work(8, second, y)))
-    n1 = work(9, to_far, n, swapped(9, "row", 1, work(9, second, n)))
-    yfar = swapped(9, "row", 2, work(9, second, y1))
-    nfar = swapped(9, "row", 2, work(9, second, n1))
+        return sums[0], gives[0]
+
+    y, _ = line_sum(6, yp, ynear, False)
+    moved = swapped(7, "col", line[0], work(7, lambda v: v[1].astype(BF16), y))
+    y = work(8, lambda v, got: (v[0] + got.astype(F32)).astype(BF16), y, moved)
+    got = swapped(8, "row", 1, work(8, second, y))
+    y = work(8, lambda v, got: halves(ordered(v[0], got, core_bit, 1), far_bit, 0), y, got)
+    got = swapped(8, "row", 2, work(8, second, y))
     output = work(9, lambda v, got: (
         inputs.astype(F32) + ordered(v[0], got, far_bit, 1).astype(F32)
-    ).astype(BF16), y1, yfar)
-
-    got = swapped(9, "row", 1, gain)
-    gain = work(9, lambda v, got: ordered(v, got, core_bit, 0), gain, got)
-    gain = work(9, lambda v, other: behind(v, other[0]), gain, n1)
-    got = swapped(9, "row", 2, gain)
-    gain_gradient = work(
-        9, lambda v, got: ordered(v, got, far_bit, 0) / layer_norm_gain, gain, got
-    )
-
-    def input_gradient(v, got, made):
+    ).astype(BF16), y, got)
+
+    n, last_sent = line_sum(7, np_, nnear, True)
+    got = swapped(8, "row", 1, work(8, lambda v: v[:, 1].astype(BF16), n))
+    n = work(
+        8,
+        lambda v, got: halves(ordered(v[:, 0], got.astype(F32), core_bit, 2), far_bit, 1),
+        n,
+        got,
+    )
+    own_line = swapped(8, "col", line[0], work(8, lambda v: v[0][1].astype(BF16), n))
+    far_line = across(8, work(8, lambda v: v[1][1].astype(BF16), n))
+    far_own = swapped(8, "row", 2, work(8, lambda v: v[1][0].astype(BF16), n))
+
+    def input_gradient(v, own_line, far_own, far_line, made):
         standard, deviation = made[2:]
-        scaled = ordered(v[0], got, far_bit, 1).astype(F32) * layer_norm_gain[None, :]
+        mine = v[0][0] + own_line.astype(F32)
+        other = far_own.astype(F32) + far_line.astype(F32)
+        scaled = ordered(mine, other, far_bit, 1) * layer_norm_gain[None, :]
         result = deviation * (
             scaled
             - jnp.mean(scaled, axis=1, keepdims=True)
@@ -464,14 +487,14 @@
         )
         return (out_grad.astype(F32) + result).astype(BF16)
 
-    grad_inputs = work(9, input_gradient, n1, nfar, x0)
+    grad_inputs = work(9, input_gradient, n, own_line, far_own, far_line, x0)
 
     def weight_gradient(mask, before, *parts):
         left, right = parts[:last], parts[last:]
         return outer(jnp.concatenate(left), jnp.concatenate(right), behind(mask, before))
 
     grad_w_out = work(4 + last, weight_gradient, mask_out, last_give, *act, *gc)
-    grad_w_in = work(8, weight_gradient, mask_in, last_sent, *xc, *d_pre)
+    grad_w_in = work(7, weight_gradient, mask_in, last_sent, *xc, *d_pre)
 
     return plan.run((output, grad_inputs, grad_w_in, grad_w_out, gain_gradient))
 

time: 122 us -> 115 us (0.943)
  waiting for transfers between devices: 31.8 us -> 24.8 us
    ppermute x38 -> x40, waiting for transfers between devices: 31.8 us -> 24.8 us  [swap(): return lax.ppermute(value, axis, [(i, i ^ distance) for i in range(size)])]
    ppermute x38 -> x40, starting transfers between devices: 41.6 us -> 41.5 us  [swap(): return lax.ppermute(value, axis, [(i, i ^ distance) for i in range(size)])]
  transfers between devices with their start and end apart: 38 -> 40, of which waited for: 19 -> 18; matrix products, arithmetic and copies ran while one was open for 6% -> 6% of each run, Pallas kernels for 29% -> 30%
where the time goes in v3:
time: 115 us; the launch traced here: 114 us
  starting transfers between devices  41.5 us (36%)
  Pallas kernels  37.3 us (32%)
  waiting for transfers between devices  24.8 us (22%)
  other arithmetic  7.31 us (6%)
  local copies, waits for them, and re-layouts  1.77 us (2%)
  between operations  1.59 us (1%)
    ppermute x40, starting transfers between devices, swap(): return lax.ppermute(value, axis, [(i, i ^ distance) for i in range(size)])  41.5 us
    ppermute x40, waiting for transfers between devices, swap(): return lax.ppermute(value, axis, [(i, i ^ distance) for i in range(size)])  24.8 us
    pallas_call x8, Pallas kernels, product(): pl.pallas_call(product_kernel, out_shape=jax.ShapeDtypeStruct((left.shape...  11.9 us
    pallas_call x2, Pallas kernels, outer(): pl.pallas_call(outer_kernel, grid=(rows // step,), out_shape=jax.ShapeDty...  11.4 us
    pallas_call x2, Pallas kernels, keep(): pl.pallas_call(keep_kernel, out_shape=pltpu.VMEM(weight.shape, weight.dty...  7.28 us
    pallas_call x2, Pallas kernels, turn(): pl.pallas_call(turn_kernel, out_shape=pltpu.VMEM(weight.shape[::-1], weig...  5.54 us
  transfers between devices with their start and end apart: 40, of which 18 were waited for; matrix products, arithmetic and copies ran while one was open for 6% of the time, Pallas kernels for 30%

profile of v3, /device:TPU:0, one launch (start us, length us, event | category | flops | bytes accessed | tf_op | source)
XLA Modules:
  0.0 114.3 jit_solution(9562884072025031512)
XLA Ops:
  0.7 1.3 %shard_map.110 = (bf16[8,4096]{1,0:T(8,128)(2,1)S(1)}, bf16[8,4096]{1,0:T(8,128)(2,1)S(1)}, f32[8,8192]{1,0:T(8,128)S(1)}, f32[8,1]{1,0:T(8,128)S(1)}) custom-call(s32[1]{0:T(128)} %bitcast.far_ref, bf16[8,8192]{1,0:T(8,128)(2,1)} %input_hbm.1, f32[1,8192]{1,0:T(1,128)} %bitcast.104), custom_call_target="tpu_custom_call" | custom-call | tf_op jit(solution)/shard_map/pallas_call | solution.py:151
  2.0 5.1 %collective-permute-start.2 = (bf16[8,4096]{1,0:T(8,128)(2,1)S(1)}, bf16[8,4096]{1,0:T(8,128)(2,1)S(1)}, u32[]{:S(2)}, u32[]{:S(2)}) collective-permute-start(bf16[8,4096]{1,0:T(8,128)(2,1)S(1)} %get-tuple-element.132), channel_id=1, source_target_pairs={{0,20},{1,21},{2,22},{3,23},{4,16},{5,17},{6,18},{7,19},{8,28},{9,... | collective-permute-start | bytes 196616 | tf_op jit(solution)/shard_map/ppermute | solution.py:202
  7.5 0.9 broadcast_select_fusion.3
  8.4 1.6 %collective-permute-start.3 = (bf16[8,4096]{1,0:T(8,128)(2,1)S(1)}, bf16[8,4096]{1,0:T(8,128)(2,1)S(1)}, u32[]{:S(2)}, u32[]{:S(2)}) collective-permute-start(bf16[8,4096]{1,0:T(8,128)(2,1)S(1)} %get-tuple-element.292), channel_id=1, source_target_pairs={{0,16},{8,24},{16,0},{24,8},{1,17},{9,25},{17,1},{25,9},{2,18},{10... | collective-permute-start | bytes 196616 | tf_op jit(solution)/shard_map/ppermute | solution.py:202
  11.5 3.9 %shard_map.111.weight_ref = bf16[2048,2048]{1,0:T(8,128)(2,1)S(1)} custom-call(s32[8,8]{1,0:T(8,128)S(1)} %convert_element_type.157.mask_ref, bf16[2048,2048]{1,0:T(8,128)(2,1)} %weight_ref.2), custom_call_target="tpu_custom_call" | custom-call | tf_op jit(solution)/shard_map/pallas_call | solution.py:56
  16.0 1.1 collective-permute-done.4
  17.3 1.3 %collective-permute-start.8 = (bf16[2,2,16,2048]{3,2,1,0:T(8,128)(2,1)S(1)}, bf16[2,2,16,2048]{3,2,1,0:T(8,128)(2,1)S(1)}, u32[]{:S(2)}, u32[]{:S(2)}) collective-permute-start(bf16[2,2,16,2048]{3,2,1,0:T(8,128)(2,1)S(1)} %constant_dynamic-update-slice_fusion), channel_id=1, source_target_pairs={{0,1},{1,0},{2,3},{3,2},{4,5},{5,4},{6,7},{7,6},{8,9},{9,8},{10,11... | collective-permute-start | bytes 786440 | tf_op jit(solution)/shard_map/ppermute | solution.py:202
  18.6 1.5 %collective-permute-start.6 = (bf16[2,2,16,2048]{3,2,1,0:T(8,128)(2,1)S(1)}, bf16[2,2,16,2048]{3,2,1,0:T(8,128)(2,1)S(1)}, u32[]{:S(2)}, u32[]{:S(2)}) collective-permute-start(bf16[2,2,16,2048]{3,2,1,0:T(8,128)(2,1)S(1)} %constant_dynamic-update-slice_fusion), channel_id=1, source_target_pairs={{0,2},{1,3},{2,0},{3,1},{4,6},{5,7},{6,4},{7,5},{8,10},{9,11},{10,... | collective-permute-start | bytes 786440 | tf_op jit(solution)/shard_map/ppermute | solution.py:202
  20.9 2.4 %collective-permute-start.7 = (bf16[1,2,16,2048]{3,2,1,0:T(8,128)(2,1)S(1)}, bf16[1,2,16,2048]{3,2,1,0:T(8,128)(2,1)S(1)}, u32[]{:S(2)}, u32[]{:S(2)}) collective-permute-start(bf16[1,2,16,2048]{3,2,1,0:T(8,128)(2,1)S(1)} %maximum_bitcast_fusion.6), channel_id=1, source_target_pairs={{0,4},{1,5},{2,6},{3,7},{4,0},{5,1},{6,2},{7,3},{8,12},{9,13},{10,... | collective-permute-start | bytes 393224 | tf_op jit(solution)/shard_map/ppermute | solution.py:202
  23.3 3.4 %shard_map.112.weight_ref = bf16[2048,2048]{1,0:T(8,128)(2,1)S(1)} custom-call(s32[8,8]{1,0:T(8,128)S(1)} %convert_element_type.158.mask_ref, bf16[2048,2048]{1,0:T(8,128)(2,1)} %weight_ref.3), custom_call_target="tpu_custom_call" | custom-call | tf_op jit(solution)/shard_map/pallas_call | solution.py:56
  26.9 1.5 %shard_map.113 = f32[128,2048]{1,0:T(8,128)S(1)} custom-call(bf16[128,2048]{1,0:T(8,128)(2,1)S(1)} %bitcast.85, bf16[2048,2048]{1,0:T(8,128)(2,1)S(1)} %shard_map.111.weight_ref), custom_call_target="tpu_custom_call" | custom-call | tf_op jit(solution)/shard_map/pallas_call | solution.py:80
  28.5 0.9 collective-permute-done.6
  30.2 1.3 %collective-permute-start.13 = (bf16[1,2,16,2048]{3,2,1,0:T(8,128)(2,1)S(1)}, bf16[1,2,16,2048]{3,2,1,0:T(8,128)(2,1)S(1)}, u32[]{:S(2)}, u32[]{:S(2)}) collective-permute-start(bf16[1,2,16,2048]{3,2,1,0:T(8,128)(2,1)S(1)} %collective-permute-done.7), channel_id=1, source_target_pairs={{0,1},{1,0},{2,3},{3,2},{4,5},{5,4},{6,7},{7,6},{8,9},{9,8},{10,11... | collective-permute-start | bytes 393224 | tf_op jit(solution)/shard_map/ppermute | solution.py:202
  32.2 2.6 %collective-permute-start.12 = (bf16[2,2,16,2048]{3,2,1,0:T(8,128)(2,1)S(1)}, bf16[2,2,16,2048]{3,2,1,0:T(8,128)(2,1)S(1)}, u32[]{:S(2)}, u32[]{:S(2)}) collective-permute-start(bf16[2,2,16,2048]{3,2,1,0:T(8,128)(2,1)S(1)} %pad_maximum_fusion.7), channel_id=1, source_target_pairs={{0,2},{1,3},{2,0},{3,1},{4,6},{5,7},{6,4},{7,5},{8,10},{9,11},{10,... | collective-permute-start | bytes 786440 | tf_op jit(solution)/shard_map/ppermute | solution.py:202
  34.8 2.8 %shard_map.114.weight_ref = bf16[2048,2048]{1,0:T(8,128)(2,1)S(1)} custom-call(bf16[2048,2048]{1,0:T(8,128)(2,1)S(1)} %shard_map.112.weight_ref), custom_call_target="tpu_custom_call" | custom-call | tf_op jit(solution)/shard_map/pallas_call | solution.py:181
  37.6 3.5 %collective-permute-done.13 = bf16[1,2,16,2048]{3,2,1,0:T(8,128)(2,1)S(1)} collective-permute-done((bf16[1,2,16,2048]{3,2,1,0:T(8,128)(2,1)S(1)}, bf16[1,2,16,2048]{3,2,1,0:T(8,128)(2,1)S(1)}, u32[]{:S(2)}, u32[]{:S(2)}) %collective-permute-start.13) | collective-permute-done | bytes 131104 | tf_op jit(solution)/shard_map/ppermute | solution.py:202
  41.1 1.5 %shard_map.115 = f32[128,2048]{1,0:T(8,128)S(1)} custom-call(bf16[128,2048]{1,0:T(8,128)(2,1)S(1)} %bitcast.92, bf16[2048,2048]{1,0:T(8,128)(2,1)S(1)} %shard_map.114.weight_ref), custom_call_target="tpu_custom_call" | custom-call | tf_op jit(solution)/shard_map/pallas_call | solution.py:80
  42.8 1.5 %shard_map.116 = f32[128,2048]{1,0:T(8,128)S(1)} custom-call(bf16[128,2048]{1,0:T(8,128)(2,1)S(1)} %bitcast.88, bf16[2048,2048]{1,0:T(8,128)(2,1)S(1)} %shard_map.111.weight_ref), custom_call_target="tpu_custom_call" | custom-call | tf_op jit(solution)/shard_map/pallas_call | solution.py:80
  47.8 1.5 %shard_map.119 = f32[128,2048]{1,0:T(8,128)S(1)} custom-call(bf16[128,2048]{1,0:T(8,128)(2,1)S(1)} %get-tuple-element.210.left_ref, bf16[2048,2048]{1,0:T(8,128)(2,1)S(1)} %shard_map.112.weight_ref), custom_call_target="tpu_custom_call" | custom-call | tf_op jit(solution)/shard_map/pallas_call | solution.py:80
  49.4 1.3 %collective-permute-start.18 = (bf16[2,2,16,2048]{3,2,1,0:T(8,128)(2,1)S(1)}, bf16[2,2,16,2048]{3,2,1,0:T(8,128)(2,1)S(1)}, u32[]{:S(2)}, u32[]{:S(2)}) collective-permute-start(bf16[2,2,16,2048]{3,2,1,0:T(8,128)(2,1)S(1)} %slice.130), channel_id=1, source_target_pairs={{0,1},{1,0},{2,3},{3,2},{4,5},{5,4},{6,7},{7,6},{8,9},{9,8},{10,11... | collective-permute-start | bytes 786440 | tf_op jit(solution)/shard_map/ppermute | solution.py:202
  50.7 2.8 %shard_map.118.weight_ref = bf16[2048,2048]{1,0:T(8,128)(2,1)S(1)} custom-call(bf16[2048,2048]{1,0:T(8,128)(2,1)S(1)} %shard_map.111.weight_ref), custom_call_target="tpu_custom_call" | custom-call | tf_op jit(solution)/shard_map/pallas_call | solution.py:181
  53.8 1.5 %shard_map.117 = f32[128,2048]{1,0:T(8,128)S(1)} custom-call(bf16[128,2048]{1,0:T(8,128)(2,1)S(1)} %bitcast.94, bf16[2048,2048]{1,0:T(8,128)(2,1)S(1)} %shard_map.114.weight_ref), custom_call_target="tpu_custom_call" | custom-call | tf_op jit(solution)/shard_map/pallas_call | solution.py:80
  55.3 3.6 %collective-permute-done.18 = bf16[2,2,16,2048]{3,2,1,0:T(8,128)(2,1)S(1)} collective-permute-done((bf16[2,2,16,2048]{3,2,1,0:T(8,128)(2,1)S(1)}, bf16[2,2,16,2048]{3,2,1,0:T(8,128)(2,1)S(1)}, u32[]{:S(2)}, u32[]{:S(2)}) %collective-permute-start.18) | collective-permute-done | bytes 262176 | tf_op jit(solution)/shard_map/ppermute | solution.py:202
  58.9 1.7 %collective-permute-done.15 = bf16[128,2048]{1,0:T(8,128)(2,1)S(1)} collective-permute-done((bf16[128,2048]{1,0:T(8,128)(2,1)S(1)}, bf16[128,2048]{1,0:T(8,128)(2,1)S(1)}, u32[]{:S(2)}, u32[]{:S(2)}) %collective-permute-start.15) | collective-permute-done | bytes 524320 | tf_op jit(solution)/shard_map/ppermute | solution.py:202
  63.6 1.5 %shard_map.120 = f32[128,2048]{1,0:T(8,128)S(1)} custom-call(bf16[128,2048]{1,0:T(8,128)(2,1)S(1)} %get-tuple-element.211.left_ref, bf16[2048,2048]{1,0:T(8,128)(2,1)S(1)} %shard_map.112.weight_ref), custom_call_target="tpu_custom_call" | custom-call | tf_op jit(solution)/shard_map/pallas_call | solution.py:80
  66.2 1.5 %shard_map.121 = f32[128,2048]{1,0:T(8,128)S(1)} custom-call(bf16[128,2048]{1,0:T(8,128)(2,1)S(1)} %multiply_convert_fusion.1.left_ref, bf16[2048,2048]{1,0:T(8,128)(2,1)S(1)} %shard_map.118.weight_ref), custom_call_target="tpu_custom_call" | custom-call | tf_op jit(solution)/shard_map/pallas_call | solution.py:80
  67.7 2.9 %collective-permute-done.20 = bf16[64,2048]{1,0:T(8,128)(2,1)S(1)} collective-permute-done((bf16[64,2048]{1,0:T(8,128)(2,1)S(1)}, bf16[64,2048]{1,0:T(8,128)(2,1)S(1)}, u32[]{:S(2)}, u32[]{:S(2)}) %collective-permute-start.20) | collective-permute-done | bytes 262176 | tf_op jit(solution)/shard_map/ppermute | solution.py:202
  70.6 3.3 %collective-permute-done.22 = bf16[2,2,16,2048]{3,2,1,0:T(8,128)(2,1)S(1)} collective-permute-done((bf16[2,2,16,2048]{3,2,1,0:T(8,128)(2,1)S(1)}, bf16[2,2,16,2048]{3,2,1,0:T(8,128)(2,1)S(1)}, u32[]{:S(2)}, u32[]{:S(2)}) %collective-permute-start.22) | collective-permute-done | bytes 262176 | tf_op jit(solution)/shard_map/ppermute | solution.py:202
  74.2 2.4 %collective-permute-start.26 = (bf16[2,2,16,2048]{3,2,1,0:T(8,128)(2,1)S(1)}, bf16[2,2,16,2048]{3,2,1,0:T(8,128)(2,1)S(1)}, u32[]{:S(2)}, u32[]{:S(2)}) collective-permute-start(bf16[2,2,16,2048]{3,2,1,0:T(8,128)(2,1)S(1)} %fusion.19), channel_id=1, source_target_pairs={{0,2},{1,3},{2,0},{3,1},{4,6},{5,7},{6,4},{7,5},{8,10},{9,11},{10,... | collective-permute-start | bytes 786440 | tf_op jit(solution)/shard_map/ppermute | solution.py:202
  76.9 1.5 %shard_map.122 = f32[128,2048]{1,0:T(8,128)S(1)} custom-call(bf16[128,2048]{1,0:T(8,128)(2,1)S(1)} %multiply_convert_fusion.left_ref, bf16[2048,2048]{1,0:T(8,128)(2,1)S(1)} %shard_map.118.weight_ref), custom_call_target="tpu_custom_call" | custom-call | tf_op jit(solution)/shard_map/pallas_call | solution.py:80
  78.6 0.8 collective-permute-start.25
  79.5 1.3 %collective-permute-start.24 = (f32[2048]{0:T(1024)S(1)}, f32[2048]{0:T(1024)S(1)}, u32[]{:S(2)}, u32[]{:S(2)}) collective-permute-start(f32[2048]{0:T(1024)S(1)} %add.141), channel_id=1, source_target_pairs={{0,1},{1,0},{2,3},{3,2},{4,5},{5,4},{6,7},{7,6},{8,9},{9,8},{10,11... | collective-permute-start | bytes 24584 | tf_op jit(solution)/shard_map/ppermute | solution.py:202
  81.0 5.8 %shard_map.123 = bf16[2048,2048]{1,0:T(8,128)(2,1)} custom-call(s32[8,8]{1,0:T(8,128)S(1)} %convert_element_type.158.mask_ref, bf16[256,2048]{1,0:T(8,128)(2,1)S(1)} %pad_maximum_fusion.left_ref, bf16[256,2048]{1,0:T(8,128)(2,1)S(1)} %pad_maximum_fusion.1.right_ref), custom_call_target="tpu_custom_call" | custom-call | tf_op jit(solution)/shard_map/pallas_call | solution.py:108
  87.2 1.0 collective-permute-start.27
  88.3 0.8 collective-permute-start.29
  89.2 1.8 %collective-permute-start.30 = (bf16[2,16,2048]{2,1,0:T(8,128)(2,1)S(1)}, bf16[2,16,2048]{2,1,0:T(8,128)(2,1)S(1)}, u32[]{:S(2)}, u32[]{:S(2)}) collective-permute-start(bf16[2,16,2048]{2,1,0:T(8,128)(2,1)S(1)} %fusion.22), channel_id=1, source_target_pairs={{0,4},{1,5},{2,6},{3,7},{4,0},{5,1},{6,2},{7,3},{8,12},{9,13},{10,... | collective-permute-start | bytes 393224 | tf_op jit(solution)/shard_map/ppermute | solution.py:202
  91.1 1.1 collective-permute-start.31
  92.3 1.2 %collective-permute-start.28 = (f32[2048]{0:T(1024)S(1)}, f32[2048]{0:T(1024)S(1)}, u32[]{:S(2)}, u32[]{:S(2)}) collective-permute-start(f32[2048]{0:T(1024)S(1)} %add.145), channel_id=1, source_target_pairs={{0,4},{1,5},{2,6},{3,7},{4,0},{5,1},{6,2},{7,3},{8,12},{9,13},{10,... | collective-permute-start | bytes 24584 | tf_op jit(solution)/shard_map/ppermute | solution.py:202
  93.7 5.6 %shard_map.124 = bf16[2048,2048]{1,0:T(8,128)(2,1)} custom-call(s32[8,8]{1,0:T(8,128)S(1)} %convert_element_type.157.mask_ref, bf16[256,2048]{1,0:T(8,128)(2,1)S(1)} %pad_maximum_fusion.2.left_ref, bf16[256,2048]{1,0:T(8,128)(2,1)S(1)} %pad_maximum_fusion.3.right_ref), custom_call_target="tpu_custom_call" | custom-call | tf_op jit(solution)/shard_map/pallas_call | solution.py:108
  99.3 0.9 collective-permute-done.31
  101.5 1.0 collective-permute-start.33
  102.6 1.1 collective-permute-start.35
  103.9 1.9 %collective-permute-start.37 = (bf16[8,4096]{1,0:T(8,128)(2,1)S(1)}, bf16[8,4096]{1,0:T(8,128)(2,1)S(1)}, u32[]{:S(2)}, u32[]{:S(2)}) collective-permute-start(bf16[8,4096]{1,0:T(8,128)(2,1)S(1)} %fusion.24), channel_id=1, source_target_pairs={{0,4},{1,5},{2,6},{3,7},{4,0},{5,1},{6,2},{7,3},{8,12},{9,13},{10,... | collective-permute-start | bytes 196616 | tf_op jit(solution)/shard_map/ppermute | solution.py:202
  105.8 1.6 %collective-permute-start.38 = (bf16[8,4096]{1,0:T(8,128)(2,1)S(1)}, bf16[8,4096]{1,0:T(8,128)(2,1)S(1)}, u32[]{:S(2)}, u32[]{:S(2)}) collective-permute-start(bf16[8,4096]{1,0:T(8,128)(2,1)S(1)} %get-tuple-element.281), channel_id=1, source_target_pairs={{0,20},{1,21},{2,22},{3,23},{4,16},{5,17},{6,18},{7,19},{8,28},{9,... | collective-permute-start | bytes 196616 | tf_op jit(solution)/shard_map/ppermute | solution.py:202
  107.4 1.1 collective-permute-start.39
  109.1 1.7 %collective-permute-done.37 = bf16[8,4096]{1,0:T(8,128)(2,1)S(1)} collective-permute-done((bf16[8,4096]{1,0:T(8,128)(2,1)S(1)}, bf16[8,4096]{1,0:T(8,128)(2,1)S(1)}, u32[]{:S(2)}, u32[]{:S(2)}) %collective-permute-start.37) | collective-permute-done | bytes 65568 | tf_op jit(solution)/shard_map/ppermute | solution.py:202
  110.8 2.3 %collective-permute-done.38 = bf16[8,4096]{1,0:T(8,128)(2,1)S(1)} collective-permute-done((bf16[8,4096]{1,0:T(8,128)(2,1)S(1)}, bf16[8,4096]{1,0:T(8,128)(2,1)S(1)}, u32[]{:S(2)}, u32[]{:S(2)}) %collective-permute-start.38) | collective-permute-done | bytes 65568 | tf_op jit(solution)/shard_map/ppermute | solution.py:202
  113.5 0.8 add_convert_fusion.3
  (160 shorter events, 17.7 us)
Async XLA Ops:
  0.6 14.7 %copy-start = (s32[32,32]{1,0:T(8,128)S(1)}, s32[32,32]{1,0:T(8,128)}, u32[]{:S(2)}) copy-start(s32[32,32]{1,0:T(8,128)} %param.12) | copy-start | bytes 12292
  2.0 13.4 %collective-permute-start.2 = (bf16[8,4096]{1,0:T(8,128)(2,1)S(1)}, bf16[8,4096]{1,0:T(8,128)(2,1)S(1)}, u32[]{:S(2)}, u32[]{:S(2)}) collective-permute-start(bf16[8,4096]{1,0:T(8,128)(2,1)S(1)} %get-tuple-element.132), channel_id=1, source_target_pairs={{0,20},{1,21},{2,22},{3,23},{4,16},{5,17},{6,18},{7,19},{8,28},{9,... | collective-permute-start | bytes 196616 | tf_op jit(solution)/shard_map/ppermute | solution.py:202
  7.0 8.5 %collective-permute-start = (bf16[8,4096]{1,0:T(8,128)(2,1)S(1)}, bf16[8,4096]{1,0:T(8,128)(2,1)S(1)}, u32[]{:S(2)}, u32[]{:S(2)}) collective-permute-start(bf16[8,4096]{1,0:T(8,128)(2,1)S(1)} %get-tuple-element.132), channel_id=1, source_target_pairs={{0,16},{8,24},{16,0},{24,8},{1,17},{9,25},{17,1},{25,9},{2,18},{10... | collective-permute-start | bytes 196616 | tf_op jit(solution)/shard_map/ppermute | solution.py:202
  8.4 7.0 %collective-permute-start.3 = (bf16[8,4096]{1,0:T(8,128)(2,1)S(1)}, bf16[8,4096]{1,0:T(8,128)(2,1)S(1)}, u32[]{:S(2)}, u32[]{:S(2)}) collective-permute-start(bf16[8,4096]{1,0:T(8,128)(2,1)S(1)} %get-tuple-element.292), channel_id=1, source_target_pairs={{0,16},{8,24},{16,0},{24,8},{1,17},{9,25},{17,1},{25,9},{2,18},{10... | collective-permute-start | bytes 196616 | tf_op jit(solution)/shard_map/ppermute | solution.py:202
  10.0 5.4 %collective-permute-start.1 = (bf16[8,4096]{1,0:T(8,128)(2,1)S(1)}, bf16[8,4096]{1,0:T(8,128)(2,1)S(1)}, u32[]{:S(2)}, u32[]{:S(2)}) collective-permute-start(bf16[8,4096]{1,0:T(8,128)(2,1)S(1)} %get-tuple-element.131), channel_id=1, source_target_pairs={{0,4},{1,5},{2,6},{3,7},{4,0},{5,1},{6,2},{7,3},{8,12},{9,13},{10,... | collective-permute-start | bytes 196616 | tf_op jit(solution)/shard_map/ppermute | solution.py:202
  15.6 1.5 %collective-permute-start.4 = (bf16[3,16,2048]{2,1,0:T(8,128)(2,1)S(1)}, bf16[3,16,2048]{2,1,0:T(8,128)(2,1)S(1)}, u32[]{:S(2)}, u32[]{:S(2)}) collective-permute-start(bf16[3,16,2048]{2,1,0:T(8,128)(2,1)S(1)} %pad_maximum_fusion.8), channel_id=1, source_target_pairs={{0,8},{8,0},{16,24},{24,16},{1,9},{9,1},{17,25},{25,17},{2,10},{10... | collective-permute-start | bytes 589832 | tf_op jit(solution)/shard_map/ppermute | solution.py:202
  17.3 9.4 %collective-permute-start.8 = (bf16[2,2,16,2048]{3,2,1,0:T(8,128)(2,1)S(1)}, bf16[2,2,16,2048]{3,2,1,0:T(8,128)(2,1)S(1)}, u32[]{:S(2)}, u32[]{:S(2)}) collective-permute-start(bf16[2,2,16,2048]{3,2,1,0:T(8,128)(2,1)S(1)} %constant_dynamic-update-slice_fusion), channel_id=1, source_target_pairs={{0,1},{1,0},{2,3},{3,2},{4,5},{5,4},{6,7},{7,6},{8,9},{9,8},{10,11... | collective-permute-start | bytes 786440 | tf_op jit(solution)/shard_map/ppermute | solution.py:202
  18.6 10.9 %collective-permute-start.6 = (bf16[2,2,16,2048]{3,2,1,0:T(8,128)(2,1)S(1)}, bf16[2,2,16,2048]{3,2,1,0:T(8,128)(2,1)S(1)}, u32[]{:S(2)}, u32[]{:S(2)}) collective-permute-start(bf16[2,2,16,2048]{3,2,1,0:T(8,128)(2,1)S(1)} %constant_dynamic-update-slice_fusion), channel_id=1, source_target_pairs={{0,2},{1,3},{2,0},{3,1},{4,6},{5,7},{6,4},{7,5},{8,10},{9,11},{10,... | collective-permute-start | bytes 786440 | tf_op jit(solution)/shard_map/ppermute | solution.py:202
  20.1 8.3 %collective-permute-start.5 = (bf16[1,2,16,2048]{3,2,1,0:T(8,128)(2,1)S(1)}, bf16[1,2,16,2048]{3,2,1,0:T(8,128)(2,1)S(1)}, u32[]{:S(2)}, u32[]{:S(2)}) collective-permute-start(bf16[1,2,16,2048]{3,2,1,0:T(8,128)(2,1)S(1)} %maximum_bitcast_fusion.6), channel_id=1, source_target_pairs={{0,1},{1,0},{2,3},{3,2},{4,5},{5,4},{6,7},{7,6},{8,9},{9,8},{10,11... | collective-permute-start | bytes 393224 | tf_op jit(solution)/shard_map/ppermute | solution.py:202
  20.9 7.7 %collective-permute-start.7 = (bf16[1,2,16,2048]{3,2,1,0:T(8,128)(2,1)S(1)}, bf16[1,2,16,2048]{3,2,1,0:T(8,128)(2,1)S(1)}, u32[]{:S(2)}, u32[]{:S(2)}) collective-permute-start(bf16[1,2,16,2048]{3,2,1,0:T(8,128)(2,1)S(1)} %maximum_bitcast_fusion.6), channel_id=1, source_target_pairs={{0,4},{1,5},{2,6},{3,7},{4,0},{5,1},{6,2},{7,3},{8,12},{9,13},{10,... | collective-permute-start | bytes 393224 | tf_op jit(solution)/shard_map/ppermute | solution.py:202
  29.5 2.1 %collective-permute-start.9 = (bf16[64,2048]{1,0:T(8,128)(2,1)S(1)}, bf16[64,2048]{1,0:T(8,128)(2,1)S(1)}, u32[]{:S(2)}, u32[]{:S(2)}) collective-permute-start(bf16[64,2048]{1,0:T(8,128)(2,1)S(1)} %slice.212), channel_id=1, source_target_pairs={{0,8},{8,0},{16,24},{24,16},{1,9},{9,1},{17,25},{25,17},{2,10},{10... | collective-permute-start | bytes 786440 | tf_op jit(solution)/shard_map/ppermute | solution.py:202
  29.5 13.2 %collective-permute-start.11 = (bf16[2,2,16,2048]{3,2,1,0:T(8,128)(2,1)S(1)}, bf16[2,2,16,2048]{3,2,1,0:T(8,128)(2,1)S(1)}, u32[]{:S(2)}, u32[]{:S(2)}) collective-permute-start(bf16[2,2,16,2048]{3,2,1,0:T(8,128)(2,1)S(1)} %collective-permute-done.6), channel_id=1, source_target_pairs={{0,1},{1,0},{2,3},{3,2},{4,5},{5,4},{6,7},{7,6},{8,9},{9,8},{10,11... | collective-permute-start | bytes 786440 | tf_op jit(solution)/shard_map/ppermute | solution.py:202
  30.2 10.8 %collective-permute-start.13 = (bf16[1,2,16,2048]{3,2,1,0:T(8,128)(2,1)S(1)}, bf16[1,2,16,2048]{3,2,1,0:T(8,128)(2,1)S(1)}, u32[]{:S(2)}, u32[]{:S(2)}) collective-permute-start(bf16[1,2,16,2048]{3,2,1,0:T(8,128)(2,1)S(1)} %collective-permute-done.7), channel_id=1, source_target_pairs={{0,1},{1,0},{2,3},{3,2},{4,5},{5,4},{6,7},{7,6},{8,9},{9,8},{10,11... | collective-permute-start | bytes 393224 | tf_op jit(solution)/shard_map/ppermute | solution.py:202
  31.6 11.0 %collective-permute-start.10 = (bf16[64,2048]{1,0:T(8,128)(2,1)S(1)}, bf16[64,2048]{1,0:T(8,128)(2,1)S(1)}, u32[]{:S(2)}, u32[]{:S(2)}) collective-permute-start(bf16[64,2048]{1,0:T(8,128)(2,1)S(1)} %get-tuple-element.263), channel_id=1, source_target_pairs={{0,16},{8,24},{16,0},{24,8},{1,17},{9,25},{17,1},{25,9},{2,18},{10... | collective-permute-start | bytes 786440 | tf_op jit(solution)/shard_map/ppermute | solution.py:202
  32.2 10.5 %collective-permute-start.12 = (bf16[2,2,16,2048]{3,2,1,0:T(8,128)(2,1)S(1)}, bf16[2,2,16,2048]{3,2,1,0:T(8,128)(2,1)S(1)}, u32[]{:S(2)}, u32[]{:S(2)}) collective-permute-start(bf16[2,2,16,2048]{3,2,1,0:T(8,128)(2,1)S(1)} %pad_maximum_fusion.7), channel_id=1, source_target_pairs={{0,2},{1,3},{2,0},{3,1},{4,6},{5,7},{6,4},{7,5},{8,10},{9,11},{10,... | collective-permute-start | bytes 786440 | tf_op jit(solution)/shard_map/ppermute | solution.py:202
  42.6 1.8 %copy-start.2 = (f32[128,2048]{1,0:T(8,128)}, f32[128,2048]{1,0:T(8,128)S(1)}, u32[]{:S(2)}) copy-start(f32[128,2048]{1,0:T(8,128)S(1)} %shard_map.115) | copy-start | bytes 3145732
  44.4 2.0 %collective-permute-start.14 = (bf16[128,2048]{1,0:T(8,128)(2,1)S(1)}, bf16[128,2048]{1,0:T(8,128)(2,1)S(1)}, u32[]{:S(2)}, u32[]{:S(2)}) collective-permute-start(bf16[128,2048]{1,0:T(8,128)(2,1)S(1)} %pad_maximum_fusion.4), channel_id=1, source_target_pairs={{0,8},{8,0},{16,24},{24,16},{1,9},{9,1},{17,25},{25,17},{2,10},{10... | collective-permute-start | bytes 1572872 | tf_op jit(solution)/shard_map/ppermute | solution.py:202
  44.5 1.9 %slice-start = ((f32[128,2048]{1,0:T(8,128)}), f32[64,2048]{1,0:T(8,128)S(1)}, s32[]{:S(2)}) async-start(f32[128,2048]{1,0:T(8,128)} %copy-done.2), calls=%async_computation | async-start | bytes 1048576 | tf_op jit(solution)/shard_map/slice | solution.py:311
  44.5 9.2 %collective-permute-start.16 = (bf16[2,2,16,2048]{3,2,1,0:T(8,128)(2,1)S(1)}, bf16[2,2,16,2048]{3,2,1,0:T(8,128)(2,1)S(1)}, u32[]{:S(2)}, u32[]{:S(2)}) collective-permute-start(bf16[2,2,16,2048]{3,2,1,0:T(8,128)(2,1)S(1)} %collective-permute-done.12), channel_id=1, source_target_pairs={{0,1},{1,0},{2,3},{3,2},{4,5},{5,4},{6,7},{7,6},{8,9},{9,8},{10,11... | collective-permute-start | bytes 786440 | tf_op jit(solution)/shard_map/ppermute | solution.py:202
  45.4 1.7 %collective-permute-start.17 = (bf16[64,2048]{1,0:T(8,128)(2,1)S(1)}, bf16[64,2048]{1,0:T(8,128)(2,1)S(1)}, u32[]{:S(2)}, u32[]{:S(2)}) collective-permute-start(bf16[64,2048]{1,0:T(8,128)(2,1)S(1)} %add_convert_fusion.2), channel_id=1, source_target_pairs={{0,8},{8,0},{16,24},{24,16},{1,9},{9,1},{17,25},{25,17},{2,10},{10... | collective-permute-start | bytes 786440 | tf_op jit(solution)/shard_map/ppermute | solution.py:202
  46.5 14.0 %collective-permute-start.15 = (bf16[128,2048]{1,0:T(8,128)(2,1)S(1)}, bf16[128,2048]{1,0:T(8,128)(2,1)S(1)}, u32[]{:S(2)}, u32[]{:S(2)}) collective-permute-start(bf16[128,2048]{1,0:T(8,128)(2,1)S(1)} %get-tuple-element.261), channel_id=1, source_target_pairs={{0,16},{8,24},{16,0},{24,8},{1,17},{9,25},{17,1},{25,9},{2,18},{10... | collective-permute-start | bytes 1572872 | tf_op jit(solution)/shard_map/ppermute | solution.py:202
  49.4 9.5 %collective-permute-start.18 = (bf16[2,2,16,2048]{3,2,1,0:T(8,128)(2,1)S(1)}, bf16[2,2,16,2048]{3,2,1,0:T(8,128)(2,1)S(1)}, u32[]{:S(2)}, u32[]{:S(2)}) collective-permute-start(bf16[2,2,16,2048]{3,2,1,0:T(8,128)(2,1)S(1)} %slice.130), channel_id=1, source_target_pairs={{0,1},{1,0},{2,3},{3,2},{4,5},{5,4},{6,7},{7,6},{8,9},{9,8},{10,11... | collective-permute-start | bytes 786440 | tf_op jit(solution)/shard_map/ppermute | solution.py:202
  60.6 1.5 %collective-permute-start.19 = (bf16[64,2048]{1,0:T(8,128)(2,1)S(1)}, bf16[64,2048]{1,0:T(8,128)(2,1)S(1)}, u32[]{:S(2)}, u32[]{:S(2)}) collective-permute-start(bf16[64,2048]{1,0:T(8,128)(2,1)S(1)} %slice.209), channel_id=1, source_target_pairs={{0,8},{8,0},{16,24},{24,16},{1,9},{9,1},{17,25},{25,17},{2,10},{10... | collective-permute-start | bytes 786440 | tf_op jit(solution)/shard_map/ppermute | solution.py:202
  60.7 2.2 %collective-permute-start.21 = (bf16[128,2048]{1,0:T(8,128)(2,1)S(1)}, bf16[128,2048]{1,0:T(8,128)(2,1)S(1)}, u32[]{:S(2)}, u32[]{:S(2)}) collective-permute-start(bf16[128,2048]{1,0:T(8,128)(2,1)S(1)} %add_convert_fusion), channel_id=1, source_target_pairs={{0,8},{8,0},{16,24},{24,16},{1,9},{9,1},{17,25},{25,17},{2,10},{10... | collective-permute-start | bytes 1572872 | tf_op jit(solution)/shard_map/ppermute | solution.py:202
  62.2 8.4 %collective-permute-start.20 = (bf16[64,2048]{1,0:T(8,128)(2,1)S(1)}, bf16[64,2048]{1,0:T(8,128)(2,1)S(1)}, u32[]{:S(2)}, u32[]{:S(2)}) collective-permute-start(bf16[64,2048]{1,0:T(8,128)(2,1)S(1)} %get-tuple-element.259), channel_id=1, source_target_pairs={{0,16},{8,24},{16,0},{24,8},{1,17},{9,25},{17,1},{25,9},{2,18},{10... | collective-permute-start | bytes 786440 | tf_op jit(solution)/shard_map/ppermute | solution.py:202
  65.3 8.6 %collective-permute-start.22 = (bf16[2,2,16,2048]{3,2,1,0:T(8,128)(2,1)S(1)}, bf16[2,2,16,2048]{3,2,1,0:T(8,128)(2,1)S(1)}, u32[]{:S(2)}, u32[]{:S(2)}) collective-permute-start(bf16[2,2,16,2048]{3,2,1,0:T(8,128)(2,1)S(1)} %slice.165), channel_id=1, source_target_pairs={{0,1},{1,0},{2,3},{3,2},{4,5},{5,4},{6,7},{7,6},{8,9},{9,8},{10,11... | collective-permute-start | bytes 786440 | tf_op jit(solution)/shard_map/ppermute | solution.py:202
  73.9 2.8 %collective-permute-start.23 = (bf16[64,2048]{1,0:T(8,128)(2,1)S(1)}, bf16[64,2048]{1,0:T(8,128)(2,1)S(1)}, u32[]{:S(2)}, u32[]{:S(2)}) collective-permute-start(bf16[64,2048]{1,0:T(8,128)(2,1)S(1)} %add_convert_fusion.1), channel_id=1, source_target_pairs={{0,8},{8,0},{16,24},{24,16},{1,9},{9,1},{17,25},{25,17},{2,10},{10... | collective-permute-start | bytes 786440 | tf_op jit(solution)/shard_map/ppermute | solution.py:202
  74.2 12.5 %collective-permute-start.26 = (bf16[2,2,16,2048]{3,2,1,0:T(8,128)(2,1)S(1)}, bf16[2,2,16,2048]{3,2,1,0:T(8,128)(2,1)S(1)}, u32[]{:S(2)}, u32[]{:S(2)}) collective-permute-start(bf16[2,2,16,2048]{3,2,1,0:T(8,128)(2,1)S(1)} %fusion.19), channel_id=1, source_target_pairs={{0,2},{1,3},{2,0},{3,1},{4,6},{5,7},{6,4},{7,5},{8,10},{9,11},{10,... | collective-permute-start | bytes 786440 | tf_op jit(solution)/shard_map/ppermute | solution.py:202
  78.6 8.7 %collective-permute-start.25 = (bf16[2,2,16,2048]{3,2,0,1:T(8,128)(2,1)S(1)}, bf16[2,2,16,2048]{3,2,0,1:T(8,128)(2,1)S(1)}, u32[]{:S(2)}, u32[]{:S(2)}) collective-permute-start(bf16[2,2,16,2048]{3,2,0,1:T(8,128)(2,1)S(1)} %slice.168), channel_id=1, source_target_pairs={{0,1},{1,0},{2,3},{3,2},{4,5},{5,4},{6,7},{7,6},{8,9},{9,8},{10,11... | collective-permute-start | bytes 786440 | tf_op jit(solution)/shard_map/ppermute | solution.py:202
  79.5 7.7 %collective-permute-start.24 = (f32[2048]{0:T(1024)S(1)}, f32[2048]{0:T(1024)S(1)}, u32[]{:S(2)}, u32[]{:S(2)}) collective-permute-start(f32[2048]{0:T(1024)S(1)} %add.141), channel_id=1, source_target_pairs={{0,1},{1,0},{2,3},{3,2},{4,5},{5,4},{6,7},{7,6},{8,9},{9,8},{10,11... | collective-permute-start | bytes 24584 | tf_op jit(solution)/shard_map/ppermute | solution.py:202
  87.2 5.1 %collective-permute-start.27 = (f32[2048]{0:T(1024)S(1)}, f32[2048]{0:T(1024)S(1)}, u32[]{:S(2)}, u32[]{:S(2)}) collective-permute-start(f32[2048]{0:T(1024)S(1)} %add.144), channel_id=1, source_target_pairs={{0,2},{1,3},{2,0},{3,1},{4,6},{5,7},{6,4},{7,5},{8,10},{9,11},{10,... | collective-permute-start | bytes 24584 | tf_op jit(solution)/shard_map/ppermute | solution.py:202
  88.3 11.0 %collective-permute-start.29 = (bf16[2,2,16,2048]{3,2,0,1:T(8,128)(2,1)S(1)}, bf16[2,2,16,2048]{3,2,0,1:T(8,128)(2,1)S(1)}, u32[]{:S(2)}, u32[]{:S(2)}) collective-permute-start(bf16[2,2,16,2048]{3,2,0,1:T(8,128)(2,1)S(1)} %slice.140), channel_id=1, source_target_pairs={{0,1},{1,0},{2,3},{3,2},{4,5},{5,4},{6,7},{7,6},{8,9},{9,8},{10,11... | collective-permute-start | bytes 786440 | tf_op jit(solution)/shard_map/ppermute | solution.py:202
  89.2 10.1 %collective-permute-start.30 = (bf16[2,16,2048]{2,1,0:T(8,128)(2,1)S(1)}, bf16[2,16,2048]{2,1,0:T(8,128)(2,1)S(1)}, u32[]{:S(2)}, u32[]{:S(2)}) collective-permute-start(bf16[2,16,2048]{2,1,0:T(8,128)(2,1)S(1)} %fusion.22), channel_id=1, source_target_pairs={{0,4},{1,5},{2,6},{3,7},{4,0},{5,1},{6,2},{7,3},{8,12},{9,13},{10,... | collective-permute-start | bytes 393224 | tf_op jit(solution)/shard_map/ppermute | solution.py:202
  91.1 9.1 %collective-permute-start.31 = (bf16[2,2,16,2048]{3,2,0,1:T(8,128)(2,1)S(1)}, bf16[2,2,16,2048]{3,2,0,1:T(8,128)(2,1)S(1)}, u32[]{:S(2)}, u32[]{:S(2)}) collective-permute-start(bf16[2,2,16,2048]{3,2,0,1:T(8,128)(2,1)S(1)} %fusion.18), channel_id=1, source_target_pairs={{0,2},{1,3},{2,0},{3,1},{4,6},{5,7},{6,4},{7,5},{8,10},{9,11},{10,... | collective-permute-start | bytes 786440 | tf_op jit(solution)/shard_map/ppermute | solution.py:202
  92.3 6.9 %collective-permute-start.28 = (f32[2048]{0:T(1024)S(1)}, f32[2048]{0:T(1024)S(1)}, u32[]{:S(2)}, u32[]{:S(2)}) collective-permute-start(f32[2048]{0:T(1024)S(1)} %add.145), channel_id=1, source_target_pairs={{0,4},{1,5},{2,6},{3,7},{4,0},{5,1},{6,2},{7,3},{8,12},{9,13},{10,... | collective-permute-start | bytes 24584 | tf_op jit(solution)/shard_map/ppermute | solution.py:202
  100.3 8.1 %copy-start.4 = (f32[8192]{0:T(1024)S(1)}, f32[8192]{0:T(1024)}, u32[]{:S(2)}) copy-start(f32[8192]{0:T(1024)} %param.8) | copy-start | bytes 98308
  100.3 1.2 %collective-permute-start.32 = (f32[2048]{0:T(1024)S(1)}, f32[2048]{0:T(1024)S(1)}, u32[]{:S(2)}, u32[]{:S(2)}) collective-permute-start(f32[2048]{0:T(1024)S(1)} %add.148), channel_id=1, source_target_pairs={{0,8},{8,0},{16,24},{24,16},{1,9},{9,1},{17,25},{25,17},{2,10},{10... | collective-permute-start | bytes 24584 | tf_op jit(solution)/shard_map/ppermute | solution.py:202
  100.4 2.1 %collective-permute-start.34 = (bf16[16,2048]{1,0:T(8,128)(2,1)S(1)}, bf16[16,2048]{1,0:T(8,128)(2,1)S(1)}, u32[]{:S(2)}, u32[]{:S(2)}) collective-permute-start(bf16[16,2048]{1,0:T(8,128)(2,1)S(1)} %get-tuple-element.284), channel_id=1, source_target_pairs={{0,8},{8,0},{16,24},{24,16},{1,9},{9,1},{17,25},{25,17},{2,10},{10... | collective-permute-start | bytes 196616 | tf_op jit(solution)/shard_map/ppermute | solution.py:202
  101.0 2.7 %collective-permute-start.36 = (bf16[2,16,2048]{2,1,0:T(8,128)(2,1)S(1)}, bf16[2,16,2048]{2,1,0:T(8,128)(2,1)S(1)}, u32[]{:S(2)}, u32[]{:S(2)}) collective-permute-start(bf16[2,16,2048]{2,1,0:T(8,128)(2,1)S(1)} %fusion.23), channel_id=1, source_target_pairs={{0,8},{8,0},{16,24},{24,16},{1,9},{9,1},{17,25},{25,17},{2,10},{10... | collective-permute-start | bytes 393224 | tf_op jit(solution)/shard_map/ppermute | solution.py:202
  101.5 6.9 %collective-permute-start.33 = (f32[4096]{0:T(1024)S(1)}, f32[4096]{0:T(1024)S(1)}, u32[]{:S(2)}, u32[]{:S(2)}) collective-permute-start(f32[4096]{0:T(1024)S(1)} %maximum_select_fusion.8), channel_id=1, source_target_pairs={{0,16},{8,24},{16,0},{24,8},{1,17},{9,25},{17,1},{25,9},{2,18},{10... | collective-permute-start | bytes 49160 | tf_op jit(solution)/shard_map/ppermute | solution.py:202
  102.6 10.9 %copy-start.3 = (bf16[8,8192]{1,0:T(8,128)(2,1)S(1)}, bf16[8,8192]{1,0:T(8,128)(2,1)}, u32[]{:S(2)}) copy-start(bf16[8,8192]{1,0:T(8,128)(2,1)} %input_hbm.1) | copy-start | bytes 393220
  102.6 10.9 %copy-start.5 = (bf16[8,8192]{1,0:T(8,128)(2,1)S(1)}, bf16[8,8192]{1,0:T(8,128)(2,1)}, u32[]{:S(2)}) copy-start(bf16[8,8192]{1,0:T(8,128)(2,1)} %param.13) | copy-start | bytes 393220
  102.6 6.5 %collective-permute-start.35 = (bf16[8,4096]{1,0:T(8,128)(2,1)S(1)}, bf16[8,4096]{1,0:T(8,128)(2,1)S(1)}, u32[]{:S(2)}, u32[]{:S(2)}) collective-permute-start(bf16[8,4096]{1,0:T(8,128)(2,1)S(1)} %get-tuple-element.282), channel_id=1, source_target_pairs={{0,16},{8,24},{16,0},{24,8},{1,17},{9,25},{17,1},{25,9},{2,18},{10... | collective-permute-start | bytes 196616 | tf_op jit(solution)/shard_map/ppermute | solution.py:202
  103.8 10.6 %copy-start.1 = (s32[32,32]{1,0:T(8,128)S(1)}, s32[32,32]{1,0:T(8,128)}, u32[]{:S(2)}) copy-start(s32[32,32]{1,0:T(8,128)} %param.12) | copy-start | bytes 12292
  103.9 6.9 %collective-permute-start.37 = (bf16[8,4096]{1,0:T(8,128)(2,1)S(1)}, bf16[8,4096]{1,0:T(8,128)(2,1)S(1)}, u32[]{:S(2)}, u32[]{:S(2)}) collective-permute-start(bf16[8,4096]{1,0:T(8,128)(2,1)S(1)} %fusion.24), channel_id=1, source_target_pairs={{0,4},{1,5},{2,6},{3,7},{4,0},{5,1},{6,2},{7,3},{8,12},{9,13},{10,... | collective-permute-start | bytes 196616 | tf_op jit(solution)/shard_map/ppermute | solution.py:202
  105.8 7.3 %collective-permute-start.38 = (bf16[8,4096]{1,0:T(8,128)(2,1)S(1)}, bf16[8,4096]{1,0:T(8,128)(2,1)S(1)}, u32[]{:S(2)}, u32[]{:S(2)}) collective-permute-start(bf16[8,4096]{1,0:T(8,128)(2,1)S(1)} %get-tuple-element.281), channel_id=1, source_target_pairs={{0,20},{1,21},{2,22},{3,23},{4,16},{5,17},{6,18},{7,19},{8,28},{9,... | collective-permute-start | bytes 196616 | tf_op jit(solution)/shard_map/ppermute | solution.py:202
  107.4 5.7 %collective-permute-start.39 = (bf16[8,4096]{1,0:T(8,128)(2,1)S(1)}, bf16[8,4096]{1,0:T(8,128)(2,1)S(1)}, u32[]{:S(2)}, u32[]{:S(2)}) collective-permute-start(bf16[8,4096]{1,0:T(8,128)(2,1)S(1)} %get-tuple-element.280), channel_id=1, source_target_pairs={{0,16},{8,24},{16,0},{24,8},{1,17},{9,25},{17,1},{25,9},{2,18},{10... | collective-permute-start | bytes 196616 | tf_op jit(solution)/shard_map/ppermute | solution.py:202

commit v4 on v3

--- a/solution.py
+++ b/solution.py
@@ -219,12 +219,15 @@
     def __init__(self, staged):
         self.staged = staged
         self.tasks = []
+        self.first = set()
 
     def work(self, stage, function, *deps):
         self.tasks.append((stage if self.staged else 0, function, deps))
         return len(self.tasks) - 1
 
-    def swap(self, stage, axis, distance, dep):
+    def swap(self, stage, axis, distance, dep, urgent=False):
+        if urgent:
+            self.first.add(len(self.tasks))
         return self.work(stage, functools.partial(swap, axis=axis, distance=distance), dep)
 
     def run(self, results):
@@ -234,7 +237,8 @@
                 if when == stage:
                     values[task] = function(*(values[d] for d in deps))
             wanted = {d for when, _, deps in self.tasks if when > stage for d in deps}
-            live = sorted((wanted | set(results)) & set(values))
+            live = (wanted | set(results)) & set(values)
+            live = sorted(live, key=lambda t: (t not in self.first, t))
             values.update(zip(live, lax.optimization_barrier(tuple(values[n] for n in live))))
         return tuple(values[n] for n in results)
 
@@ -364,6 +368,7 @@
     out_t = work(3, turn, out_e)
     gc = [work(3, chunk, gown, gfirst, gline[0], gnear[0])]
     gp = [work(3, product, gc[0], out_t)]
+    plan.first |= {gc[0], gp[0]}
     gnear.append(swapped(4, "col", 1, gline[-1]))
     d_act = []
     for i in range(1, last):
@@ -415,8 +420,9 @@
         return sum(jnp.sum(n * x.astype(F32), axis=0) for n, x in zip(left, right))
 
     gain = work(6, gain_terms, *np_, *xc)
-    for b, distance in enumerate([1] + line[::-1]):
-        gain = work(7 if b < last else 8, add, gain, swapped(min(6 + b, 7), "col", distance, gain))
+    for distance in [1] + line[:0:-1]:
+        gain = work(6, add, gain, swapped(6, "col", distance, gain))
+    gain = work(8, add, gain, swapped(7, "col", line[0], gain))
     got = swapped(8, "row", 1, gain)
     gain = work(8, lambda v, got: ordered(v, got, core_bit, 0), gain, got)
     got = swapped(8, "row", 2, gain)
@@ -427,7 +433,7 @@
     nnear = [
         swapped(7, "col", 1, work(7, functools.partial(give_near, i), np_[i]))
         for i in range(last - 1)
-    ] + [swapped(4 + last, "col", 1, last_give)]
+    ] + [swapped(4 + last, "col", 1, last_give, True)]
 
     def line_sum(stage, products, got, late):
         sums, gives = [
@@ -442,7 +448,7 @@
         for i in reversed(range(1, last)):
             when = stage + last - 1 - i
             gives.append(work(when, to_bf16, sums[i]))
-            moved = swapped(when, "col", line[i], gives[-1])
+            moved = swapped(when, "col", line[i], gives[-1], late)
             for m in range(i):
                 start = sum(places[:m])
                 sums[m] = work(
@@ -493,7 +499,7 @@
         left, right = parts[:last], parts[last:]
         return outer(jnp.concatenate(left), jnp.concatenate(right), behind(mask, before))
 
-    grad_w_out = work(4 + last, weight_gradient, mask_out, last_give, *act, *gc)
+    grad_w_out = work(5, weight_gradient, mask_out, ygive[-1], *act, *gc)
     grad_w_in = work(7, weight_gradient, mask_in, last_sent, *xc, *d_pre)
 
     return plan.run((output, grad_inputs, grad_w_in, grad_w_out, gain_gradient))

time: 115 us -> 113 us (0.983)
  waiting for transfers between devices: 24.8 us -> 21.6 us
  starting transfers between devices: 41.5 us -> 43.3 us
    ppermute x40, waiting for transfers between devices: 24.8 us -> 21.6 us  [swap(): return lax.ppermute(value, axis, [(i, i ^ distance) for i in range(size)])]
    ppermute x40, starting transfers between devices: 41.5 us -> 43.3 us  [swap(): return lax.ppermute(value, axis, [(i, i ^ distance) for i in range(size)])]
  transfers between devices with their start and end apart: 40 -> 40, of which waited for: 18 -> 14; matrix products, arithmetic and copies ran while one was open for 6% -> 6% of each run, Pallas kernels for 30% -> 29%
where the time goes in v4:
time: 113 us
  starting transfers between devices  43.3 us (38%)
  Pallas kernels  37.4 us (33%)
  waiting for transfers between devices  21.6 us (19%)
  other arithmetic  7.33 us (6%)
  local copies, waits for them, and re-layouts  1.75 us (2%)
  between operations  1.57 us (1%)
    ppermute x40, starting transfers between devices, swap(): return lax.ppermute(value, axis, [(i, i ^ distance) for i in range(size)])  43.3 us
    ppermute x40, waiting for transfers between devices, swap(): return lax.ppermute(value, axis, [(i, i ^ distance) for i in range(size)])  21.6 us
    pallas_call x8, Pallas kernels, product(): pl.pallas_call(product_kernel, out_shape=jax.ShapeDtypeStruct((left.shape...  12 us
    pallas_call x2, Pallas kernels, outer(): pl.pallas_call(outer_kernel, grid=(rows // step,), out_shape=jax.ShapeDty...  11.2 us
    pallas_call x2, Pallas kernels, keep(): pl.pallas_call(keep_kernel, out_shape=pltpu.VMEM(weight.shape, weight.dty...  7.4 us
    pallas_call x2, Pallas kernels, turn(): pl.pallas_call(turn_kernel, out_shape=pltpu.VMEM(weight.shape[::-1], weig...  5.53 us
  transfers between devices with their start and end apart: 40, of which 14 were waited for; matrix products, arithmetic and copies ran while one was open for 6% of the time, Pallas kernels for 29%

profile of v4, /device:TPU:0, one launch (start us, length us, event | category | flops | bytes accessed | tf_op | source)
XLA Modules:
  0.0 113.0 jit_solution(12146731094493083681)
XLA Ops:
  0.7 1.3 %shard_map.110 = (bf16[8,4096]{1,0:T(8,128)(2,1)S(1)}, bf16[8,4096]{1,0:T(8,128)(2,1)S(1)}, f32[8,8192]{1,0:T(8,128)S(1)}, f32[8,1]{1,0:T(8,128)S(1)}) custom-call(s32[1]{0:T(128)} %bitcast.far_ref, bf16[8,8192]{1,0:T(8,128)(2,1)} %input_hbm.1, f32[1,8192]{1,0:T(1,128)} %bitcast.104), custom_call_target="tpu_custom_call" | custom-call | tf_op jit(solution)/shard_map/pallas_call | solution.py:151
  2.0 5.1 %collective-permute-start.2 = (bf16[8,4096]{1,0:T(8,128)(2,1)S(1)}, bf16[8,4096]{1,0:T(8,128)(2,1)S(1)}, u32[]{:S(2)}, u32[]{:S(2)}) collective-permute-start(bf16[8,4096]{1,0:T(8,128)(2,1)S(1)} %get-tuple-element.127), channel_id=1, source_target_pairs={{0,20},{1,21},{2,22},{3,23},{4,16},{5,17},{6,18},{7,19},{8,28},{9,... | collective-permute-start | bytes 196616 | tf_op jit(solution)/shard_map/ppermute | solution.py:202
  7.5 0.9 broadcast_select_fusion.3
  8.4 1.6 %collective-permute-start.3 = (bf16[8,4096]{1,0:T(8,128)(2,1)S(1)}, bf16[8,4096]{1,0:T(8,128)(2,1)S(1)}, u32[]{:S(2)}, u32[]{:S(2)}) collective-permute-start(bf16[8,4096]{1,0:T(8,128)(2,1)S(1)} %get-tuple-element.282), channel_id=1, source_target_pairs={{0,16},{8,24},{16,0},{24,8},{1,17},{9,25},{17,1},{25,9},{2,18},{10... | collective-permute-start | bytes 196616 | tf_op jit(solution)/shard_map/ppermute | solution.py:202
  11.5 3.8 %shard_map.111.weight_ref = bf16[2048,2048]{1,0:T(8,128)(2,1)S(1)} custom-call(s32[8,8]{1,0:T(8,128)S(1)} %convert_element_type.157.mask_ref, bf16[2048,2048]{1,0:T(8,128)(2,1)} %weight_ref.2), custom_call_target="tpu_custom_call" | custom-call | tf_op jit(solution)/shard_map/pallas_call | solution.py:56
  16.0 1.1 collective-permute-done.4
  17.2 1.4 %collective-permute-start.8 = (bf16[2,2,16,2048]{3,2,1,0:T(8,128)(2,1)S(1)}, bf16[2,2,16,2048]{3,2,1,0:T(8,128)(2,1)S(1)}, u32[]{:S(2)}, u32[]{:S(2)}) collective-permute-start(bf16[2,2,16,2048]{3,2,1,0:T(8,128)(2,1)S(1)} %constant_dynamic-update-slice_fusion), channel_id=1, source_target_pairs={{0,1},{1,0},{2,3},{3,2},{4,5},{5,4},{6,7},{7,6},{8,9},{9,8},{10,11... | collective-permute-start | bytes 786440 | tf_op jit(solution)/shard_map/ppermute | solution.py:202
  18.6 1.7 %collective-permute-start.6 = (bf16[2,2,16,2048]{3,2,1,0:T(8,128)(2,1)S(1)}, bf16[2,2,16,2048]{3,2,1,0:T(8,128)(2,1)S(1)}, u32[]{:S(2)}, u32[]{:S(2)}) collective-permute-start(bf16[2,2,16,2048]{3,2,1,0:T(8,128)(2,1)S(1)} %constant_dynamic-update-slice_fusion), channel_id=1, source_target_pairs={{0,2},{1,3},{2,0},{3,1},{4,6},{5,7},{6,4},{7,5},{8,10},{9,11},{10,... | collective-permute-start | bytes 786440 | tf_op jit(solution)/shard_map/ppermute | solution.py:202
  20.7 2.8 %collective-permute-start.7 = (bf16[1,2,16,2048]{3,2,1,0:T(8,128)(2,1)S(1)}, bf16[1,2,16,2048]{3,2,1,0:T(8,128)(2,1)S(1)}, u32[]{:S(2)}, u32[]{:S(2)}) collective-permute-start(bf16[1,2,16,2048]{3,2,1,0:T(8,128)(2,1)S(1)} %maximum_bitcast_fusion.6), channel_id=1, source_target_pairs={{0,4},{1,5},{2,6},{3,7},{4,0},{5,1},{6,2},{7,3},{8,12},{9,13},{10,... | collective-permute-start | bytes 393224 | tf_op jit(solution)/shard_map/ppermute | solution.py:202
  23.5 3.6 %shard_map.112.weight_ref = bf16[2048,2048]{1,0:T(8,128)(2,1)S(1)} custom-call(s32[8,8]{1,0:T(8,128)S(1)} %convert_element_type.158.mask_ref, bf16[2048,2048]{1,0:T(8,128)(2,1)} %weight_ref.3), custom_call_target="tpu_custom_call" | custom-call | tf_op jit(solution)/shard_map/pallas_call | solution.py:56
  27.3 1.5 %shard_map.113 = f32[128,2048]{1,0:T(8,128)S(1)} custom-call(bf16[128,2048]{1,0:T(8,128)(2,1)S(1)} %bitcast.85, bf16[2048,2048]{1,0:T(8,128)(2,1)S(1)} %shard_map.111.weight_ref), custom_call_target="tpu_custom_call" | custom-call | tf_op jit(solution)/shard_map/pallas_call | solution.py:80
  29.4 1.0 collective-permute-start.9
  30.4 1.1 collective-permute-start.12
  32.2 2.4 %collective-permute-start.13 = (bf16[2,2,16,2048]{3,2,1,0:T(8,128)(2,1)S(1)}, bf16[2,2,16,2048]{3,2,1,0:T(8,128)(2,1)S(1)}, u32[]{:S(2)}, u32[]{:S(2)}) collective-permute-start(bf16[2,2,16,2048]{3,2,1,0:T(8,128)(2,1)S(1)} %pad_maximum_fusion.7), channel_id=1, source_target_pairs={{0,2},{1,3},{2,0},{3,1},{4,6},{5,7},{6,4},{7,5},{8,10},{9,11},{10,... | collective-permute-start | bytes 786440 | tf_op jit(solution)/shard_map/ppermute | solution.py:202
  34.5 2.8 %shard_map.114.weight_ref = bf16[2048,2048]{1,0:T(8,128)(2,1)S(1)} custom-call(bf16[2048,2048]{1,0:T(8,128)(2,1)S(1)} %shard_map.112.weight_ref), custom_call_target="tpu_custom_call" | custom-call | tf_op jit(solution)/shard_map/pallas_call | solution.py:181
  37.4 1.5 %shard_map.115 = f32[128,2048]{1,0:T(8,128)S(1)} custom-call(bf16[128,2048]{1,0:T(8,128)(2,1)S(1)} %bitcast.92, bf16[2048,2048]{1,0:T(8,128)(2,1)S(1)} %shard_map.114.weight_ref), custom_call_target="tpu_custom_call" | custom-call | tf_op jit(solution)/shard_map/pallas_call | solution.py:80
  38.9 2.0 %collective-permute-done.12 = bf16[2,2,16,2048]{3,2,1,0:T(8,128)(2,1)S(1)} collective-permute-done((bf16[2,2,16,2048]{3,2,1,0:T(8,128)(2,1)S(1)}, bf16[2,2,16,2048]{3,2,1,0:T(8,128)(2,1)S(1)}, u32[]{:S(2)}, u32[]{:S(2)}) %collective-permute-start.12) | collective-permute-done | bytes 262176 | tf_op jit(solution)/shard_map/ppermute | solution.py:202
  41.1 1.5 %shard_map.116 = f32[128,2048]{1,0:T(8,128)S(1)} custom-call(bf16[128,2048]{1,0:T(8,128)(2,1)S(1)} %bitcast.88, bf16[2048,2048]{1,0:T(8,128)(2,1)S(1)} %shard_map.111.weight_ref), custom_call_target="tpu_custom_call" | custom-call | tf_op jit(solution)/shard_map/pallas_call | solution.py:80
  42.8 1.0 collective-permute-start.16
  44.9 1.6 %collective-permute-start.15 = (bf16[128,2048]{1,0:T(8,128)(2,1)S(1)}, bf16[128,2048]{1,0:T(8,128)(2,1)S(1)}, u32[]{:S(2)}, u32[]{:S(2)}) collective-permute-start(bf16[128,2048]{1,0:T(8,128)(2,1)S(1)} %get-tuple-element.251), channel_id=1, source_target_pairs={{0,16},{8,24},{16,0},{24,8},{1,17},{9,25},{17,1},{25,9},{2,18},{10... | collective-permute-start | bytes 1572872 | tf_op jit(solution)/shard_map/ppermute | solution.py:202
  47.2 1.5 %shard_map.119 = f32[128,2048]{1,0:T(8,128)S(1)} custom-call(bf16[128,2048]{1,0:T(8,128)(2,1)S(1)} %get-tuple-element.186.left_ref, bf16[2048,2048]{1,0:T(8,128)(2,1)S(1)} %shard_map.112.weight_ref), custom_call_target="tpu_custom_call" | custom-call | tf_op jit(solution)/shard_map/pallas_call | solution.py:80
  49.5 2.8 %shard_map.118.weight_ref = bf16[2048,2048]{1,0:T(8,128)(2,1)S(1)} custom-call(bf16[2048,2048]{1,0:T(8,128)(2,1)S(1)} %shard_map.111.weight_ref), custom_call_target="tpu_custom_call" | custom-call | tf_op jit(solution)/shard_map/pallas_call | solution.py:181
  52.4 1.5 %shard_map.117 = f32[128,2048]{1,0:T(8,128)S(1)} custom-call(bf16[128,2048]{1,0:T(8,128)(2,1)S(1)} %bitcast.94, bf16[2048,2048]{1,0:T(8,128)(2,1)S(1)} %shard_map.114.weight_ref), custom_call_target="tpu_custom_call" | custom-call | tf_op jit(solution)/shard_map/pallas_call | solution.py:80
  53.9 3.3 %collective-permute-done.18 = bf16[2,2,16,2048]{3,2,1,0:T(8,128)(2,1)S(1)} collective-permute-done((bf16[2,2,16,2048]{3,2,1,0:T(8,128)(2,1)S(1)}, bf16[2,2,16,2048]{3,2,1,0:T(8,128)(2,1)S(1)}, u32[]{:S(2)}, u32[]{:S(2)}) %collective-permute-start.18) | collective-permute-done | bytes 262176 | tf_op jit(solution)/shard_map/ppermute | solution.py:202
  57.2 1.7 %collective-permute-done.15 = bf16[128,2048]{1,0:T(8,128)(2,1)S(1)} collective-permute-done((bf16[128,2048]{1,0:T(8,128)(2,1)S(1)}, bf16[128,2048]{1,0:T(8,128)(2,1)S(1)}, u32[]{:S(2)}, u32[]{:S(2)}) %collective-permute-start.15) | collective-permute-done | bytes 524320 | tf_op jit(solution)/shard_map/ppermute | solution.py:202
  60.5 1.6 %collective-permute-start.20 = (bf16[64,2048]{1,0:T(8,128)(2,1)S(1)}, bf16[64,2048]{1,0:T(8,128)(2,1)S(1)}, u32[]{:S(2)}, u32[]{:S(2)}) collective-permute-start(bf16[64,2048]{1,0:T(8,128)(2,1)S(1)} %get-tuple-element.249), channel_id=1, source_target_pairs={{0,16},{8,24},{16,0},{24,8},{1,17},{9,25},{17,1},{25,9},{2,18},{10... | collective-permute-start | bytes 786440 | tf_op jit(solution)/shard_map/ppermute | solution.py:202
  62.9 1.5 %shard_map.120 = f32[128,2048]{1,0:T(8,128)S(1)} custom-call(bf16[128,2048]{1,0:T(8,128)(2,1)S(1)} %get-tuple-element.262.left_ref, bf16[2048,2048]{1,0:T(8,128)(2,1)S(1)} %shard_map.112.weight_ref), custom_call_target="tpu_custom_call" | custom-call | tf_op jit(solution)/shard_map/pallas_call | solution.py:80
  65.5 1.5 %shard_map.121 = f32[128,2048]{1,0:T(8,128)S(1)} custom-call(bf16[128,2048]{1,0:T(8,128)(2,1)S(1)} %multiply_convert_fusion.1.left_ref, bf16[2048,2048]{1,0:T(8,128)(2,1)S(1)} %shard_map.118.weight_ref), custom_call_target="tpu_custom_call" | custom-call | tf_op jit(solution)/shard_map/pallas_call | solution.py:80
  67.1 5.6 %shard_map.122 = bf16[2048,2048]{1,0:T(8,128)(2,1)} custom-call(s32[8,8]{1,0:T(8,128)S(1)} %convert_element_type.158.mask_ref, bf16[256,2048]{1,0:T(8,128)(2,1)S(1)} %pad_maximum_fusion.left_ref, bf16[256,2048]{1,0:T(8,128)(2,1)S(1)} %pad_maximum_fusion.1.right_ref), custom_call_target="tpu_custom_call" | custom-call | tf_op jit(solution)/shard_map/pallas_call | solution.py:108
  73.0 1.3 %collective-permute-done.23 = bf16[64,2048]{1,0:T(8,128)(2,1)S(1)} collective-permute-done((bf16[64,2048]{1,0:T(8,128)(2,1)S(1)}, bf16[64,2048]{1,0:T(8,128)(2,1)S(1)}, u32[]{:S(2)}, u32[]{:S(2)}) %collective-permute-start.23) | collective-permute-done | bytes 262176 | tf_op jit(solution)/shard_map/ppermute | solution.py:202
  74.4 1.7 %shard_map.123 = f32[128,2048]{1,0:T(8,128)S(1)} custom-call(bf16[128,2048]{1,0:T(8,128)(2,1)S(1)} %multiply_convert_fusion.left_ref, bf16[2048,2048]{1,0:T(8,128)(2,1)S(1)} %shard_map.118.weight_ref), custom_call_target="tpu_custom_call" | custom-call | tf_op jit(solution)/shard_map/pallas_call | solution.py:80
  76.3 1.3 %collective-permute-start.25 = (f32[2048]{0:T(1024)S(1)}, f32[2048]{0:T(1024)S(1)}, u32[]{:S(2)}, u32[]{:S(2)}) collective-permute-start(f32[2048]{0:T(1024)S(1)} %add.141), channel_id=1, source_target_pairs={{0,1},{1,0},{2,3},{3,2},{4,5},{5,4},{6,7},{7,6},{8,9},{9,8},{10,11... | collective-permute-start | bytes 24584 | tf_op jit(solution)/shard_map/ppermute | solution.py:202
  77.7 1.9 %collective-permute-start.27 = (bf16[2,2,16,2048]{3,2,1,0:T(8,128)(2,1)S(1)}, bf16[2,2,16,2048]{3,2,1,0:T(8,128)(2,1)S(1)}, u32[]{:S(2)}, u32[]{:S(2)}) collective-permute-start(bf16[2,2,16,2048]{3,2,1,0:T(8,128)(2,1)S(1)} %fusion.19), channel_id=1, source_target_pairs={{0,2},{1,3},{2,0},{3,1},{4,6},{5,7},{6,4},{7,5},{8,10},{9,11},{10,... | collective-permute-start | bytes 786440 | tf_op jit(solution)/shard_map/ppermute | solution.py:202
  79.6 1.3 %collective-permute-start.24 = (bf16[2,2,16,2048]{3,2,0,1:T(8,128)(2,1)S(1)}, bf16[2,2,16,2048]{3,2,0,1:T(8,128)(2,1)S(1)}, u32[]{:S(2)}, u32[]{:S(2)}) collective-permute-start(bf16[2,2,16,2048]{3,2,0,1:T(8,128)(2,1)S(1)} %slice.168), channel_id=1, source_target_pairs={{0,1},{1,0},{2,3},{3,2},{4,5},{5,4},{6,7},{7,6},{8,9},{9,8},{10,11... | collective-permute-start | bytes 786440 | tf_op jit(solution)/shard_map/ppermute | solution.py:202
  80.9 1.4 %collective-permute-start.26 = (f32[2048]{0:T(1024)S(1)}, f32[2048]{0:T(1024)S(1)}, u32[]{:S(2)}, u32[]{:S(2)}) collective-permute-start(f32[2048]{0:T(1024)S(1)} %add.142), channel_id=1, source_target_pairs={{0,2},{1,3},{2,0},{3,1},{4,6},{5,7},{6,4},{7,5},{8,10},{9,11},{10,... | collective-permute-start | bytes 24584 | tf_op jit(solution)/shard_map/ppermute | solution.py:202
  82.3 3.7 %collective-permute-done.26 = f32[2048]{0:T(1024)S(1)} collective-permute-done((f32[2048]{0:T(1024)S(1)}, f32[2048]{0:T(1024)S(1)}, u32[]{:S(2)}, u32[]{:S(2)}) %collective-permute-start.26) | collective-permute-done | bytes 8224 | tf_op jit(solution)/shard_map/ppermute | solution.py:202
  86.1 1.4 %collective-permute-done.24 = bf16[2,2,16,2048]{3,2,0,1:T(8,128)(2,1)S(1)} collective-permute-done((bf16[2,2,16,2048]{3,2,0,1:T(8,128)(2,1)S(1)}, bf16[2,2,16,2048]{3,2,0,1:T(8,128)(2,1)S(1)}, u32[]{:S(2)}, u32[]{:S(2)}) %collective-permute-start.24) | collective-permute-done | bytes 262176 | tf_op jit(solution)/shard_map/ppermute | solution.py:202
  88.0 1.7 %collective-permute-start.29 = (f32[2048]{0:T(1024)S(1)}, f32[2048]{0:T(1024)S(1)}, u32[]{:S(2)}, u32[]{:S(2)}) collective-permute-start(f32[2048]{0:T(1024)S(1)} %add.143), channel_id=1, source_target_pairs={{0,4},{1,5},{2,6},{3,7},{4,0},{5,1},{6,2},{7,3},{8,12},{9,13},{10,... | collective-permute-start | bytes 24584 | tf_op jit(solution)/shard_map/ppermute | solution.py:202
  89.7 1.3 %collective-permute-start.30 = (bf16[2,2,16,2048]{3,2,0,1:T(8,128)(2,1)S(1)}, bf16[2,2,16,2048]{3,2,0,1:T(8,128)(2,1)S(1)}, u32[]{:S(2)}, u32[]{:S(2)}) collective-permute-start(bf16[2,2,16,2048]{3,2,0,1:T(8,128)(2,1)S(1)} %slice.141), channel_id=1, source_target_pairs={{0,1},{1,0},{2,3},{3,2},{4,5},{5,4},{6,7},{7,6},{8,9},{9,8},{10,11... | collective-permute-start | bytes 786440 | tf_op jit(solution)/shard_map/ppermute | solution.py:202
  91.1 1.3 %collective-permute-start.31 = (bf16[2,16,2048]{2,1,0:T(8,128)(2,1)S(1)}, bf16[2,16,2048]{2,1,0:T(8,128)(2,1)S(1)}, u32[]{:S(2)}, u32[]{:S(2)}) collective-permute-start(bf16[2,16,2048]{2,1,0:T(8,128)(2,1)S(1)} %fusion.22), channel_id=1, source_target_pairs={{0,4},{1,5},{2,6},{3,7},{4,0},{5,1},{6,2},{7,3},{8,12},{9,13},{10,... | collective-permute-start | bytes 393224 | tf_op jit(solution)/shard_map/ppermute | solution.py:202
  92.6 5.6 %shard_map.124 = bf16[2048,2048]{1,0:T(8,128)(2,1)} custom-call(s32[8,8]{1,0:T(8,128)S(1)} %convert_element_type.157.mask_ref, bf16[256,2048]{1,0:T(8,128)(2,1)S(1)} %pad_maximum_fusion.2.left_ref, bf16[256,2048]{1,0:T(8,128)(2,1)S(1)} %pad_maximum_fusion.3.right_ref), custom_call_target="tpu_custom_call" | custom-call | tf_op jit(solution)/shard_map/pallas_call | solution.py:108
  100.8 1.7 %collective-permute-start.35 = (bf16[8,4096]{1,0:T(8,128)(2,1)S(1)}, bf16[8,4096]{1,0:T(8,128)(2,1)S(1)}, u32[]{:S(2)}, u32[]{:S(2)}) collective-permute-start(bf16[8,4096]{1,0:T(8,128)(2,1)S(1)} %get-tuple-element.272), channel_id=1, source_target_pairs={{0,16},{8,24},{16,0},{24,8},{1,17},{9,25},{17,1},{25,9},{2,18},{10... | collective-permute-start | bytes 196616 | tf_op jit(solution)/shard_map/ppermute | solution.py:202
  102.7 1.1 collective-permute-start.37
  103.7 1.8 %collective-permute-start.38 = (bf16[8,4096]{1,0:T(8,128)(2,1)S(1)}, bf16[8,4096]{1,0:T(8,128)(2,1)S(1)}, u32[]{:S(2)}, u32[]{:S(2)}) collective-permute-start(bf16[8,4096]{1,0:T(8,128)(2,1)S(1)} %get-tuple-element.271), channel_id=1, source_target_pairs={{0,20},{1,21},{2,22},{3,23},{4,16},{5,17},{6,18},{7,19},{8,28},{9,... | collective-permute-start | bytes 196616 | tf_op jit(solution)/shard_map/ppermute | solution.py:202
  105.5 1.7 %collective-permute-start.39 = (bf16[8,4096]{1,0:T(8,128)(2,1)S(1)}, bf16[8,4096]{1,0:T(8,128)(2,1)S(1)}, u32[]{:S(2)}, u32[]{:S(2)}) collective-permute-start(bf16[8,4096]{1,0:T(8,128)(2,1)S(1)} %get-tuple-element.270), channel_id=1, source_target_pairs={{0,16},{8,24},{16,0},{24,8},{1,17},{9,25},{17,1},{25,9},{2,18},{10... | collective-permute-start | bytes 196616 | tf_op jit(solution)/shard_map/ppermute | solution.py:202
  107.8 2.9 %collective-permute-done.37 = bf16[8,4096]{1,0:T(8,128)(2,1)S(1)} collective-permute-done((bf16[8,4096]{1,0:T(8,128)(2,1)S(1)}, bf16[8,4096]{1,0:T(8,128)(2,1)S(1)}, u32[]{:S(2)}, u32[]{:S(2)}) %collective-permute-start.37) | collective-permute-done | bytes 65568 | tf_op jit(solution)/shard_map/ppermute | solution.py:202
  110.8 1.0 collective-permute-done.38
  112.1 0.8 add_convert_fusion.3
  (160 shorter events, 16.4 us)
Async XLA Ops:
  0.6 14.7 %copy-start = (s32[32,32]{1,0:T(8,128)S(1)}, s32[32,32]{1,0:T(8,128)}, u32[]{:S(2)}) copy-start(s32[32,32]{1,0:T(8,128)} %param.12) | copy-start | bytes 12292
  2.0 13.4 %collective-permute-start.2 = (bf16[8,4096]{1,0:T(8,128)(2,1)S(1)}, bf16[8,4096]{1,0:T(8,128)(2,1)S(1)}, u32[]{:S(2)}, u32[]{:S(2)}) collective-permute-start(bf16[8,4096]{1,0:T(8,128)(2,1)S(1)} %get-tuple-element.127), channel_id=1, source_target_pairs={{0,20},{1,21},{2,22},{3,23},{4,16},{5,17},{6,18},{7,19},{8,28},{9,... | collective-permute-start | bytes 196616 | tf_op jit(solution)/shard_map/ppermute | solution.py:202
  7.0 8.5 %collective-permute-start = (bf16[8,4096]{1,0:T(8,128)(2,1)S(1)}, bf16[8,4096]{1,0:T(8,128)(2,1)S(1)}, u32[]{:S(2)}, u32[]{:S(2)}) collective-permute-start(bf16[8,4096]{1,0:T(8,128)(2,1)S(1)} %get-tuple-element.127), channel_id=1, source_target_pairs={{0,16},{8,24},{16,0},{24,8},{1,17},{9,25},{17,1},{25,9},{2,18},{10... | collective-permute-start | bytes 196616 | tf_op jit(solution)/shard_map/ppermute | solution.py:202
  8.4 7.0 %collective-permute-start.3 = (bf16[8,4096]{1,0:T(8,128)(2,1)S(1)}, bf16[8,4096]{1,0:T(8,128)(2,1)S(1)}, u32[]{:S(2)}, u32[]{:S(2)}) collective-permute-start(bf16[8,4096]{1,0:T(8,128)(2,1)S(1)} %get-tuple-element.282), channel_id=1, source_target_pairs={{0,16},{8,24},{16,0},{24,8},{1,17},{9,25},{17,1},{25,9},{2,18},{10... | collective-permute-start | bytes 196616 | tf_op jit(solution)/shard_map/ppermute | solution.py:202
  10.0 5.3 %collective-permute-start.1 = (bf16[8,4096]{1,0:T(8,128)(2,1)S(1)}, bf16[8,4096]{1,0:T(8,128)(2,1)S(1)}, u32[]{:S(2)}, u32[]{:S(2)}) collective-permute-start(bf16[8,4096]{1,0:T(8,128)(2,1)S(1)} %get-tuple-element.126), channel_id=1, source_target_pairs={{0,4},{1,5},{2,6},{3,7},{4,0},{5,1},{6,2},{7,3},{8,12},{9,13},{10,... | collective-permute-start | bytes 196616 | tf_op jit(solution)/shard_map/ppermute | solution.py:202
  15.6 1.5 %collective-permute-start.4 = (bf16[3,16,2048]{2,1,0:T(8,128)(2,1)S(1)}, bf16[3,16,2048]{2,1,0:T(8,128)(2,1)S(1)}, u32[]{:S(2)}, u32[]{:S(2)}) collective-permute-start(bf16[3,16,2048]{2,1,0:T(8,128)(2,1)S(1)} %pad_maximum_fusion.8), channel_id=1, source_target_pairs={{0,8},{8,0},{16,24},{24,16},{1,9},{9,1},{17,25},{25,17},{2,10},{10... | collective-permute-start | bytes 589832 | tf_op jit(solution)/shard_map/ppermute | solution.py:202
  17.2 9.9 %collective-permute-start.8 = (bf16[2,2,16,2048]{3,2,1,0:T(8,128)(2,1)S(1)}, bf16[2,2,16,2048]{3,2,1,0:T(8,128)(2,1)S(1)}, u32[]{:S(2)}, u32[]{:S(2)}) collective-permute-start(bf16[2,2,16,2048]{3,2,1,0:T(8,128)(2,1)S(1)} %constant_dynamic-update-slice_fusion), channel_id=1, source_target_pairs={{0,1},{1,0},{2,3},{3,2},{4,5},{5,4},{6,7},{7,6},{8,9},{9,8},{10,11... | collective-permute-start | bytes 786440 | tf_op jit(solution)/shard_map/ppermute | solution.py:202
  18.6 10.9 %collective-permute-start.6 = (bf16[2,2,16,2048]{3,2,1,0:T(8,128)(2,1)S(1)}, bf16[2,2,16,2048]{3,2,1,0:T(8,128)(2,1)S(1)}, u32[]{:S(2)}, u32[]{:S(2)}) collective-permute-start(bf16[2,2,16,2048]{3,2,1,0:T(8,128)(2,1)S(1)} %constant_dynamic-update-slice_fusion), channel_id=1, source_target_pairs={{0,2},{1,3},{2,0},{3,1},{4,6},{5,7},{6,4},{7,5},{8,10},{9,11},{10,... | collective-permute-start | bytes 786440 | tf_op jit(solution)/shard_map/ppermute | solution.py:202
  20.3 8.5 %collective-permute-start.5 = (bf16[1,2,16,2048]{3,2,1,0:T(8,128)(2,1)S(1)}, bf16[1,2,16,2048]{3,2,1,0:T(8,128)(2,1)S(1)}, u32[]{:S(2)}, u32[]{:S(2)}) collective-permute-start(bf16[1,2,16,2048]{3,2,1,0:T(8,128)(2,1)S(1)} %maximum_bitcast_fusion.6), channel_id=1, source_target_pairs={{0,1},{1,0},{2,3},{3,2},{4,5},{5,4},{6,7},{7,6},{8,9},{9,8},{10,11... | collective-permute-start | bytes 393224 | tf_op jit(solution)/shard_map/ppermute | solution.py:202
  20.7 8.1 %collective-permute-start.7 = (bf16[1,2,16,2048]{3,2,1,0:T(8,128)(2,1)S(1)}, bf16[1,2,16,2048]{3,2,1,0:T(8,128)(2,1)S(1)}, u32[]{:S(2)}, u32[]{:S(2)}) collective-permute-start(bf16[1,2,16,2048]{3,2,1,0:T(8,128)(2,1)S(1)} %maximum_bitcast_fusion.6), channel_id=1, source_target_pairs={{0,4},{1,5},{2,6},{3,7},{4,0},{5,1},{6,2},{7,3},{8,12},{9,13},{10,... | collective-permute-start | bytes 393224 | tf_op jit(solution)/shard_map/ppermute | solution.py:202
  29.4 2.1 %collective-permute-start.10 = (bf16[64,2048]{1,0:T(8,128)(2,1)S(1)}, bf16[64,2048]{1,0:T(8,128)(2,1)S(1)}, u32[]{:S(2)}, u32[]{:S(2)}) collective-permute-start(bf16[64,2048]{1,0:T(8,128)(2,1)S(1)} %slice.212), channel_id=1, source_target_pairs={{0,8},{8,0},{16,24},{24,16},{1,9},{9,1},{17,25},{25,17},{2,10},{10... | collective-permute-start | bytes 786440 | tf_op jit(solution)/shard_map/ppermute | solution.py:202
  29.4 7.9 %collective-permute-start.9 = (bf16[1,2,16,2048]{3,2,1,0:T(8,128)(2,1)S(1)}, bf16[1,2,16,2048]{3,2,1,0:T(8,128)(2,1)S(1)}, u32[]{:S(2)}, u32[]{:S(2)}) collective-permute-start(bf16[1,2,16,2048]{3,2,1,0:T(8,128)(2,1)S(1)} %collective-permute-done.7), channel_id=1, source_target_pairs={{0,1},{1,0},{2,3},{3,2},{4,5},{5,4},{6,7},{7,6},{8,9},{9,8},{10,11... | collective-permute-start | bytes 393224 | tf_op jit(solution)/shard_map/ppermute | solution.py:202
  30.4 10.6 %collective-permute-start.12 = (bf16[2,2,16,2048]{3,2,1,0:T(8,128)(2,1)S(1)}, bf16[2,2,16,2048]{3,2,1,0:T(8,128)(2,1)S(1)}, u32[]{:S(2)}, u32[]{:S(2)}) collective-permute-start(bf16[2,2,16,2048]{3,2,1,0:T(8,128)(2,1)S(1)} %collective-permute-done.6), channel_id=1, source_target_pairs={{0,1},{1,0},{2,3},{3,2},{4,5},{5,4},{6,7},{7,6},{8,9},{9,8},{10,11... | collective-permute-start | bytes 786440 | tf_op jit(solution)/shard_map/ppermute | solution.py:202
  31.6 9.4 %collective-permute-start.11 = (bf16[64,2048]{1,0:T(8,128)(2,1)S(1)}, bf16[64,2048]{1,0:T(8,128)(2,1)S(1)}, u32[]{:S(2)}, u32[]{:S(2)}) collective-permute-start(bf16[64,2048]{1,0:T(8,128)(2,1)S(1)} %get-tuple-element.253), channel_id=1, source_target_pairs={{0,16},{8,24},{16,0},{24,8},{1,17},{9,25},{17,1},{25,9},{2,18},{10... | collective-permute-start | bytes 786440 | tf_op jit(solution)/shard_map/ppermute | solution.py:202
  32.2 8.8 %collective-permute-start.13 = (bf16[2,2,16,2048]{3,2,1,0:T(8,128)(2,1)S(1)}, bf16[2,2,16,2048]{3,2,1,0:T(8,128)(2,1)S(1)}, u32[]{:S(2)}, u32[]{:S(2)}) collective-permute-start(bf16[2,2,16,2048]{3,2,1,0:T(8,128)(2,1)S(1)} %pad_maximum_fusion.7), channel_id=1, source_target_pairs={{0,2},{1,3},{2,0},{3,1},{4,6},{5,7},{6,4},{7,5},{8,10},{9,11},{10,... | collective-permute-start | bytes 786440 | tf_op jit(solution)/shard_map/ppermute | solution.py:202
  38.9 3.8 %copy-start.2 = (f32[128,2048]{1,0:T(8,128)}, f32[128,2048]{1,0:T(8,128)S(1)}, u32[]{:S(2)}) copy-start(f32[128,2048]{1,0:T(8,128)S(1)} %shard_map.115) | copy-start | bytes 3145732
  42.7 2.0 %collective-permute-start.14 = (bf16[128,2048]{1,0:T(8,128)(2,1)S(1)}, bf16[128,2048]{1,0:T(8,128)(2,1)S(1)}, u32[]{:S(2)}, u32[]{:S(2)}) collective-permute-start(bf16[128,2048]{1,0:T(8,128)(2,1)S(1)} %pad_maximum_fusion.4), channel_id=1, source_target_pairs={{0,8},{8,0},{16,24},{24,16},{1,9},{9,1},{17,25},{25,17},{2,10},{10... | collective-permute-start | bytes 1572872 | tf_op jit(solution)/shard_map/ppermute | solution.py:202
  42.8 1.9 %slice-start = ((f32[128,2048]{1,0:T(8,128)}), f32[64,2048]{1,0:T(8,128)S(1)}, s32[]{:S(2)}) async-start(f32[128,2048]{1,0:T(8,128)} %copy-done.2), calls=%async_computation | async-start | bytes 1048576 | tf_op jit(solution)/shard_map/slice | solution.py:315
  42.8 9.4 %collective-permute-start.16 = (bf16[2,2,16,2048]{3,2,1,0:T(8,128)(2,1)S(1)}, bf16[2,2,16,2048]{3,2,1,0:T(8,128)(2,1)S(1)}, u32[]{:S(2)}, u32[]{:S(2)}) collective-permute-start(bf16[2,2,16,2048]{3,2,1,0:T(8,128)(2,1)S(1)} %collective-permute-done.13), channel_id=1, source_target_pairs={{0,1},{1,0},{2,3},{3,2},{4,5},{5,4},{6,7},{7,6},{8,9},{9,8},{10,11... | collective-permute-start | bytes 786440 | tf_op jit(solution)/shard_map/ppermute | solution.py:202
  43.9 2.6 %collective-permute-start.17 = (bf16[64,2048]{1,0:T(8,128)(2,1)S(1)}, bf16[64,2048]{1,0:T(8,128)(2,1)S(1)}, u32[]{:S(2)}, u32[]{:S(2)}) collective-permute-start(bf16[64,2048]{1,0:T(8,128)(2,1)S(1)} %add_convert_fusion.2), channel_id=1, source_target_pairs={{0,8},{8,0},{16,24},{24,16},{1,9},{9,1},{17,25},{25,17},{2,10},{10... | collective-permute-start | bytes 786440 | tf_op jit(solution)/shard_map/ppermute | solution.py:202
  44.9 14.0 %collective-permute-start.15 = (bf16[128,2048]{1,0:T(8,128)(2,1)S(1)}, bf16[128,2048]{1,0:T(8,128)(2,1)S(1)}, u32[]{:S(2)}, u32[]{:S(2)}) collective-permute-start(bf16[128,2048]{1,0:T(8,128)(2,1)S(1)} %get-tuple-element.251), channel_id=1, source_target_pairs={{0,16},{8,24},{16,0},{24,8},{1,17},{9,25},{17,1},{25,9},{2,18},{10... | collective-permute-start | bytes 1572872 | tf_op jit(solution)/shard_map/ppermute | solution.py:202
  48.8 8.4 %collective-permute-start.18 = (bf16[2,2,16,2048]{3,2,1,0:T(8,128)(2,1)S(1)}, bf16[2,2,16,2048]{3,2,1,0:T(8,128)(2,1)S(1)}, u32[]{:S(2)}, u32[]{:S(2)}) collective-permute-start(bf16[2,2,16,2048]{3,2,1,0:T(8,128)(2,1)S(1)} %slice.130), channel_id=1, source_target_pairs={{0,1},{1,0},{2,3},{3,2},{4,5},{5,4},{6,7},{7,6},{8,9},{9,8},{10,11... | collective-permute-start | bytes 786440 | tf_op jit(solution)/shard_map/ppermute | solution.py:202
  58.9 1.5 %collective-permute-start.19 = (bf16[64,2048]{1,0:T(8,128)(2,1)S(1)}, bf16[64,2048]{1,0:T(8,128)(2,1)S(1)}, u32[]{:S(2)}, u32[]{:S(2)}) collective-permute-start(bf16[64,2048]{1,0:T(8,128)(2,1)S(1)} %slice.209), channel_id=1, source_target_pairs={{0,8},{8,0},{16,24},{24,16},{1,9},{9,1},{17,25},{25,17},{2,10},{10... | collective-permute-start | bytes 786440 | tf_op jit(solution)/shard_map/ppermute | solution.py:202
  59.0 3.1 %collective-permute-start.21 = (bf16[128,2048]{1,0:T(8,128)(2,1)S(1)}, bf16[128,2048]{1,0:T(8,128)(2,1)S(1)}, u32[]{:S(2)}, u32[]{:S(2)}) collective-permute-start(bf16[128,2048]{1,0:T(8,128)(2,1)S(1)} %add_convert_fusion), channel_id=1, source_target_pairs={{0,8},{8,0},{16,24},{24,16},{1,9},{9,1},{17,25},{25,17},{2,10},{10... | collective-permute-start | bytes 1572872 | tf_op jit(solution)/shard_map/ppermute | solution.py:202
  60.5 12.1 %collective-permute-start.20 = (bf16[64,2048]{1,0:T(8,128)(2,1)S(1)}, bf16[64,2048]{1,0:T(8,128)(2,1)S(1)}, u32[]{:S(2)}, u32[]{:S(2)}) collective-permute-start(bf16[64,2048]{1,0:T(8,128)(2,1)S(1)} %get-tuple-element.249), channel_id=1, source_target_pairs={{0,16},{8,24},{16,0},{24,8},{1,17},{9,25},{17,1},{25,9},{2,18},{10... | collective-permute-start | bytes 786440 | tf_op jit(solution)/shard_map/ppermute | solution.py:202
  64.5 8.1 %collective-permute-start.22 = (bf16[2,2,16,2048]{3,2,1,0:T(8,128)(2,1)S(1)}, bf16[2,2,16,2048]{3,2,1,0:T(8,128)(2,1)S(1)}, u32[]{:S(2)}, u32[]{:S(2)}) collective-permute-start(bf16[2,2,16,2048]{3,2,1,0:T(8,128)(2,1)S(1)} %slice.165), channel_id=1, source_target_pairs={{0,1},{1,0},{2,3},{3,2},{4,5},{5,4},{6,7},{7,6},{8,9},{9,8},{10,11... | collective-permute-start | bytes 786440 | tf_op jit(solution)/shard_map/ppermute | solution.py:202
  72.7 1.6 %collective-permute-start.23 = (bf16[64,2048]{1,0:T(8,128)(2,1)S(1)}, bf16[64,2048]{1,0:T(8,128)(2,1)S(1)}, u32[]{:S(2)}, u32[]{:S(2)}) collective-permute-start(bf16[64,2048]{1,0:T(8,128)(2,1)S(1)} %add_convert_fusion.1), channel_id=1, source_target_pairs={{0,8},{8,0},{16,24},{24,16},{1,9},{9,1},{17,25},{25,17},{2,10},{10... | collective-permute-start | bytes 786440 | tf_op jit(solution)/shard_map/ppermute | solution.py:202
  76.3 4.6 %collective-permute-start.25 = (f32[2048]{0:T(1024)S(1)}, f32[2048]{0:T(1024)S(1)}, u32[]{:S(2)}, u32[]{:S(2)}) collective-permute-start(f32[2048]{0:T(1024)S(1)} %add.141), channel_id=1, source_target_pairs={{0,1},{1,0},{2,3},{3,2},{4,5},{5,4},{6,7},{7,6},{8,9},{9,8},{10,11... | collective-permute-start | bytes 24584 | tf_op jit(solution)/shard_map/ppermute | solution.py:202
  77.7 8.4 %collective-permute-start.27 = (bf16[2,2,16,2048]{3,2,1,0:T(8,128)(2,1)S(1)}, bf16[2,2,16,2048]{3,2,1,0:T(8,128)(2,1)S(1)}, u32[]{:S(2)}, u32[]{:S(2)}) collective-permute-start(bf16[2,2,16,2048]{3,2,1,0:T(8,128)(2,1)S(1)} %fusion.19), channel_id=1, source_target_pairs={{0,2},{1,3},{2,0},{3,1},{4,6},{5,7},{6,4},{7,5},{8,10},{9,11},{10,... | collective-permute-start | bytes 786440 | tf_op jit(solution)/shard_map/ppermute | solution.py:202
  79.6 7.8 %collective-permute-start.24 = (bf16[2,2,16,2048]{3,2,0,1:T(8,128)(2,1)S(1)}, bf16[2,2,16,2048]{3,2,0,1:T(8,128)(2,1)S(1)}, u32[]{:S(2)}, u32[]{:S(2)}) collective-permute-start(bf16[2,2,16,2048]{3,2,0,1:T(8,128)(2,1)S(1)} %slice.168), channel_id=1, source_target_pairs={{0,1},{1,0},{2,3},{3,2},{4,5},{5,4},{6,7},{7,6},{8,9},{9,8},{10,11... | collective-permute-start | bytes 786440 | tf_op jit(solution)/shard_map/ppermute | solution.py:202
  80.9 5.2 %collective-permute-start.26 = (f32[2048]{0:T(1024)S(1)}, f32[2048]{0:T(1024)S(1)}, u32[]{:S(2)}, u32[]{:S(2)}) collective-permute-start(f32[2048]{0:T(1024)S(1)} %add.142), channel_id=1, source_target_pairs={{0,2},{1,3},{2,0},{3,1},{4,6},{5,7},{6,4},{7,5},{8,10},{9,11},{10,... | collective-permute-start | bytes 24584 | tf_op jit(solution)/shard_map/ppermute | solution.py:202
  87.5 11.4 %collective-permute-start.28 = (bf16[2,2,16,2048]{3,2,0,1:T(8,128)(2,1)S(1)}, bf16[2,2,16,2048]{3,2,0,1:T(8,128)(2,1)S(1)}, u32[]{:S(2)}, u32[]{:S(2)}) collective-permute-start(bf16[2,2,16,2048]{3,2,0,1:T(8,128)(2,1)S(1)} %fusion.18), channel_id=1, source_target_pairs={{0,2},{1,3},{2,0},{3,1},{4,6},{5,7},{6,4},{7,5},{8,10},{9,11},{10,... | collective-permute-start | bytes 786440 | tf_op jit(solution)/shard_map/ppermute | solution.py:202
  88.0 10.3 %collective-permute-start.29 = (f32[2048]{0:T(1024)S(1)}, f32[2048]{0:T(1024)S(1)}, u32[]{:S(2)}, u32[]{:S(2)}) collective-permute-start(f32[2048]{0:T(1024)S(1)} %add.143), channel_id=1, source_target_pairs={{0,4},{1,5},{2,6},{3,7},{4,0},{5,1},{6,2},{7,3},{8,12},{9,13},{10,... | collective-permute-start | bytes 24584 | tf_op jit(solution)/shard_map/ppermute | solution.py:202
  89.7 9.2 %collective-permute-start.30 = (bf16[2,2,16,2048]{3,2,0,1:T(8,128)(2,1)S(1)}, bf16[2,2,16,2048]{3,2,0,1:T(8,128)(2,1)S(1)}, u32[]{:S(2)}, u32[]{:S(2)}) collective-permute-start(bf16[2,2,16,2048]{3,2,0,1:T(8,128)(2,1)S(1)} %slice.141), channel_id=1, source_target_pairs={{0,1},{1,0},{2,3},{3,2},{4,5},{5,4},{6,7},{7,6},{8,9},{9,8},{10,11... | collective-permute-start | bytes 786440 | tf_op jit(solution)/shard_map/ppermute | solution.py:202
  91.1 7.8 %collective-permute-start.31 = (bf16[2,16,2048]{2,1,0:T(8,128)(2,1)S(1)}, bf16[2,16,2048]{2,1,0:T(8,128)(2,1)S(1)}, u32[]{:S(2)}, u32[]{:S(2)}) collective-permute-start(bf16[2,16,2048]{2,1,0:T(8,128)(2,1)S(1)} %fusion.22), channel_id=1, source_target_pairs={{0,4},{1,5},{2,6},{3,7},{4,0},{5,1},{6,2},{7,3},{8,12},{9,13},{10,... | collective-permute-start | bytes 393224 | tf_op jit(solution)/shard_map/ppermute | solution.py:202
  99.1 8.1 %copy-start.4 = (f32[8192]{0:T(1024)S(1)}, f32[8192]{0:T(1024)}, u32[]{:S(2)}) copy-start(f32[8192]{0:T(1024)} %param.8) | copy-start | bytes 98308
  99.1 1.2 %collective-permute-start.32 = (f32[2048]{0:T(1024)S(1)}, f32[2048]{0:T(1024)S(1)}, u32[]{:S(2)}, u32[]{:S(2)}) collective-permute-start(f32[2048]{0:T(1024)S(1)} %add.148), channel_id=1, source_target_pairs={{0,8},{8,0},{16,24},{24,16},{1,9},{9,1},{17,25},{25,17},{2,10},{10... | collective-permute-start | bytes 24584 | tf_op jit(solution)/shard_map/ppermute | solution.py:202
  99.2 1.5 %collective-permute-start.34 = (bf16[16,2048]{1,0:T(8,128)(2,1)S(1)}, bf16[16,2048]{1,0:T(8,128)(2,1)S(1)}, u32[]{:S(2)}, u32[]{:S(2)}) collective-permute-start(bf16[16,2048]{1,0:T(8,128)(2,1)S(1)} %get-tuple-element.274), channel_id=1, source_target_pairs={{0,8},{8,0},{16,24},{24,16},{1,9},{9,1},{17,25},{25,17},{2,10},{10... | collective-permute-start | bytes 196616 | tf_op jit(solution)/shard_map/ppermute | solution.py:202
  99.8 2.7 %collective-permute-start.36 = (bf16[2,16,2048]{2,1,0:T(8,128)(2,1)S(1)}, bf16[2,16,2048]{2,1,0:T(8,128)(2,1)S(1)}, u32[]{:S(2)}, u32[]{:S(2)}) collective-permute-start(bf16[2,16,2048]{2,1,0:T(8,128)(2,1)S(1)} %fusion.23), channel_id=1, source_target_pairs={{0,8},{8,0},{16,24},{24,16},{1,9},{9,1},{17,25},{25,17},{2,10},{10... | collective-permute-start | bytes 393224 | tf_op jit(solution)/shard_map/ppermute | solution.py:202
  100.3 6.9 %collective-permute-start.33 = (f32[4096]{0:T(1024)S(1)}, f32[4096]{0:T(1024)S(1)}, u32[]{:S(2)}, u32[]{:S(2)}) collective-permute-start(f32[4096]{0:T(1024)S(1)} %maximum_select_fusion.8), channel_id=1, source_target_pairs={{0,16},{8,24},{16,0},{24,8},{1,17},{9,25},{17,1},{25,9},{2,18},{10... | collective-permute-start | bytes 49160 | tf_op jit(solution)/shard_map/ppermute | solution.py:202
  100.7 11.4 %copy-start.3 = (bf16[8,8192]{1,0:T(8,128)(2,1)S(1)}, bf16[8,8192]{1,0:T(8,128)(2,1)}, u32[]{:S(2)}) copy-start(bf16[8,8192]{1,0:T(8,128)(2,1)} %input_hbm.1) | copy-start | bytes 393220
  100.7 11.4 %copy-start.5 = (bf16[8,8192]{1,0:T(8,128)(2,1)S(1)}, bf16[8,8192]{1,0:T(8,128)(2,1)}, u32[]{:S(2)}) copy-start(bf16[8,8192]{1,0:T(8,128)(2,1)} %param.13) | copy-start | bytes 393220
  100.8 7.1 %collective-permute-start.35 = (bf16[8,4096]{1,0:T(8,128)(2,1)S(1)}, bf16[8,4096]{1,0:T(8,128)(2,1)S(1)}, u32[]{:S(2)}, u32[]{:S(2)}) collective-permute-start(bf16[8,4096]{1,0:T(8,128)(2,1)S(1)} %get-tuple-element.272), channel_id=1, source_target_pairs={{0,16},{8,24},{16,0},{24,8},{1,17},{9,25},{17,1},{25,9},{2,18},{10... | collective-permute-start | bytes 196616 | tf_op jit(solution)/shard_map/ppermute | solution.py:202
  102.5 10.5 %copy-start.1 = (s32[32,32]{1,0:T(8,128)S(1)}, s32[32,32]{1,0:T(8,128)}, u32[]{:S(2)}) copy-start(s32[32,32]{1,0:T(8,128)} %param.12) | copy-start | bytes 12292
  102.7 8.1 %collective-permute-start.37 = (bf16[8,4096]{1,0:T(8,128)(2,1)S(1)}, bf16[8,4096]{1,0:T(8,128)(2,1)S(1)}, u32[]{:S(2)}, u32[]{:S(2)}) collective-permute-start(bf16[8,4096]{1,0:T(8,128)(2,1)S(1)} %fusion.24), channel_id=1, source_target_pairs={{0,4},{1,5},{2,6},{3,7},{4,0},{5,1},{6,2},{7,3},{8,12},{9,13},{10,... | collective-permute-start | bytes 196616 | tf_op jit(solution)/shard_map/ppermute | solution.py:202
  103.7 8.0 %collective-permute-start.38 = (bf16[8,4096]{1,0:T(8,128)(2,1)S(1)}, bf16[8,4096]{1,0:T(8,128)(2,1)S(1)}, u32[]{:S(2)}, u32[]{:S(2)}) collective-permute-start(bf16[8,4096]{1,0:T(8,128)(2,1)S(1)} %get-tuple-element.271), channel_id=1, source_target_pairs={{0,20},{1,21},{2,22},{3,23},{4,16},{5,17},{6,18},{7,19},{8,28},{9,... | collective-permute-start | bytes 196616 | tf_op jit(solution)/shard_map/ppermute | solution.py:202
  105.5 6.2 %collective-permute-start.39 = (bf16[8,4096]{1,0:T(8,128)(2,1)S(1)}, bf16[8,4096]{1,0:T(8,128)(2,1)S(1)}, u32[]{:S(2)}, u32[]{:S(2)}) collective-permute-start(bf16[8,4096]{1,0:T(8,128)(2,1)S(1)} %get-tuple-element.270), channel_id=1, source_target_pairs={{0,16},{8,24},{16,0},{24,8},{1,17},{9,25},{17,1},{25,9},{2,18},{10... | collective-permute-start | bytes 196616 | tf_op jit(solution)/shard_map/ppermute | solution.py:202

commit v5 on v4

--- a/solution.py
+++ b/solution.py
@@ -350,7 +350,7 @@
     gfirst, gnear = swapped(2, "col", 1, gown), []
     xheld, gheld = [xown, xline0], [gown]
     for i in range(1, last):
-        xline.append(swapped(1 + i, "col", line[i], work(1 + i, join, *xheld)))
+        xline.append(swapped(1 + i, "col", line[i], work(1 + i, join, *xheld), True))
         xheld.append(xline[i])
     gline.append(swapped(2, "col", line[0], gown))
     gheld.append(gline[0])

time: 113 us -> 113 us (level)
  no operation moved by 1% of the time
where the time goes in v5:
time: 113 us
  starting transfers between devices  42.8 us (38%)
  Pallas kernels  37.5 us (33%)
  waiting for transfers between devices  21.7 us (19%)
  other arithmetic  7.33 us (6%)
  local copies, waits for them, and re-layouts  1.75 us (2%)
  between operations  1.57 us (1%)
    ppermute x40, starting transfers between devices, swap(): return lax.ppermute(value, axis, [(i, i ^ distance) for i in range(size)])  42.8 us
    ppermute x40, waiting for transfers between devices, swap(): return lax.ppermute(value, axis, [(i, i ^ distance) for i in range(size)])  21.7 us
    pallas_call x8, Pallas kernels, product(): pl.pallas_call(product_kernel, out_shape=jax.ShapeDtypeStruct((left.shape...  12.1 us
    pallas_call x2, Pallas kernels, outer(): pl.pallas_call(outer_kernel, grid=(rows // step,), out_shape=jax.ShapeDty...  11.2 us
    pallas_call x2, Pallas kernels, keep(): pl.pallas_call(keep_kernel, out_shape=pltpu.VMEM(weight.shape, weight.dty...  7.44 us
    pallas_call x2, Pallas kernels, turn(): pl.pallas_call(turn_kernel, out_shape=pltpu.VMEM(weight.shape[::-1], weig...  5.54 us
  transfers between devices with their start and end apart: 40, of which 14 were waited for; matrix products, arithmetic and copies ran while one was open for 6% of the time, Pallas kernels for 29%

profile of v5, /device:TPU:0, one launch (start us, length us, event | category | flops | bytes accessed | tf_op | source)
XLA Modules:
  0.0 112.7 jit_solution(12146731094493083681)
XLA Ops:
  0.7 1.3 %shard_map.110 = (bf16[8,4096]{1,0:T(8,128)(2,1)S(1)}, bf16[8,4096]{1,0:T(8,128)(2,1)S(1)}, f32[8,8192]{1,0:T(8,128)S(1)}, f32[8,1]{1,0:T(8,128)S(1)}) custom-call(s32[1]{0:T(128)} %bitcast.far_ref, bf16[8,8192]{1,0:T(8,128)(2,1)} %input_hbm.1, f32[1,8192]{1,0:T(1,128)} %bitcast.104), custom_call_target="tpu_custom_call" | custom-call | tf_op jit(solution)/shard_map/pallas_call | solution.py:151
  2.0 5.1 %collective-permute-start.2 = (bf16[8,4096]{1,0:T(8,128)(2,1)S(1)}, bf16[8,4096]{1,0:T(8,128)(2,1)S(1)}, u32[]{:S(2)}, u32[]{:S(2)}) collective-permute-start(bf16[8,4096]{1,0:T(8,128)(2,1)S(1)} %get-tuple-element.127), channel_id=1, source_target_pairs={{0,20},{1,21},{2,22},{3,23},{4,16},{5,17},{6,18},{7,19},{8,28},{9,... | collective-permute-start | bytes 196616 | tf_op jit(solution)/shard_map/ppermute | solution.py:202
  7.5 0.9 broadcast_select_fusion.3
  8.4 1.6 %collective-permute-start.3 = (bf16[8,4096]{1,0:T(8,128)(2,1)S(1)}, bf16[8,4096]{1,0:T(8,128)(2,1)S(1)}, u32[]{:S(2)}, u32[]{:S(2)}) collective-permute-start(bf16[8,4096]{1,0:T(8,128)(2,1)S(1)} %get-tuple-element.282), channel_id=1, source_target_pairs={{0,16},{8,24},{16,0},{24,8},{1,17},{9,25},{17,1},{25,9},{2,18},{10... | collective-permute-start | bytes 196616 | tf_op jit(solution)/shard_map/ppermute | solution.py:202
  11.5 3.7 %shard_map.111.weight_ref = bf16[2048,2048]{1,0:T(8,128)(2,1)S(1)} custom-call(s32[8,8]{1,0:T(8,128)S(1)} %convert_element_type.157.mask_ref, bf16[2048,2048]{1,0:T(8,128)(2,1)} %weight_ref.2), custom_call_target="tpu_custom_call" | custom-call | tf_op jit(solution)/shard_map/pallas_call | solution.py:56
  15.9 1.1 collective-permute-done.4
  17.1 1.5 %collective-permute-start.8 = (bf16[2,2,16,2048]{3,2,1,0:T(8,128)(2,1)S(1)}, bf16[2,2,16,2048]{3,2,1,0:T(8,128)(2,1)S(1)}, u32[]{:S(2)}, u32[]{:S(2)}) collective-permute-start(bf16[2,2,16,2048]{3,2,1,0:T(8,128)(2,1)S(1)} %constant_dynamic-update-slice_fusion), channel_id=1, source_target_pairs={{0,1},{1,0},{2,3},{3,2},{4,5},{5,4},{6,7},{7,6},{8,9},{9,8},{10,11... | collective-permute-start | bytes 786440 | tf_op jit(solution)/shard_map/ppermute | solution.py:202
  18.6 1.6 %collective-permute-start.5 = (bf16[2,2,16,2048]{3,2,1,0:T(8,128)(2,1)S(1)}, bf16[2,2,16,2048]{3,2,1,0:T(8,128)(2,1)S(1)}, u32[]{:S(2)}, u32[]{:S(2)}) collective-permute-start(bf16[2,2,16,2048]{3,2,1,0:T(8,128)(2,1)S(1)} %constant_dynamic-update-slice_fusion), channel_id=1, source_target_pairs={{0,2},{1,3},{2,0},{3,1},{4,6},{5,7},{6,4},{7,5},{8,10},{9,11},{10,... | collective-permute-start | bytes 786440 | tf_op jit(solution)/shard_map/ppermute | solution.py:202
  20.7 2.5 %collective-permute-start.7 = (bf16[1,2,16,2048]{3,2,1,0:T(8,128)(2,1)S(1)}, bf16[1,2,16,2048]{3,2,1,0:T(8,128)(2,1)S(1)}, u32[]{:S(2)}, u32[]{:S(2)}) collective-permute-start(bf16[1,2,16,2048]{3,2,1,0:T(8,128)(2,1)S(1)} %maximum_bitcast_fusion.6), channel_id=1, source_target_pairs={{0,4},{1,5},{2,6},{3,7},{4,0},{5,1},{6,2},{7,3},{8,12},{9,13},{10,... | collective-permute-start | bytes 393224 | tf_op jit(solution)/shard_map/ppermute | solution.py:202
  23.2 3.7 %shard_map.112.weight_ref = bf16[2048,2048]{1,0:T(8,128)(2,1)S(1)} custom-call(s32[8,8]{1,0:T(8,128)S(1)} %convert_element_type.158.mask_ref, bf16[2048,2048]{1,0:T(8,128)(2,1)} %weight_ref.3), custom_call_target="tpu_custom_call" | custom-call | tf_op jit(solution)/shard_map/pallas_call | solution.py:56
  27.1 1.5 %shard_map.113 = f32[128,2048]{1,0:T(8,128)S(1)} custom-call(bf16[128,2048]{1,0:T(8,128)(2,1)S(1)} %bitcast.85, bf16[2048,2048]{1,0:T(8,128)(2,1)S(1)} %shard_map.111.weight_ref), custom_call_target="tpu_custom_call" | custom-call | tf_op jit(solution)/shard_map/pallas_call | solution.py:80
  30.1 1.4 %collective-permute-start.12 = (bf16[2,2,16,2048]{3,2,1,0:T(8,128)(2,1)S(1)}, bf16[2,2,16,2048]{3,2,1,0:T(8,128)(2,1)S(1)}, u32[]{:S(2)}, u32[]{:S(2)}) collective-permute-start(bf16[2,2,16,2048]{3,2,1,0:T(8,128)(2,1)S(1)} %collective-permute-done.5), channel_id=1, source_target_pairs={{0,1},{1,0},{2,3},{3,2},{4,5},{5,4},{6,7},{7,6},{8,9},{9,8},{10,11... | collective-permute-start | bytes 786440 | tf_op jit(solution)/shard_map/ppermute | solution.py:202
  31.6 0.9 collective-permute-start.11
  32.4 2.4 %collective-permute-start.13 = (bf16[2,2,16,2048]{3,2,1,0:T(8,128)(2,1)S(1)}, bf16[2,2,16,2048]{3,2,1,0:T(8,128)(2,1)S(1)}, u32[]{:S(2)}, u32[]{:S(2)}) collective-permute-start(bf16[2,2,16,2048]{3,2,1,0:T(8,128)(2,1)S(1)} %pad_maximum_fusion.7), channel_id=1, source_target_pairs={{0,2},{1,3},{2,0},{3,1},{4,6},{5,7},{6,4},{7,5},{8,10},{9,11},{10,... | collective-permute-start | bytes 786440 | tf_op jit(solution)/shard_map/ppermute | solution.py:202
  34.8 2.8 %shard_map.114.weight_ref = bf16[2048,2048]{1,0:T(8,128)(2,1)S(1)} custom-call(bf16[2048,2048]{1,0:T(8,128)(2,1)S(1)} %shard_map.112.weight_ref), custom_call_target="tpu_custom_call" | custom-call | tf_op jit(solution)/shard_map/pallas_call | solution.py:181
  37.7 1.5 %shard_map.115 = f32[128,2048]{1,0:T(8,128)S(1)} custom-call(bf16[128,2048]{1,0:T(8,128)(2,1)S(1)} %bitcast.92, bf16[2048,2048]{1,0:T(8,128)(2,1)S(1)} %shard_map.114.weight_ref), custom_call_target="tpu_custom_call" | custom-call | tf_op jit(solution)/shard_map/pallas_call | solution.py:80
  39.2 1.7 %collective-permute-done.12 = bf16[2,2,16,2048]{3,2,1,0:T(8,128)(2,1)S(1)} collective-permute-done((bf16[2,2,16,2048]{3,2,1,0:T(8,128)(2,1)S(1)}, bf16[2,2,16,2048]{3,2,1,0:T(8,128)(2,1)S(1)}, u32[]{:S(2)}, u32[]{:S(2)}) %collective-permute-start.12) | collective-permute-done | bytes 262176 | tf_op jit(solution)/shard_map/ppermute | solution.py:202
  41.1 1.5 %shard_map.116 = f32[128,2048]{1,0:T(8,128)S(1)} custom-call(bf16[128,2048]{1,0:T(8,128)(2,1)S(1)} %bitcast.88, bf16[2048,2048]{1,0:T(8,128)(2,1)S(1)} %shard_map.111.weight_ref), custom_call_target="tpu_custom_call" | custom-call | tf_op jit(solution)/shard_map/pallas_call | solution.py:80
  44.9 1.4 %collective-permute-start.15 = (bf16[128,2048]{1,0:T(8,128)(2,1)S(1)}, bf16[128,2048]{1,0:T(8,128)(2,1)S(1)}, u32[]{:S(2)}, u32[]{:S(2)}) collective-permute-start(bf16[128,2048]{1,0:T(8,128)(2,1)S(1)} %get-tuple-element.251), channel_id=1, source_target_pairs={{0,16},{8,24},{16,0},{24,8},{1,17},{9,25},{17,1},{25,9},{2,18},{10... | collective-permute-start | bytes 1572872 | tf_op jit(solution)/shard_map/ppermute | solution.py:202
  47.0 1.5 %shard_map.119 = f32[128,2048]{1,0:T(8,128)S(1)} custom-call(bf16[128,2048]{1,0:T(8,128)(2,1)S(1)} %get-tuple-element.186.left_ref, bf16[2048,2048]{1,0:T(8,128)(2,1)S(1)} %shard_map.112.weight_ref), custom_call_target="tpu_custom_call" | custom-call | tf_op jit(solution)/shard_map/pallas_call | solution.py:80
  49.4 2.8 %shard_map.118.weight_ref = bf16[2048,2048]{1,0:T(8,128)(2,1)S(1)} custom-call(bf16[2048,2048]{1,0:T(8,128)(2,1)S(1)} %shard_map.111.weight_ref), custom_call_target="tpu_custom_call" | custom-call | tf_op jit(solution)/shard_map/pallas_call | solution.py:181
  52.3 1.5 %shard_map.117 = f32[128,2048]{1,0:T(8,128)S(1)} custom-call(bf16[128,2048]{1,0:T(8,128)(2,1)S(1)} %bitcast.94, bf16[2048,2048]{1,0:T(8,128)(2,1)S(1)} %shard_map.114.weight_ref), custom_call_target="tpu_custom_call" | custom-call | tf_op jit(solution)/shard_map/pallas_call | solution.py:80
  53.8 3.4 %collective-permute-done.18 = bf16[2,2,16,2048]{3,2,1,0:T(8,128)(2,1)S(1)} collective-permute-done((bf16[2,2,16,2048]{3,2,1,0:T(8,128)(2,1)S(1)}, bf16[2,2,16,2048]{3,2,1,0:T(8,128)(2,1)S(1)}, u32[]{:S(2)}, u32[]{:S(2)}) %collective-permute-start.18) | collective-permute-done | bytes 262176 | tf_op jit(solution)/shard_map/ppermute | solution.py:202
  57.2 1.7 %collective-permute-done.15 = bf16[128,2048]{1,0:T(8,128)(2,1)S(1)} collective-permute-done((bf16[128,2048]{1,0:T(8,128)(2,1)S(1)}, bf16[128,2048]{1,0:T(8,128)(2,1)S(1)}, u32[]{:S(2)}, u32[]{:S(2)}) %collective-permute-start.15) | collective-permute-done | bytes 524320 | tf_op jit(solution)/shard_map/ppermute | solution.py:202
  60.5 1.4 %collective-permute-start.20 = (bf16[64,2048]{1,0:T(8,128)(2,1)S(1)}, bf16[64,2048]{1,0:T(8,128)(2,1)S(1)}, u32[]{:S(2)}, u32[]{:S(2)}) collective-permute-start(bf16[64,2048]{1,0:T(8,128)(2,1)S(1)} %get-tuple-element.249), channel_id=1, source_target_pairs={{0,16},{8,24},{16,0},{24,8},{1,17},{9,25},{17,1},{25,9},{2,18},{10... | collective-permute-start | bytes 786440 | tf_op jit(solution)/shard_map/ppermute | solution.py:202
  62.7 1.5 %shard_map.120 = f32[128,2048]{1,0:T(8,128)S(1)} custom-call(bf16[128,2048]{1,0:T(8,128)(2,1)S(1)} %get-tuple-element.262.left_ref, bf16[2048,2048]{1,0:T(8,128)(2,1)S(1)} %shard_map.112.weight_ref), custom_call_target="tpu_custom_call" | custom-call | tf_op jit(solution)/shard_map/pallas_call | solution.py:80
  64.3 0.8 collective-permute-start.22
  65.3 1.5 %shard_map.121 = f32[128,2048]{1,0:T(8,128)S(1)} custom-call(bf16[128,2048]{1,0:T(8,128)(2,1)S(1)} %multiply_convert_fusion.1.left_ref, bf16[2048,2048]{1,0:T(8,128)(2,1)S(1)} %shard_map.118.weight_ref), custom_call_target="tpu_custom_call" | custom-call | tf_op jit(solution)/shard_map/pallas_call | solution.py:80
  66.9 5.6 %shard_map.122 = bf16[2048,2048]{1,0:T(8,128)(2,1)} custom-call(s32[8,8]{1,0:T(8,128)S(1)} %convert_element_type.158.mask_ref, bf16[256,2048]{1,0:T(8,128)(2,1)S(1)} %pad_maximum_fusion.left_ref, bf16[256,2048]{1,0:T(8,128)(2,1)S(1)} %pad_maximum_fusion.1.right_ref), custom_call_target="tpu_custom_call" | custom-call | tf_op jit(solution)/shard_map/pallas_call | solution.py:108
  72.8 1.3 %collective-permute-done.23 = bf16[64,2048]{1,0:T(8,128)(2,1)S(1)} collective-permute-done((bf16[64,2048]{1,0:T(8,128)(2,1)S(1)}, bf16[64,2048]{1,0:T(8,128)(2,1)S(1)}, u32[]{:S(2)}, u32[]{:S(2)}) %collective-permute-start.23) | collective-permute-done | bytes 262176 | tf_op jit(solution)/shard_map/ppermute | solution.py:202
  74.2 1.7 %shard_map.123 = f32[128,2048]{1,0:T(8,128)S(1)} custom-call(bf16[128,2048]{1,0:T(8,128)(2,1)S(1)} %multiply_convert_fusion.left_ref, bf16[2048,2048]{1,0:T(8,128)(2,1)S(1)} %shard_map.118.weight_ref), custom_call_target="tpu_custom_call" | custom-call | tf_op jit(solution)/shard_map/pallas_call | solution.py:80
  76.1 1.3 %collective-permute-start.25 = (f32[2048]{0:T(1024)S(1)}, f32[2048]{0:T(1024)S(1)}, u32[]{:S(2)}, u32[]{:S(2)}) collective-permute-start(f32[2048]{0:T(1024)S(1)} %add.141), channel_id=1, source_target_pairs={{0,1},{1,0},{2,3},{3,2},{4,5},{5,4},{6,7},{7,6},{8,9},{9,8},{10,11... | collective-permute-start | bytes 24584 | tf_op jit(solution)/shard_map/ppermute | solution.py:202
  77.5 1.9 %collective-permute-start.27 = (bf16[2,2,16,2048]{3,2,1,0:T(8,128)(2,1)S(1)}, bf16[2,2,16,2048]{3,2,1,0:T(8,128)(2,1)S(1)}, u32[]{:S(2)}, u32[]{:S(2)}) collective-permute-start(bf16[2,2,16,2048]{3,2,1,0:T(8,128)(2,1)S(1)} %fusion.19), channel_id=1, source_target_pairs={{0,2},{1,3},{2,0},{3,1},{4,6},{5,7},{6,4},{7,5},{8,10},{9,11},{10,... | collective-permute-start | bytes 786440 | tf_op jit(solution)/shard_map/ppermute | solution.py:202
  79.5 1.2 %collective-permute-start.24 = (bf16[2,2,16,2048]{3,2,0,1:T(8,128)(2,1)S(1)}, bf16[2,2,16,2048]{3,2,0,1:T(8,128)(2,1)S(1)}, u32[]{:S(2)}, u32[]{:S(2)}) collective-permute-start(bf16[2,2,16,2048]{3,2,0,1:T(8,128)(2,1)S(1)} %slice.168), channel_id=1, source_target_pairs={{0,1},{1,0},{2,3},{3,2},{4,5},{5,4},{6,7},{7,6},{8,9},{9,8},{10,11... | collective-permute-start | bytes 786440 | tf_op jit(solution)/shard_map/ppermute | solution.py:202
  80.7 1.4 %collective-permute-start.26 = (f32[2048]{0:T(1024)S(1)}, f32[2048]{0:T(1024)S(1)}, u32[]{:S(2)}, u32[]{:S(2)}) collective-permute-start(f32[2048]{0:T(1024)S(1)} %add.142), channel_id=1, source_target_pairs={{0,2},{1,3},{2,0},{3,1},{4,6},{5,7},{6,4},{7,5},{8,10},{9,11},{10,... | collective-permute-start | bytes 24584 | tf_op jit(solution)/shard_map/ppermute | solution.py:202
  82.1 3.8 %collective-permute-done.26 = f32[2048]{0:T(1024)S(1)} collective-permute-done((f32[2048]{0:T(1024)S(1)}, f32[2048]{0:T(1024)S(1)}, u32[]{:S(2)}, u32[]{:S(2)}) %collective-permute-start.26) | collective-permute-done | bytes 8224 | tf_op jit(solution)/shard_map/ppermute | solution.py:202
  85.9 1.4 %collective-permute-done.24 = bf16[2,2,16,2048]{3,2,0,1:T(8,128)(2,1)S(1)} collective-permute-done((bf16[2,2,16,2048]{3,2,0,1:T(8,128)(2,1)S(1)}, bf16[2,2,16,2048]{3,2,0,1:T(8,128)(2,1)S(1)}, u32[]{:S(2)}, u32[]{:S(2)}) %collective-permute-start.24) | collective-permute-done | bytes 262176 | tf_op jit(solution)/shard_map/ppermute | solution.py:202
  87.8 1.6 %collective-permute-start.29 = (f32[2048]{0:T(1024)S(1)}, f32[2048]{0:T(1024)S(1)}, u32[]{:S(2)}, u32[]{:S(2)}) collective-permute-start(f32[2048]{0:T(1024)S(1)} %add.143), channel_id=1, source_target_pairs={{0,4},{1,5},{2,6},{3,7},{4,0},{5,1},{6,2},{7,3},{8,12},{9,13},{10,... | collective-permute-start | bytes 24584 | tf_op jit(solution)/shard_map/ppermute | solution.py:202
  89.5 1.3 %collective-permute-start.30 = (bf16[2,2,16,2048]{3,2,0,1:T(8,128)(2,1)S(1)}, bf16[2,2,16,2048]{3,2,0,1:T(8,128)(2,1)S(1)}, u32[]{:S(2)}, u32[]{:S(2)}) collective-permute-start(bf16[2,2,16,2048]{3,2,0,1:T(8,128)(2,1)S(1)} %slice.141), channel_id=1, source_target_pairs={{0,1},{1,0},{2,3},{3,2},{4,5},{5,4},{6,7},{7,6},{8,9},{9,8},{10,11... | collective-permute-start | bytes 786440 | tf_op jit(solution)/shard_map/ppermute | solution.py:202
  90.9 1.4 %collective-permute-start.31 = (bf16[2,16,2048]{2,1,0:T(8,128)(2,1)S(1)}, bf16[2,16,2048]{2,1,0:T(8,128)(2,1)S(1)}, u32[]{:S(2)}, u32[]{:S(2)}) collective-permute-start(bf16[2,16,2048]{2,1,0:T(8,128)(2,1)S(1)} %fusion.22), channel_id=1, source_target_pairs={{0,4},{1,5},{2,6},{3,7},{4,0},{5,1},{6,2},{7,3},{8,12},{9,13},{10,... | collective-permute-start | bytes 393224 | tf_op jit(solution)/shard_map/ppermute | solution.py:202
  92.4 5.6 %shard_map.124 = bf16[2048,2048]{1,0:T(8,128)(2,1)} custom-call(s32[8,8]{1,0:T(8,128)S(1)} %convert_element_type.157.mask_ref, bf16[256,2048]{1,0:T(8,128)(2,1)S(1)} %pad_maximum_fusion.2.left_ref, bf16[256,2048]{1,0:T(8,128)(2,1)S(1)} %pad_maximum_fusion.3.right_ref), custom_call_target="tpu_custom_call" | custom-call | tf_op jit(solution)/shard_map/pallas_call | solution.py:108
  100.5 1.7 %collective-permute-start.35 = (bf16[8,4096]{1,0:T(8,128)(2,1)S(1)}, bf16[8,4096]{1,0:T(8,128)(2,1)S(1)}, u32[]{:S(2)}, u32[]{:S(2)}) collective-permute-start(bf16[8,4096]{1,0:T(8,128)(2,1)S(1)} %get-tuple-element.272), channel_id=1, source_target_pairs={{0,16},{8,24},{16,0},{24,8},{1,17},{9,25},{17,1},{25,9},{2,18},{10... | collective-permute-start | bytes 196616 | tf_op jit(solution)/shard_map/ppermute | solution.py:202
  102.4 1.1 collective-permute-start.37
  103.5 1.8 %collective-permute-start.38 = (bf16[8,4096]{1,0:T(8,128)(2,1)S(1)}, bf16[8,4096]{1,0:T(8,128)(2,1)S(1)}, u32[]{:S(2)}, u32[]{:S(2)}) collective-permute-start(bf16[8,4096]{1,0:T(8,128)(2,1)S(1)} %get-tuple-element.271), channel_id=1, source_target_pairs={{0,20},{1,21},{2,22},{3,23},{4,16},{5,17},{6,18},{7,19},{8,28},{9,... | collective-permute-start | bytes 196616 | tf_op jit(solution)/shard_map/ppermute | solution.py:202
  105.3 1.6 %collective-permute-start.39 = (bf16[8,4096]{1,0:T(8,128)(2,1)S(1)}, bf16[8,4096]{1,0:T(8,128)(2,1)S(1)}, u32[]{:S(2)}, u32[]{:S(2)}) collective-permute-start(bf16[8,4096]{1,0:T(8,128)(2,1)S(1)} %get-tuple-element.270), channel_id=1, source_target_pairs={{0,16},{8,24},{16,0},{24,8},{1,17},{9,25},{17,1},{25,9},{2,18},{10... | collective-permute-start | bytes 196616 | tf_op jit(solution)/shard_map/ppermute | solution.py:202
  107.6 2.9 %collective-permute-done.37 = bf16[8,4096]{1,0:T(8,128)(2,1)S(1)} collective-permute-done((bf16[8,4096]{1,0:T(8,128)(2,1)S(1)}, bf16[8,4096]{1,0:T(8,128)(2,1)S(1)}, u32[]{:S(2)}, u32[]{:S(2)}) %collective-permute-start.37) | collective-permute-done | bytes 65568 | tf_op jit(solution)/shard_map/ppermute | solution.py:202
  110.5 1.0 collective-permute-done.38
  111.9 0.8 add_convert_fusion.3
  (160 shorter events, 16.8 us)
Async XLA Ops:
  0.6 14.6 %copy-start = (s32[32,32]{1,0:T(8,128)S(1)}, s32[32,32]{1,0:T(8,128)}, u32[]{:S(2)}) copy-start(s32[32,32]{1,0:T(8,128)} %param.12) | copy-start | bytes 12292
  2.0 13.3 %collective-permute-start.2 = (bf16[8,4096]{1,0:T(8,128)(2,1)S(1)}, bf16[8,4096]{1,0:T(8,128)(2,1)S(1)}, u32[]{:S(2)}, u32[]{:S(2)}) collective-permute-start(bf16[8,4096]{1,0:T(8,128)(2,1)S(1)} %get-tuple-element.127), channel_id=1, source_target_pairs={{0,20},{1,21},{2,22},{3,23},{4,16},{5,17},{6,18},{7,19},{8,28},{9,... | collective-permute-start | bytes 196616 | tf_op jit(solution)/shard_map/ppermute | solution.py:202
  7.0 8.4 %collective-permute-start = (bf16[8,4096]{1,0:T(8,128)(2,1)S(1)}, bf16[8,4096]{1,0:T(8,128)(2,1)S(1)}, u32[]{:S(2)}, u32[]{:S(2)}) collective-permute-start(bf16[8,4096]{1,0:T(8,128)(2,1)S(1)} %get-tuple-element.127), channel_id=1, source_target_pairs={{0,16},{8,24},{16,0},{24,8},{1,17},{9,25},{17,1},{25,9},{2,18},{10... | collective-permute-start | bytes 196616 | tf_op jit(solution)/shard_map/ppermute | solution.py:202
  8.4 6.8 %collective-permute-start.3 = (bf16[8,4096]{1,0:T(8,128)(2,1)S(1)}, bf16[8,4096]{1,0:T(8,128)(2,1)S(1)}, u32[]{:S(2)}, u32[]{:S(2)}) collective-permute-start(bf16[8,4096]{1,0:T(8,128)(2,1)S(1)} %get-tuple-element.282), channel_id=1, source_target_pairs={{0,16},{8,24},{16,0},{24,8},{1,17},{9,25},{17,1},{25,9},{2,18},{10... | collective-permute-start | bytes 196616 | tf_op jit(solution)/shard_map/ppermute | solution.py:202
  10.0 5.2 %collective-permute-start.1 = (bf16[8,4096]{1,0:T(8,128)(2,1)S(1)}, bf16[8,4096]{1,0:T(8,128)(2,1)S(1)}, u32[]{:S(2)}, u32[]{:S(2)}) collective-permute-start(bf16[8,4096]{1,0:T(8,128)(2,1)S(1)} %get-tuple-element.126), channel_id=1, source_target_pairs={{0,4},{1,5},{2,6},{3,7},{4,0},{5,1},{6,2},{7,3},{8,12},{9,13},{10,... | collective-permute-start | bytes 196616 | tf_op jit(solution)/shard_map/ppermute | solution.py:202
  15.5 1.5 %collective-permute-start.4 = (bf16[3,16,2048]{2,1,0:T(8,128)(2,1)S(1)}, bf16[3,16,2048]{2,1,0:T(8,128)(2,1)S(1)}, u32[]{:S(2)}, u32[]{:S(2)}) collective-permute-start(bf16[3,16,2048]{2,1,0:T(8,128)(2,1)S(1)} %pad_maximum_fusion.8), channel_id=1, source_target_pairs={{0,8},{8,0},{16,24},{24,16},{1,9},{9,1},{17,25},{25,17},{2,10},{10... | collective-permute-start | bytes 589832 | tf_op jit(solution)/shard_map/ppermute | solution.py:202
  17.1 9.8 %collective-permute-start.8 = (bf16[2,2,16,2048]{3,2,1,0:T(8,128)(2,1)S(1)}, bf16[2,2,16,2048]{3,2,1,0:T(8,128)(2,1)S(1)}, u32[]{:S(2)}, u32[]{:S(2)}) collective-permute-start(bf16[2,2,16,2048]{3,2,1,0:T(8,128)(2,1)S(1)} %constant_dynamic-update-slice_fusion), channel_id=1, source_target_pairs={{0,1},{1,0},{2,3},{3,2},{4,5},{5,4},{6,7},{7,6},{8,9},{9,8},{10,11... | collective-permute-start | bytes 786440 | tf_op jit(solution)/shard_map/ppermute | solution.py:202
  18.6 10.9 %collective-permute-start.5 = (bf16[2,2,16,2048]{3,2,1,0:T(8,128)(2,1)S(1)}, bf16[2,2,16,2048]{3,2,1,0:T(8,128)(2,1)S(1)}, u32[]{:S(2)}, u32[]{:S(2)}) collective-permute-start(bf16[2,2,16,2048]{3,2,1,0:T(8,128)(2,1)S(1)} %constant_dynamic-update-slice_fusion), channel_id=1, source_target_pairs={{0,2},{1,3},{2,0},{3,1},{4,6},{5,7},{6,4},{7,5},{8,10},{9,11},{10,... | collective-permute-start | bytes 786440 | tf_op jit(solution)/shard_map/ppermute | solution.py:202
  20.2 8.4 %collective-permute-start.6 = (bf16[1,2,16,2048]{3,2,1,0:T(8,128)(2,1)S(1)}, bf16[1,2,16,2048]{3,2,1,0:T(8,128)(2,1)S(1)}, u32[]{:S(2)}, u32[]{:S(2)}) collective-permute-start(bf16[1,2,16,2048]{3,2,1,0:T(8,128)(2,1)S(1)} %maximum_bitcast_fusion.6), channel_id=1, source_target_pairs={{0,1},{1,0},{2,3},{3,2},{4,5},{5,4},{6,7},{7,6},{8,9},{9,8},{10,11... | collective-permute-start | bytes 393224 | tf_op jit(solution)/shard_map/ppermute | solution.py:202
  20.7 8.0 %collective-permute-start.7 = (bf16[1,2,16,2048]{3,2,1,0:T(8,128)(2,1)S(1)}, bf16[1,2,16,2048]{3,2,1,0:T(8,128)(2,1)S(1)}, u32[]{:S(2)}, u32[]{:S(2)}) collective-permute-start(bf16[1,2,16,2048]{3,2,1,0:T(8,128)(2,1)S(1)} %maximum_bitcast_fusion.6), channel_id=1, source_target_pairs={{0,4},{1,5},{2,6},{3,7},{4,0},{5,1},{6,2},{7,3},{8,12},{9,13},{10,... | collective-permute-start | bytes 393224 | tf_op jit(solution)/shard_map/ppermute | solution.py:202
  29.4 2.1 %collective-permute-start.10 = (bf16[64,2048]{1,0:T(8,128)(2,1)S(1)}, bf16[64,2048]{1,0:T(8,128)(2,1)S(1)}, u32[]{:S(2)}, u32[]{:S(2)}) collective-permute-start(bf16[64,2048]{1,0:T(8,128)(2,1)S(1)} %slice.212), channel_id=1, source_target_pairs={{0,8},{8,0},{16,24},{24,16},{1,9},{9,1},{17,25},{25,17},{2,10},{10... | collective-permute-start | bytes 786440 | tf_op jit(solution)/shard_map/ppermute | solution.py:202
  29.4 8.1 %collective-permute-start.9 = (bf16[1,2,16,2048]{3,2,1,0:T(8,128)(2,1)S(1)}, bf16[1,2,16,2048]{3,2,1,0:T(8,128)(2,1)S(1)}, u32[]{:S(2)}, u32[]{:S(2)}) collective-permute-start(bf16[1,2,16,2048]{3,2,1,0:T(8,128)(2,1)S(1)} %collective-permute-done.7), channel_id=1, source_target_pairs={{0,1},{1,0},{2,3},{3,2},{4,5},{5,4},{6,7},{7,6},{8,9},{9,8},{10,11... | collective-permute-start | bytes 393224 | tf_op jit(solution)/shard_map/ppermute | solution.py:202
  30.1 10.9 %collective-permute-start.12 = (bf16[2,2,16,2048]{3,2,1,0:T(8,128)(2,1)S(1)}, bf16[2,2,16,2048]{3,2,1,0:T(8,128)(2,1)S(1)}, u32[]{:S(2)}, u32[]{:S(2)}) collective-permute-start(bf16[2,2,16,2048]{3,2,1,0:T(8,128)(2,1)S(1)} %collective-permute-done.5), channel_id=1, source_target_pairs={{0,1},{1,0},{2,3},{3,2},{4,5},{5,4},{6,7},{7,6},{8,9},{9,8},{10,11... | collective-permute-start | bytes 786440 | tf_op jit(solution)/shard_map/ppermute | solution.py:202
  31.6 9.4 %collective-permute-start.11 = (bf16[64,2048]{1,0:T(8,128)(2,1)S(1)}, bf16[64,2048]{1,0:T(8,128)(2,1)S(1)}, u32[]{:S(2)}, u32[]{:S(2)}) collective-permute-start(bf16[64,2048]{1,0:T(8,128)(2,1)S(1)} %get-tuple-element.253), channel_id=1, source_target_pairs={{0,16},{8,24},{16,0},{24,8},{1,17},{9,25},{17,1},{25,9},{2,18},{10... | collective-permute-start | bytes 786440 | tf_op jit(solution)/shard_map/ppermute | solution.py:202
  32.4 8.5 %collective-permute-start.13 = (bf16[2,2,16,2048]{3,2,1,0:T(8,128)(2,1)S(1)}, bf16[2,2,16,2048]{3,2,1,0:T(8,128)(2,1)S(1)}, u32[]{:S(2)}, u32[]{:S(2)}) collective-permute-start(bf16[2,2,16,2048]{3,2,1,0:T(8,128)(2,1)S(1)} %pad_maximum_fusion.7), channel_id=1, source_target_pairs={{0,2},{1,3},{2,0},{3,1},{4,6},{5,7},{6,4},{7,5},{8,10},{9,11},{10,... | collective-permute-start | bytes 786440 | tf_op jit(solution)/shard_map/ppermute | solution.py:202
  39.2 3.5 %copy-start.2 = (f32[128,2048]{1,0:T(8,128)}, f32[128,2048]{1,0:T(8,128)S(1)}, u32[]{:S(2)}) copy-start(f32[128,2048]{1,0:T(8,128)S(1)} %shard_map.115) | copy-start | bytes 3145732
  42.7 2.0 %collective-permute-start.14 = (bf16[128,2048]{1,0:T(8,128)(2,1)S(1)}, bf16[128,2048]{1,0:T(8,128)(2,1)S(1)}, u32[]{:S(2)}, u32[]{:S(2)}) collective-permute-start(bf16[128,2048]{1,0:T(8,128)(2,1)S(1)} %pad_maximum_fusion.4), channel_id=1, source_target_pairs={{0,8},{8,0},{16,24},{24,16},{1,9},{9,1},{17,25},{25,17},{2,10},{10... | collective-permute-start | bytes 1572872 | tf_op jit(solution)/shard_map/ppermute | solution.py:202
  42.8 1.9 %slice-start = ((f32[128,2048]{1,0:T(8,128)}), f32[64,2048]{1,0:T(8,128)S(1)}, s32[]{:S(2)}) async-start(f32[128,2048]{1,0:T(8,128)} %copy-done.2), calls=%async_computation | async-start | bytes 1048576 | tf_op jit(solution)/shard_map/slice | solution.py:315
  42.8 9.3 %collective-permute-start.16 = (bf16[2,2,16,2048]{3,2,1,0:T(8,128)(2,1)S(1)}, bf16[2,2,16,2048]{3,2,1,0:T(8,128)(2,1)S(1)}, u32[]{:S(2)}, u32[]{:S(2)}) collective-permute-start(bf16[2,2,16,2048]{3,2,1,0:T(8,128)(2,1)S(1)} %collective-permute-done.13), channel_id=1, source_target_pairs={{0,1},{1,0},{2,3},{3,2},{4,5},{5,4},{6,7},{7,6},{8,9},{9,8},{10,11... | collective-permute-start | bytes 786440 | tf_op jit(solution)/shard_map/ppermute | solution.py:202
  43.6 2.7 %collective-permute-start.17 = (bf16[64,2048]{1,0:T(8,128)(2,1)S(1)}, bf16[64,2048]{1,0:T(8,128)(2,1)S(1)}, u32[]{:S(2)}, u32[]{:S(2)}) collective-permute-start(bf16[64,2048]{1,0:T(8,128)(2,1)S(1)} %add_convert_fusion.2), channel_id=1, source_target_pairs={{0,8},{8,0},{16,24},{24,16},{1,9},{9,1},{17,25},{25,17},{2,10},{10... | collective-permute-start | bytes 786440 | tf_op jit(solution)/shard_map/ppermute | solution.py:202
  44.9 14.0 %collective-permute-start.15 = (bf16[128,2048]{1,0:T(8,128)(2,1)S(1)}, bf16[128,2048]{1,0:T(8,128)(2,1)S(1)}, u32[]{:S(2)}, u32[]{:S(2)}) collective-permute-start(bf16[128,2048]{1,0:T(8,128)(2,1)S(1)} %get-tuple-element.251), channel_id=1, source_target_pairs={{0,16},{8,24},{16,0},{24,8},{1,17},{9,25},{17,1},{25,9},{2,18},{10... | collective-permute-start | bytes 1572872 | tf_op jit(solution)/shard_map/ppermute | solution.py:202
  48.6 8.6 %collective-permute-start.18 = (bf16[2,2,16,2048]{3,2,1,0:T(8,128)(2,1)S(1)}, bf16[2,2,16,2048]{3,2,1,0:T(8,128)(2,1)S(1)}, u32[]{:S(2)}, u32[]{:S(2)}) collective-permute-start(bf16[2,2,16,2048]{3,2,1,0:T(8,128)(2,1)S(1)} %slice.130), channel_id=1, source_target_pairs={{0,1},{1,0},{2,3},{3,2},{4,5},{5,4},{6,7},{7,6},{8,9},{9,8},{10,11... | collective-permute-start | bytes 786440 | tf_op jit(solution)/shard_map/ppermute | solution.py:202
  58.9 1.5 %collective-permute-start.19 = (bf16[64,2048]{1,0:T(8,128)(2,1)S(1)}, bf16[64,2048]{1,0:T(8,128)(2,1)S(1)}, u32[]{:S(2)}, u32[]{:S(2)}) collective-permute-start(bf16[64,2048]{1,0:T(8,128)(2,1)S(1)} %slice.209), channel_id=1, source_target_pairs={{0,8},{8,0},{16,24},{24,16},{1,9},{9,1},{17,25},{25,17},{2,10},{10... | collective-permute-start | bytes 786440 | tf_op jit(solution)/shard_map/ppermute | solution.py:202
  59.0 2.9 %collective-permute-start.21 = (bf16[128,2048]{1,0:T(8,128)(2,1)S(1)}, bf16[128,2048]{1,0:T(8,128)(2,1)S(1)}, u32[]{:S(2)}, u32[]{:S(2)}) collective-permute-start(bf16[128,2048]{1,0:T(8,128)(2,1)S(1)} %add_convert_fusion), channel_id=1, source_target_pairs={{0,8},{8,0},{16,24},{24,16},{1,9},{9,1},{17,25},{25,17},{2,10},{10... | collective-permute-start | bytes 1572872 | tf_op jit(solution)/shard_map/ppermute | solution.py:202
  60.5 12.0 %collective-permute-start.20 = (bf16[64,2048]{1,0:T(8,128)(2,1)S(1)}, bf16[64,2048]{1,0:T(8,128)(2,1)S(1)}, u32[]{:S(2)}, u32[]{:S(2)}) collective-permute-start(bf16[64,2048]{1,0:T(8,128)(2,1)S(1)} %get-tuple-element.249), channel_id=1, source_target_pairs={{0,16},{8,24},{16,0},{24,8},{1,17},{9,25},{17,1},{25,9},{2,18},{10... | collective-permute-start | bytes 786440 | tf_op jit(solution)/shard_map/ppermute | solution.py:202
  64.3 8.2 %collective-permute-start.22 = (bf16[2,2,16,2048]{3,2,1,0:T(8,128)(2,1)S(1)}, bf16[2,2,16,2048]{3,2,1,0:T(8,128)(2,1)S(1)}, u32[]{:S(2)}, u32[]{:S(2)}) collective-permute-start(bf16[2,2,16,2048]{3,2,1,0:T(8,128)(2,1)S(1)} %slice.165), channel_id=1, source_target_pairs={{0,1},{1,0},{2,3},{3,2},{4,5},{5,4},{6,7},{7,6},{8,9},{9,8},{10,11... | collective-permute-start | bytes 786440 | tf_op jit(solution)/shard_map/ppermute | solution.py:202
  72.5 1.6 %collective-permute-start.23 = (bf16[64,2048]{1,0:T(8,128)(2,1)S(1)}, bf16[64,2048]{1,0:T(8,128)(2,1)S(1)}, u32[]{:S(2)}, u32[]{:S(2)}) collective-permute-start(bf16[64,2048]{1,0:T(8,128)(2,1)S(1)} %add_convert_fusion.1), channel_id=1, source_target_pairs={{0,8},{8,0},{16,24},{24,16},{1,9},{9,1},{17,25},{25,17},{2,10},{10... | collective-permute-start | bytes 786440 | tf_op jit(solution)/shard_map/ppermute | solution.py:202
  76.1 4.6 %collective-permute-start.25 = (f32[2048]{0:T(1024)S(1)}, f32[2048]{0:T(1024)S(1)}, u32[]{:S(2)}, u32[]{:S(2)}) collective-permute-start(f32[2048]{0:T(1024)S(1)} %add.141), channel_id=1, source_target_pairs={{0,1},{1,0},{2,3},{3,2},{4,5},{5,4},{6,7},{7,6},{8,9},{9,8},{10,11... | collective-permute-start | bytes 24584 | tf_op jit(solution)/shard_map/ppermute | solution.py:202
  77.5 8.4 %collective-permute-start.27 = (bf16[2,2,16,2048]{3,2,1,0:T(8,128)(2,1)S(1)}, bf16[2,2,16,2048]{3,2,1,0:T(8,128)(2,1)S(1)}, u32[]{:S(2)}, u32[]{:S(2)}) collective-permute-start(bf16[2,2,16,2048]{3,2,1,0:T(8,128)(2,1)S(1)} %fusion.19), channel_id=1, source_target_pairs={{0,2},{1,3},{2,0},{3,1},{4,6},{5,7},{6,4},{7,5},{8,10},{9,11},{10,... | collective-permute-start | bytes 786440 | tf_op jit(solution)/shard_map/ppermute | solution.py:202
  79.5 7.8 %collective-permute-start.24 = (bf16[2,2,16,2048]{3,2,0,1:T(8,128)(2,1)S(1)}, bf16[2,2,16,2048]{3,2,0,1:T(8,128)(2,1)S(1)}, u32[]{:S(2)}, u32[]{:S(2)}) collective-permute-start(bf16[2,2,16,2048]{3,2,0,1:T(8,128)(2,1)S(1)} %slice.168), channel_id=1, source_target_pairs={{0,1},{1,0},{2,3},{3,2},{4,5},{5,4},{6,7},{7,6},{8,9},{9,8},{10,11... | collective-permute-start | bytes 786440 | tf_op jit(solution)/shard_map/ppermute | solution.py:202
  80.7 5.2 %collective-permute-start.26 = (f32[2048]{0:T(1024)S(1)}, f32[2048]{0:T(1024)S(1)}, u32[]{:S(2)}, u32[]{:S(2)}) collective-permute-start(f32[2048]{0:T(1024)S(1)} %add.142), channel_id=1, source_target_pairs={{0,2},{1,3},{2,0},{3,1},{4,6},{5,7},{6,4},{7,5},{8,10},{9,11},{10,... | collective-permute-start | bytes 24584 | tf_op jit(solution)/shard_map/ppermute | solution.py:202
  87.3 11.3 %collective-permute-start.28 = (bf16[2,2,16,2048]{3,2,0,1:T(8,128)(2,1)S(1)}, bf16[2,2,16,2048]{3,2,0,1:T(8,128)(2,1)S(1)}, u32[]{:S(2)}, u32[]{:S(2)}) collective-permute-start(bf16[2,2,16,2048]{3,2,0,1:T(8,128)(2,1)S(1)} %fusion.18), channel_id=1, source_target_pairs={{0,2},{1,3},{2,0},{3,1},{4,6},{5,7},{6,4},{7,5},{8,10},{9,11},{10,... | collective-permute-start | bytes 786440 | tf_op jit(solution)/shard_map/ppermute | solution.py:202
  87.8 10.2 %collective-permute-start.29 = (f32[2048]{0:T(1024)S(1)}, f32[2048]{0:T(1024)S(1)}, u32[]{:S(2)}, u32[]{:S(2)}) collective-permute-start(f32[2048]{0:T(1024)S(1)} %add.143), channel_id=1, source_target_pairs={{0,4},{1,5},{2,6},{3,7},{4,0},{5,1},{6,2},{7,3},{8,12},{9,13},{10,... | collective-permute-start | bytes 24584 | tf_op jit(solution)/shard_map/ppermute | solution.py:202
  89.5 9.2 %collective-permute-start.30 = (bf16[2,2,16,2048]{3,2,0,1:T(8,128)(2,1)S(1)}, bf16[2,2,16,2048]{3,2,0,1:T(8,128)(2,1)S(1)}, u32[]{:S(2)}, u32[]{:S(2)}) collective-permute-start(bf16[2,2,16,2048]{3,2,0,1:T(8,128)(2,1)S(1)} %slice.141), channel_id=1, source_target_pairs={{0,1},{1,0},{2,3},{3,2},{4,5},{5,4},{6,7},{7,6},{8,9},{9,8},{10,11... | collective-permute-start | bytes 786440 | tf_op jit(solution)/shard_map/ppermute | solution.py:202
  90.9 7.8 %collective-permute-start.31 = (bf16[2,16,2048]{2,1,0:T(8,128)(2,1)S(1)}, bf16[2,16,2048]{2,1,0:T(8,128)(2,1)S(1)}, u32[]{:S(2)}, u32[]{:S(2)}) collective-permute-start(bf16[2,16,2048]{2,1,0:T(8,128)(2,1)S(1)} %fusion.22), channel_id=1, source_target_pairs={{0,4},{1,5},{2,6},{3,7},{4,0},{5,1},{6,2},{7,3},{8,12},{9,13},{10,... | collective-permute-start | bytes 393224 | tf_op jit(solution)/shard_map/ppermute | solution.py:202
  98.8 8.1 %copy-start.4 = (f32[8192]{0:T(1024)S(1)}, f32[8192]{0:T(1024)}, u32[]{:S(2)}) copy-start(f32[8192]{0:T(1024)} %param.8) | copy-start | bytes 98308
  98.8 1.2 %collective-permute-start.32 = (f32[2048]{0:T(1024)S(1)}, f32[2048]{0:T(1024)S(1)}, u32[]{:S(2)}, u32[]{:S(2)}) collective-permute-start(f32[2048]{0:T(1024)S(1)} %add.148), channel_id=1, source_target_pairs={{0,8},{8,0},{16,24},{24,16},{1,9},{9,1},{17,25},{25,17},{2,10},{10... | collective-permute-start | bytes 24584 | tf_op jit(solution)/shard_map/ppermute | solution.py:202
  98.9 1.5 %collective-permute-start.34 = (bf16[16,2048]{1,0:T(8,128)(2,1)S(1)}, bf16[16,2048]{1,0:T(8,128)(2,1)S(1)}, u32[]{:S(2)}, u32[]{:S(2)}) collective-permute-start(bf16[16,2048]{1,0:T(8,128)(2,1)S(1)} %get-tuple-element.274), channel_id=1, source_target_pairs={{0,8},{8,0},{16,24},{24,16},{1,9},{9,1},{17,25},{25,17},{2,10},{10... | collective-permute-start | bytes 196616 | tf_op jit(solution)/shard_map/ppermute | solution.py:202
  99.5 2.7 %collective-permute-start.36 = (bf16[2,16,2048]{2,1,0:T(8,128)(2,1)S(1)}, bf16[2,16,2048]{2,1,0:T(8,128)(2,1)S(1)}, u32[]{:S(2)}, u32[]{:S(2)}) collective-permute-start(bf16[2,16,2048]{2,1,0:T(8,128)(2,1)S(1)} %fusion.23), channel_id=1, source_target_pairs={{0,8},{8,0},{16,24},{24,16},{1,9},{9,1},{17,25},{25,17},{2,10},{10... | collective-permute-start | bytes 393224 | tf_op jit(solution)/shard_map/ppermute | solution.py:202
  100.0 6.9 %collective-permute-start.33 = (f32[4096]{0:T(1024)S(1)}, f32[4096]{0:T(1024)S(1)}, u32[]{:S(2)}, u32[]{:S(2)}) collective-permute-start(f32[4096]{0:T(1024)S(1)} %maximum_select_fusion.8), channel_id=1, source_target_pairs={{0,16},{8,24},{16,0},{24,8},{1,17},{9,25},{17,1},{25,9},{2,18},{10... | collective-permute-start | bytes 49160 | tf_op jit(solution)/shard_map/ppermute | solution.py:202
  100.5 11.3 %copy-start.3 = (bf16[8,8192]{1,0:T(8,128)(2,1)S(1)}, bf16[8,8192]{1,0:T(8,128)(2,1)}, u32[]{:S(2)}) copy-start(bf16[8,8192]{1,0:T(8,128)(2,1)} %input_hbm.1) | copy-start | bytes 393220
  100.5 11.3 %copy-start.5 = (bf16[8,8192]{1,0:T(8,128)(2,1)S(1)}, bf16[8,8192]{1,0:T(8,128)(2,1)}, u32[]{:S(2)}) copy-start(bf16[8,8192]{1,0:T(8,128)(2,1)} %param.13) | copy-start | bytes 393220
  100.5 7.0 %collective-permute-start.35 = (bf16[8,4096]{1,0:T(8,128)(2,1)S(1)}, bf16[8,4096]{1,0:T(8,128)(2,1)S(1)}, u32[]{:S(2)}, u32[]{:S(2)}) collective-permute-start(bf16[8,4096]{1,0:T(8,128)(2,1)S(1)} %get-tuple-element.272), channel_id=1, source_target_pairs={{0,16},{8,24},{16,0},{24,8},{1,17},{9,25},{17,1},{25,9},{2,18},{10... | collective-permute-start | bytes 196616 | tf_op jit(solution)/shard_map/ppermute | solution.py:202
  102.3 10.5 %copy-start.1 = (s32[32,32]{1,0:T(8,128)S(1)}, s32[32,32]{1,0:T(8,128)}, u32[]{:S(2)}) copy-start(s32[32,32]{1,0:T(8,128)} %param.12) | copy-start | bytes 12292
  102.4 8.1 %collective-permute-start.37 = (bf16[8,4096]{1,0:T(8,128)(2,1)S(1)}, bf16[8,4096]{1,0:T(8,128)(2,1)S(1)}, u32[]{:S(2)}, u32[]{:S(2)}) collective-permute-start(bf16[8,4096]{1,0:T(8,128)(2,1)S(1)} %fusion.24), channel_id=1, source_target_pairs={{0,4},{1,5},{2,6},{3,7},{4,0},{5,1},{6,2},{7,3},{8,12},{9,13},{10,... | collective-permute-start | bytes 196616 | tf_op jit(solution)/shard_map/ppermute | solution.py:202
  103.5 7.9 %collective-permute-start.38 = (bf16[8,4096]{1,0:T(8,128)(2,1)S(1)}, bf16[8,4096]{1,0:T(8,128)(2,1)S(1)}, u32[]{:S(2)}, u32[]{:S(2)}) collective-permute-start(bf16[8,4096]{1,0:T(8,128)(2,1)S(1)} %get-tuple-element.271), channel_id=1, source_target_pairs={{0,20},{1,21},{2,22},{3,23},{4,16},{5,17},{6,18},{7,19},{8,28},{9,... | collective-permute-start | bytes 196616 | tf_op jit(solution)/shard_map/ppermute | solution.py:202
  105.3 6.1 %collective-permute-start.39 = (bf16[8,4096]{1,0:T(8,128)(2,1)S(1)}, bf16[8,4096]{1,0:T(8,128)(2,1)S(1)}, u32[]{:S(2)}, u32[]{:S(2)}) collective-permute-start(bf16[8,4096]{1,0:T(8,128)(2,1)S(1)} %get-tuple-element.270), channel_id=1, source_target_pairs={{0,16},{8,24},{16,0},{24,8},{1,17},{9,25},{17,1},{25,9},{2,18},{10... | collective-permute-start | bytes 196616 | tf_op jit(solution)/shard_map/ppermute | solution.py:202
